TPU v7x, 32 devices: a whole 2x2x4 slice. The times are simulated.
32 devices in a mesh: dp: 4 (over y, x), vocab: 8 (over z, core).
Axes of the slice: x: 2, y: 2, z: 4, core: 2. Of those that a mesh axis runs over, the one named last changes fastest.
Arguments:
- token_ids: int32 [32, 128], P(('dp', 'vocab')), may hold values from 0 to 50256, as said below
- pick_rows: int32 [32, 64], P(('dp', 'vocab')), may hold values from 0 to 127, as said below
- target_ids: int32 [32, 64], P(('dp', 'vocab')), may hold values from 0 to 50256
- attn_in: float32 [768, 2304], P(('dp', 'vocab')), may hold values from -0.21875 to 0.21875
- attn_out: float32 [768, 768], P(('dp', 'vocab')), may hold values from -0.875 to 0.875
- mlp_in: float32 [768, 3072], P(('dp', 'vocab')), may hold values from -0.21875 to 0.21875
- mlp_out: float32 [3072, 768], P(('dp', 'vocab')), may hold values from -0.109375 to 0.109375
- positions: float32 [128, 768], P(('dp', 'vocab')), may hold values from -0.4375 to 0.4375
- vectors: float32 [14, 768], P(None, ('dp', 'vocab'))
- table: float32 [50304, 768], P('vocab'), may hold values from -0.4375 to 0.4375
- first_attn_in: float32 [768, 2304], P(('dp', 'vocab')), may hold values from -9.536743e-07 to 9.536743e-07
- first_attn_out: float32 [768, 768], P(('dp', 'vocab')), may hold values from -9.536743e-07 to 9.536743e-07
- first_mlp_in: float32 [768, 3072], P(('dp', 'vocab')), may hold values from -9.536743e-07 to 9.536743e-07
- first_mlp_out: float32 [3072, 768], P(('dp', 'vocab')), may hold values from -9.536743e-07 to 9.536743e-07
- first_positions: float32 [128, 768], P(('dp', 'vocab')), may hold values from -9.536743e-07 to 9.536743e-07
- first_vectors: float32 [14, 768], P(None, ('dp', 'vocab')), may hold values from -9.536743e-07 to 9.536743e-07
- first_table: float32 [50304, 768], P('vocab'), may hold values from -9.536743e-07 to 9.536743e-07
- second_attn_in: float32 [768, 2304], P(('dp', 'vocab')), may hold values from 2.1824333e-15 to 8.729733e-15
- second_attn_out: float32 [768, 768], P(('dp', 'vocab')), may hold values from 2.1824333e-15 to 8.729733e-15
- second_mlp_in: float32 [768, 3072], P(('dp', 'vocab')), may hold values from 2.1824333e-15 to 8.729733e-15
- second_mlp_out: float32 [3072, 768], P(('dp', 'vocab')), may hold values from 2.1824333e-15 to 8.729733e-15
- second_positions: float32 [128, 768], P(('dp', 'vocab')), may hold values from 2.1824333e-15 to 8.729733e-15
- second_vectors: float32 [14, 768], P(None, ('dp', 'vocab')), may hold values from 2.1824333e-15 to 8.729733e-15
- second_table: float32 [50304, 768], P('vocab'), may hold values from 2.1824333e-15 to 8.729733e-15
Outputs:
- loss: float32 [], replicated
- grad_norm: float32 [], replicated
- ratios: float32 [7], replicated
- new_attn_in: float32 [768, 2304], P(('dp', 'vocab'))
- new_attn_out: float32 [768, 768], P(('dp', 'vocab'))
- new_mlp_in: float32 [768, 3072], P(('dp', 'vocab'))
- new_mlp_out: float32 [3072, 768], P(('dp', 'vocab'))
- new_positions: float32 [128, 768], P(('dp', 'vocab'))
- new_vectors: float32 [14, 768], P(None, ('dp', 'vocab'))
- new_table: float32 [50304, 768], P('vocab')
- new_first_attn_in: float32 [768, 2304], P(('dp', 'vocab'))
- new_first_attn_out: float32 [768, 768], P(('dp', 'vocab'))
- new_first_mlp_in: float32 [768, 3072], P(('dp', 'vocab'))
- new_first_mlp_out: float32 [3072, 768], P(('dp', 'vocab'))
- new_first_positions: float32 [128, 768], P(('dp', 'vocab'))
- new_first_vectors: float32 [14, 768], P(None, ('dp', 'vocab'))
- new_first_table: float32 [50304, 768], P('vocab')
- new_second_attn_in: float32 [768, 2304], P(('dp', 'vocab'))
- new_second_attn_out: float32 [768, 768], P(('dp', 'vocab'))
- new_second_mlp_in: float32 [768, 3072], P(('dp', 'vocab'))
- new_second_mlp_out: float32 [3072, 768], P(('dp', 'vocab'))
- new_second_positions: float32 [128, 768], P(('dp', 'vocab'))
- new_second_vectors: float32 [14, 768], P(None, ('dp', 'vocab'))
- new_second_table: float32 [50304, 768], P('vocab')
Inputs may be any that keep to these rules, and one draw needn't show every extreme that they name: `pick_rows`: each sequence's 64 positions are distinct and increasing. `token_ids`: the table's rows split into 8 aligned blocks of 6288 ids; of one sequence's tokens at most 64 have ids in one block, and every sequence has exactly 64 in some block.
All inputs are finite; a program needn't handle non-finite values.
Results may differ from a plain program's by a relative error of at most 0.008.
The roundings to bfloat16 on the way count: a program that leaves them out, or rounds other values in their place, can miss the bound.
Values may be sent and summed in bfloat16 or wider, within the bound.
No kernel may reach another device: no remote copies, remote signals or barrier semaphores. Data moves between devices by JAX's collectives and lax.ppermute only.
A program may use at most 448 MiB of HBM per device.

v0:
```python
import jax
import jax.numpy as jnp
from jax import lax
from jax.sharding import PartitionSpec as P

HD = 64
V_REAL = 50257
STEP = 5


LN_EPS = 1e-05
SMOOTHING = 0.1
BETA_ONE = 0.9
BETA_TWO = 0.999
ADAM_EPS = 1e-12
DECAY = 0.01
RATE = 0.3
CLIP_AT = 0.01
MASKED = -1e30


def layer_norm(inputs, gain, shift):
    centre = jnp.mean(inputs, axis=-1, keepdims=True)
    centred = inputs - centre
    spread = jnp.mean(centred * centred, axis=-1, keepdims=True)
    return centred * lax.rsqrt(spread + LN_EPS) * gain + shift


def gelu_tanh(inputs):
    return (
        0.5
        * inputs
        * (1.0 + jnp.tanh(0.7978845608028654 * (inputs + 0.044715 * inputs * inputs * inputs)))
    )


def dot_plain(left_op, right_op):
    return jnp.dot(left_op, right_op, preferred_element_type=jnp.float32)


def dot_first(left_op, right_op):
    return lax.dot_general(
        left_op, right_op, (((0,), (0,)), ((), ())), preferred_element_type=jnp.float32
    )


def dot_second(left_op, right_op):
    return lax.dot_general(
        left_op, right_op, (((1,), (1,)), ((), ())), preferred_element_type=jnp.float32
    )


def block_scores(query_blk, keys_all, offset):
    scores = jnp.einsum(
        "qhd,khd->hqk", query_blk, keys_all, preferred_element_type=jnp.float32
    ) * HD ** (-0.5)
    places = offset + jnp.arange(query_blk.shape[0])[:, None]
    causal = jnp.arange(keys_all.shape[0])[None, :] <= places
    return jnp.where(causal[None], scores, MASKED)


def split_blocks(queries):
    seq_len = queries.shape[0]
    block_rows = min(512, seq_len)
    count_blocks = seq_len // block_rows
    starts = jnp.arange(count_blocks, dtype=jnp.int32) * block_rows
    return (block_rows, count_blocks, starts)


def attention_forward(queries, keys_all, values_all):
    block_rows, count_blocks, starts = split_blocks(queries)
    stacked = queries.reshape(count_blocks, block_rows, queries.shape[1], queries.shape[2])

    def one_block(inputs):
        query_blk, offset = inputs
        scores = block_scores(query_blk, keys_all, offset)
        row_top = jnp.max(scores, axis=-1, keepdims=True)
        exp_scores = jnp.exp(scores - row_top)
        totals = jnp.sum(exp_scores, axis=-1, keepdims=True)
        attn_probs = (exp_scores / totals).astype(jnp.bfloat16)
        mixed_out = jnp.einsum(
            "hqk,khd->qhd", attn_probs, values_all, preferred_element_type=jnp.float32
        )
        return (mixed_out, (row_top + jnp.log(totals))[..., 0])

    mixed_out, log_total = lax.map(one_block, (stacked, starts))
    return (mixed_out.reshape(queries.shape), log_total)


def attention_backward(queries, keys_all, values_all, log_total, grad_mixed):
    block_rows, count_blocks, starts = split_blocks(queries)
    shape_blk = (count_blocks, block_rows, queries.shape[1], queries.shape[2])

    def one_block(carry, inputs):
        query_blk, grad_blk, lse_blk, offset = inputs
        scores = block_scores(query_blk, keys_all, offset)
        soft = jnp.exp(scores - lse_blk[..., None])
        grad_p = jnp.einsum(
            "qhd,khd->hqk", grad_blk, values_all, preferred_element_type=jnp.float32
        )
        centre = jnp.sum(soft * grad_p, axis=-1, keepdims=True)
        grad_s = (soft * (grad_p - centre)).astype(jnp.bfloat16)
        grad_q = jnp.einsum(
            "hqk,khd->qhd", grad_s, keys_all, preferred_element_type=jnp.float32
        ) * HD ** (-0.5)
        grad_k = carry[0] + jnp.einsum(
            "hqk,qhd->khd", grad_s, query_blk, preferred_element_type=jnp.float32
        ) * HD ** (-0.5)
        grad_v = carry[1] + jnp.einsum(
            "hqk,qhd->khd", soft.astype(jnp.bfloat16), grad_blk, preferred_element_type=jnp.float32
        )
        return ((grad_k, grad_v), grad_q)

    zeros_kv = jnp.zeros(keys_all.shape, jnp.float32)
    (grad_k, grad_v), grad_q = lax.scan(
        one_block,
        (zeros_kv, zeros_kv),
        (queries.reshape(shape_blk), grad_mixed.reshape(shape_blk), log_total, starts),
    )
    return (grad_q.reshape(queries.shape), grad_k, grad_v)


def layer_forward(resid_in, w_qkv, w_proj, w_up, w_down, vec_rows):
    seq_len, width = resid_in.shape
    head_count = width // HD
    normed_one = layer_norm(resid_in, vec_rows[0], vec_rows[1]).astype(jnp.bfloat16)
    qkv_bias = jnp.concatenate([vec_rows[6], jnp.zeros_like(vec_rows[6]), vec_rows[7]])
    packed = (dot_plain(normed_one, w_qkv) + qkv_bias).astype(jnp.bfloat16)
    queries = packed[:, :width].reshape(seq_len, head_count, HD)
    keys_all = packed[:, width : 2 * width].reshape(seq_len, head_count, HD)
    values_all = packed[:, 2 * width :].reshape(seq_len, head_count, HD)
    attended, log_total = attention_forward(queries, keys_all, values_all)
    attended = attended.reshape(seq_len, width).astype(jnp.bfloat16)
    resid_mid = resid_in + dot_plain(attended, w_proj) + vec_rows[8]
    normed_two = layer_norm(resid_mid, vec_rows[2], vec_rows[3]).astype(jnp.bfloat16)
    hidden_pre = dot_plain(normed_two, w_up) + vec_rows[10:14].reshape(-1)
    hidden_act = gelu_tanh(hidden_pre).astype(jnp.bfloat16)
    resid_out = resid_mid + dot_plain(hidden_act, w_down) + vec_rows[9]
    kept = (
        resid_in,
        resid_mid,
        normed_one,
        normed_two,
        queries,
        keys_all,
        values_all,
        log_total,
        attended,
        hidden_pre,
        hidden_act,
    )
    return (resid_out, kept)


def layer_backward(grad_out, kept, w_qkv, w_proj, w_up, w_down, vec_rows):
    (
        resid_in,
        resid_mid,
        normed_one,
        normed_two,
        queries,
        keys_all,
        values_all,
        log_total,
        attended,
        hidden_pre,
        hidden_act,
    ) = kept
    seq_len, width = resid_in.shape
    grad_branch = grad_out.astype(jnp.bfloat16)
    grad_down = dot_first(hidden_act, grad_branch)
    bias_down = jnp.sum(grad_branch.astype(jnp.float32), axis=0)
    grad_act = dot_second(grad_branch, w_down)
    grad_pre = jax.vjp(gelu_tanh, hidden_pre)[1](grad_act)[0].astype(jnp.bfloat16)
    grad_up = dot_first(normed_two, grad_pre)
    bias_up = jnp.sum(grad_pre.astype(jnp.float32), axis=0)
    grad_two = dot_second(grad_pre, w_up)
    grad_mid, gain_two, shift_two = jax.vjp(layer_norm, resid_mid, vec_rows[2], vec_rows[3])[1](
        grad_two
    )
    grad_mid = grad_mid + grad_out
    grad_attn = grad_mid.astype(jnp.bfloat16)
    grad_proj = dot_first(attended, grad_attn)
    bias_proj = jnp.sum(grad_attn.astype(jnp.float32), axis=0)
    grad_mixed = dot_second(grad_attn, w_proj).astype(jnp.bfloat16).reshape(queries.shape)
    grad_q, grad_k, grad_v = attention_backward(
        queries, keys_all, values_all, log_total, grad_mixed
    )
    grad_packed = jnp.concatenate(
        [
            grad_q.reshape(seq_len, width),
            grad_k.reshape(seq_len, width),
            grad_v.reshape(seq_len, width),
        ],
        axis=1,
    ).astype(jnp.bfloat16)
    grad_qkv = dot_first(normed_one, grad_packed)
    bias_qkv = jnp.sum(grad_packed.astype(jnp.float32), axis=0)
    grad_one = dot_second(grad_packed, w_qkv)
    grad_in, gain_one, shift_one = jax.vjp(layer_norm, resid_in, vec_rows[0], vec_rows[1])[1](
        grad_one
    )
    grad_in = grad_in + grad_mid
    vec_grads = (
        gain_one,
        shift_one,
        gain_two,
        shift_two,
        bias_qkv[:width],
        bias_qkv[2 * width :],
        bias_proj,
        bias_down,
        bias_up.reshape(4, width),
    )
    return (grad_in, (grad_qkv, grad_proj, grad_up, grad_down), vec_grads)


def route_plan(own_ids, flat_ids, vocab_rows, vocab_start, shard_count):
    tok_count = own_ids.shape[0]
    slot_cap = 4 * tok_count // shard_count
    own_owner = own_ids // vocab_rows
    owner_hot = (own_owner[:, None] == jnp.arange(shard_count, dtype=jnp.int32)[None, :]).astype(
        jnp.int32
    )
    own_slot = jnp.sum(owner_hot * (jnp.cumsum(owner_hot, axis=0) - 1), axis=1)
    own_place = own_owner * slot_cap + own_slot
    group_local = flat_ids.reshape(shard_count, tok_count) - vocab_start
    mine = (group_local >= 0) & (group_local < vocab_rows)
    recv_slot = jnp.cumsum(mine.astype(jnp.int32), axis=1) - 1
    source_base = jnp.arange(shard_count, dtype=jnp.int32)[:, None] * slot_cap
    recv_place = jnp.where(mine, source_base + recv_slot, shard_count * slot_cap)
    recv_ids = (
        jnp.full((shard_count * slot_cap,), vocab_rows, jnp.int32)
        .at[recv_place.reshape(-1)]
        .set(group_local.reshape(-1), mode="drop")
    )
    return (slot_cap, own_place, recv_ids)


def shards(
    token_ids,
    pick_rows,
    target_ids,
    attn_in,
    attn_out,
    mlp_in,
    mlp_out,
    positions,
    vectors,
    table,
    first_attn_in,
    first_attn_out,
    first_mlp_in,
    first_mlp_out,
    first_positions,
    first_vectors,
    first_table,
    second_attn_in,
    second_attn_out,
    second_mlp_in,
    second_mlp_out,
    second_positions,
    second_vectors,
    second_table,
):
    lowered = (
        lax.all_gather(attn_in.astype(jnp.bfloat16), ("dp", "vocab"), axis=0, tiled=True),
        lax.all_gather(attn_out.astype(jnp.bfloat16), ("dp", "vocab"), axis=0, tiled=True),
        lax.all_gather(mlp_in.astype(jnp.bfloat16), ("dp", "vocab"), axis=0, tiled=True),
        lax.all_gather(mlp_out.astype(jnp.bfloat16), ("dp", "vocab"), axis=0, tiled=True),
        lax.all_gather(positions.astype(jnp.bfloat16), ("dp", "vocab"), axis=0, tiled=True),
        lax.all_gather(vectors.astype(jnp.bfloat16), ("dp", "vocab"), axis=1, tiled=True),
    )
    w_qkv, w_proj, w_up, w_down, pos_low, vec_low = lowered
    vec_rows = vec_low.astype(jnp.float32)
    table_low = table.astype(jnp.bfloat16)
    vocab_rows, width = table.shape
    shard_count = lax.axis_size("vocab")
    vocab_start = lax.axis_index("vocab") * vocab_rows
    own_ids = token_ids.reshape(-1)
    group_ids, group_targets = (
        lax.all_gather(token_ids, "vocab", axis=0, tiled=True),
        lax.all_gather(target_ids, "vocab", axis=0, tiled=True),
    )
    flat_ids = group_ids.reshape(-1)
    slot_cap, own_place, recv_ids = route_plan(
        own_ids, flat_ids, vocab_rows, vocab_start, shard_count
    )
    recv_valid = recv_ids < vocab_rows
    served = jnp.take(table_low, jnp.where(recv_valid, recv_ids, 0), axis=0)
    served = jnp.where(recv_valid[:, None], served, jnp.zeros_like(served)).reshape(
        shard_count, slot_cap, width
    )
    returned = lax.all_to_all(served, "vocab", split_axis=0, concat_axis=0, tiled=True)
    embedded = jnp.take(returned.reshape(-1, width), own_place, axis=0).astype(jnp.float32)
    resid_in = embedded + pos_low.astype(jnp.float32)
    resid_out, kept = layer_forward(resid_in, w_qkv, w_proj, w_up, w_down, vec_rows)
    final_low = layer_norm(resid_out, vec_rows[4], vec_rows[5]).astype(jnp.bfloat16)
    own_picks = pick_rows.reshape(-1)
    picked = jnp.take(final_low, own_picks, axis=0)
    head_in = lax.all_gather(picked, "vocab", axis=0, tiled=True)
    logits = dot_second(head_in, table_low)
    columns = vocab_start + jnp.arange(vocab_rows)
    is_real = columns < V_REAL
    logits = jnp.where(is_real[None, :], logits, MASKED)
    is_target = columns[None, :] == group_targets.reshape(-1)[:, None]
    target_part = jnp.sum(jnp.where(is_target, logits, 0.0), axis=1)
    logit_part = jnp.sum(jnp.where(is_real[None, :], logits, 0.0), axis=1)
    local_top = jnp.max(logits, axis=1)
    row_top = lax.pmax(local_top, "vocab")
    exp_part = jnp.sum(jnp.exp(logits - row_top[:, None]), axis=1)
    exp_total, target_logit, logit_total = lax.psum((exp_part, target_part, logit_part), "vocab")
    log_norm = row_top + jnp.log(exp_total)
    row_loss = (1.0 - SMOOTHING) * (log_norm - target_logit) + SMOOTHING * (
        log_norm - logit_total / V_REAL
    )
    token_count = lax.axis_size("dp") * lax.axis_size("vocab") * pick_rows.size
    soft = jnp.exp(logits - log_norm[:, None])
    grad_logits = (
        (soft - (1.0 - SMOOTHING) * is_target - SMOOTHING / V_REAL * is_real[None, :]) / token_count
    ).astype(jnp.bfloat16)
    table_grad = dot_first(grad_logits, head_in)
    picked_grad = lax.psum_scatter(
        dot_plain(grad_logits, table_low), "vocab", scatter_dimension=0, tiled=True
    )
    final_grad = jnp.zeros(resid_out.shape, jnp.float32).at[own_picks].add(picked_grad)
    grad_top, gain_final, shift_final = jax.vjp(layer_norm, resid_out, vec_rows[4], vec_rows[5])[1](
        final_grad
    )
    grad_in, matrix_grads, vec_grads = layer_backward(
        grad_top, kept, w_qkv, w_proj, w_up, w_down, vec_rows
    )
    grad_rows = grad_in.astype(jnp.bfloat16)
    local_ids = flat_ids - vocab_start
    inside = (local_ids >= 0) & (local_ids < vocab_rows)
    table_grad = table_grad.at[jnp.where(inside, local_ids, vocab_rows)].add(
        lax.all_gather(grad_rows, "vocab", axis=0, tiled=True).astype(jnp.float32), mode="drop"
    )
    table_grad, loss_total = lax.psum((table_grad, jnp.sum(row_loss)), "dp")
    loss = loss_total / token_count
    (
        gain_one,
        shift_one,
        gain_two,
        shift_two,
        bias_query,
        bias_value,
        bias_proj,
        bias_down,
        bias_up,
    ) = vec_grads
    vec_grad = jnp.concatenate(
        [
            jnp.stack(
                [
                    gain_one,
                    shift_one,
                    gain_two,
                    shift_two,
                    gain_final,
                    shift_final,
                    bias_query,
                    bias_value,
                    bias_proj,
                    bias_down,
                ]
            ),
            bias_up,
        ],
        axis=0,
    )
    block_grads = (
        lax.psum_scatter(matrix_grads[0], ("dp", "vocab"), scatter_dimension=0, tiled=True),
        lax.psum_scatter(matrix_grads[1], ("dp", "vocab"), scatter_dimension=0, tiled=True),
        lax.psum_scatter(matrix_grads[2], ("dp", "vocab"), scatter_dimension=0, tiled=True),
        lax.psum_scatter(matrix_grads[3], ("dp", "vocab"), scatter_dimension=0, tiled=True),
        lax.psum_scatter(grad_in, ("dp", "vocab"), scatter_dimension=0, tiled=True),
        lax.psum_scatter(vec_grad, ("dp", "vocab"), scatter_dimension=1, tiled=True),
    )
    gradients = tuple(block_grads) + (table_grad,)
    masters = (attn_in, attn_out, mlp_in, mlp_out, positions, vectors, table)
    firsts = (
        first_attn_in,
        first_attn_out,
        first_mlp_in,
        first_mlp_out,
        first_positions,
        first_vectors,
        first_table,
    )
    seconds = (
        second_attn_in,
        second_attn_out,
        second_mlp_in,
        second_mlp_out,
        second_positions,
        second_vectors,
        second_table,
    )
    shares = (1.0, 1.0, 1.0, 1.0, 1.0, 1.0, 1.0 / lax.axis_size("dp"))
    clip_term = sum(
        (jnp.sum(gradient * gradient) * share for gradient, share in zip(gradients, shares))
    )
    weight_terms = jnp.stack(
        [jnp.sum(weight * weight) * share for weight, share in zip(masters, shares)]
    )
    clip_total, weight_total = lax.psum((clip_term, weight_terms), ("dp", "vocab"))
    grad_norm = jnp.sqrt(clip_total)
    factor = jnp.minimum(1.0, CLIP_AT / grad_norm)
    new_firsts, new_seconds, updates, update_terms = ([], [], [], [])
    for weight, gradient, moment_one, moment_two, share in zip(
        masters, gradients, firsts, seconds, shares
    ):
        clipped = gradient * factor
        moment_one = BETA_ONE * moment_one + (1.0 - BETA_ONE) * clipped
        moment_two = BETA_TWO * moment_two + (1.0 - BETA_TWO) * clipped * clipped
        update = (
            moment_one
            / (1.0 - BETA_ONE**STEP)
            / (jnp.sqrt(moment_two / (1.0 - BETA_TWO**STEP)) + ADAM_EPS)
            + DECAY * weight
        )
        new_firsts.append(moment_one)
        new_seconds.append(moment_two)
        updates.append(update)
        update_terms.append(jnp.sum(update * update) * share)
    update_total = lax.psum(jnp.stack(update_terms), ("dp", "vocab"))
    ratios = jnp.sqrt(weight_total) / jnp.sqrt(update_total)
    new_weights = [
        weight - RATE * ratios[index] * update
        for index, (weight, update) in enumerate(zip(masters, updates))
    ]
    return (
        loss,
        grad_norm,
        ratios,
        new_weights[0],
        new_weights[1],
        new_weights[2],
        new_weights[3],
        new_weights[4],
        new_weights[5],
        new_weights[6],
        new_firsts[0],
        new_firsts[1],
        new_firsts[2],
        new_firsts[3],
        new_firsts[4],
        new_firsts[5],
        new_firsts[6],
        new_seconds[0],
        new_seconds[1],
        new_seconds[2],
        new_seconds[3],
        new_seconds[4],
        new_seconds[5],
        new_seconds[6],
    )


def solution(mesh):
    return jax.shard_map(
        shards,
        mesh=mesh,
        in_specs=(
            P(("dp", "vocab"), None),
            P(("dp", "vocab"), None),
            P(("dp", "vocab"), None),
            P(("dp", "vocab"), None),
            P(("dp", "vocab"), None),
            P(("dp", "vocab"), None),
            P(("dp", "vocab"), None),
            P(("dp", "vocab"), None),
            P(None, ("dp", "vocab")),
            P("vocab", None),
            P(("dp", "vocab"), None),
            P(("dp", "vocab"), None),
            P(("dp", "vocab"), None),
            P(("dp", "vocab"), None),
            P(("dp", "vocab"), None),
            P(None, ("dp", "vocab")),
            P("vocab", None),
            P(("dp", "vocab"), None),
            P(("dp", "vocab"), None),
            P(("dp", "vocab"), None),
            P(("dp", "vocab"), None),
            P(("dp", "vocab"), None),
            P(None, ("dp", "vocab")),
            P("vocab", None),
        ),
        out_specs=(
            P(),
            P(),
            P(),
            P(("dp", "vocab"), None),
            P(("dp", "vocab"), None),
            P(("dp", "vocab"), None),
            P(("dp", "vocab"), None),
            P(("dp", "vocab"), None),
            P(None, ("dp", "vocab")),
            P("vocab", None),
            P(("dp", "vocab"), None),
            P(("dp", "vocab"), None),
            P(("dp", "vocab"), None),
            P(("dp", "vocab"), None),
            P(("dp", "vocab"), None),
            P(None, ("dp", "vocab")),
            P("vocab", None),
            P(("dp", "vocab"), None),
            P(("dp", "vocab"), None),
            P(("dp", "vocab"), None),
            P(("dp", "vocab"), None),
            P(("dp", "vocab"), None),
            P(None, ("dp", "vocab")),
            P("vocab", None),
        ),
        check_vma=False,
    )
```

profile of v0, /device:TPU:0, one launch (start us, length us, event | category | flops | bytes accessed | tf_op | source)
XLA Modules:
  0.0 1660.4 jit_solution(2375315733607994212)
XLA Ops:
  13.9 13.5 all-gather
  27.8 4.3 scatter_custom_fusion
  32.3 11.3 convert_element_type.110
  43.7 7.4 gather_fusion
  52.2 3.5 all-to-all-start
  57.0 59.4 %all-gather.1 = bf16[32,4,768]{2,1,0:T(4,128)(2,1)S(1)} all-gather(bf16[1,4,768]{2,1,0:T(4,128)(2,1)S(1)} %get-tuple-element.151), channel_id=1, replica_groups=mesh['dp'=4,'vocab'=8] {'dp','vocab'}, dimensions={0}, use_global_device_ids=true | all-gather | bytes 202752 | tf_op jit(solution)/shard_map/all_gather | solution.py:271
  116.4 8.7 all-gather.3
  126.9 38.8 %all-gather.2 = bf16[32,24,14]{1,2,0:T(8,128)(2,1)S(1)} all-gather(bf16[1,24,14]{1,2,0:T(8,128)(2,1)S(1)} %convert_bitcast_fusion.1), channel_id=1, replica_groups=mesh['dp'=4,'vocab'=8] {'dp','vocab'}, dimensions={0}, use_global_device_ids=true | all-gather | bytes 22176 | tf_op jit(solution)/shard_map/all_gather | solution.py:272
  171.1 2.7 fusion.6
  177.2 30.2 %all-gather.14.cloned.1.call-done = bf16[768,3072]{1,0:T(8,128)(2,1)} async-done(((bf16[24,3072]{1,0:T(8,128)(2,1)}), bf16[768,3072]{1,0:T(8,128)(2,1)}) %all-gather.14.cloned.1.call-update) | async-done | bytes 4718608 | tf_op jit(solution)/shard_map/all_gather | solution.py:269
  207.4 3.2 convolution_add_fusion.1
  210.6 62.7 %all-gather.16.cloned.1.call-done = bf16[3072,768]{1,0:T(8,128)(2,1)} async-done(((bf16[96,768]{1,0:T(8,128)(2,1)}), bf16[3072,768]{1,0:T(8,128)(2,1)}) %all-gather.16.cloned.1.call-update) | async-done | bytes 4718608 | tf_op jit(solution)/shard_map/all_gather | solution.py:270
  273.4 3.5 fusion.67
  279.0 2.5 gather_fusion.2
  282.5 15.9 all_gather.37
  298.4 12.2 fusion.68
  310.6 16.9 %pmax.7 = f32[512]{0:T(512)} all-reduce(f32[512]{0:T(512)} %get-tuple-element.169), channel_id=1, replica_groups=mesh['dp'=4,'vocab'=8] {'vocab'}, use_global_device_ids=true, to_apply=%region_13.14 | all-reduce | flops 512 | bytes 4096 | tf_op jit(solution)/shard_map/pmax | solution.py:310
  327.5 8.0 fusion.1
  335.5 14.6 all-reduce.3
  351.4 8.0 fusion.5
  359.4 2.7 copy-done
  362.1 9.4 fusion.69
  372.9 30.1 %reduce-scatter.7.cloned.1.call-done = f32[64,768]{1,0:T(8,128)} async-done(((f32[512,768]{1,0:T(8,128)}), f32[64,768]{1,0:T(8,128)}) %reduce-scatter.7.cloned.1.call-update) | async-done | bytes 196624 | tf_op jit(solution)/shard_map/reduce_scatter | solution.py:323
  402.9 2.3 scatter_custom_fusion.1
  409.8 5.4 convert_reduce_fusion
  415.2 2.3 multiply_reduce_fusion.5
  431.9 4.8 fusion.46
  437.9 5.2 fusion.47
  444.1 5.3 fusion.48
  450.6 12.0 fusion.70
  462.6 21.4 %scatter_custom_fusion.2 = f32[6288,768]{1,0:T(8,128)} fusion(f32[6288,768]{1,0:T(8,128)} %fusion.70, s32[1024]{0:T(1024)S(1)} %bitcast.149, bf16[1024,768]{1,0:T(8,128)(2,1)} %all-gather.18.cloned.1.call-done), kind=kCustom, calls=%fused_computation.27 | custom fusion | flops 1572864 | bytes 20889600 | tf_op jit(solution)/shard_map/scatter-add | solution.py:336
  485.6 38.3 %all-reduce.1 = f32[14,768]{1,0:T(8,128)S(1)} all-reduce(f32[14,768]{1,0:T(8,128)S(1)} %concatenate.12), channel_id=8, replica_groups=mesh['dp'=4,'vocab'=8] {'dp','vocab'}, use_global_device_ids=true, to_apply=%region_51.52.clone | all-reduce | flops 10752 | bytes 86016
  524.6 60.3 %all-reduce.9.cloned.1.call-done = f32[128,768]{1,0:T(8,128)} async-done(((f32[128,768]{1,0:T(8,128)}), f32[128,768]{1,0:T(8,128)}) %all-reduce.9.cloned.1.call-update) | async-done | bytes 393232
  586.2 102.8 %reduce-scatter.11.cloned.1.call-done = f32[24,768]{1,0:T(8,128)} async-done(((f32[768,768]{1,0:T(8,128)}), f32[24,768]{1,0:T(8,128)}) %reduce-scatter.11.cloned.1.call-update) | async-done | bytes 73744 | tf_op jit(solution)/shard_map/reduce_scatter | solution.py:374
  690.5 122.4 %reduce-scatter.9.cloned.1.call-done = f32[24,2304]{1,0:T(8,128)} async-done(((f32[768,2304]{1,0:T(8,128)}), f32[24,2304]{1,0:T(8,128)}) %reduce-scatter.9.cloned.1.call-update) | async-done | bytes 221200 | tf_op jit(solution)/shard_map/reduce_scatter | solution.py:373
  815.8 139.2 %reduce-scatter.13.cloned.1.call-done = f32[24,3072]{1,0:T(8,128)} async-done(((f32[768,3072]{1,0:T(8,128)}), f32[24,3072]{1,0:T(8,128)}) %reduce-scatter.13.cloned.1.call-update) | async-done | bytes 294928 | tf_op jit(solution)/shard_map/reduce_scatter | solution.py:375
  957.2 138.9 %reduce-scatter.15.cloned.1.call-done = f32[96,768]{1,0:T(8,128)} async-done(((f32[3072,768]{1,0:T(8,128)}), f32[96,768]{1,0:T(8,128)}) %reduce-scatter.15.cloned.1.call-update) | async-done | bytes 294928 | tf_op jit(solution)/shard_map/reduce_scatter | solution.py:376
  1099.7 348.5 %all-reduce.7.cloned.1.call-done = f32[6288,768]{1,0:T(8,128)} async-done(((f32[6288,768]{1,0:T(8,128)}), f32[6288,768]{1,0:T(8,128)}) %all-reduce.7.cloned.1.call-update) | async-done | bytes 19316752 | tf_op jit(solution)/shard_map/psum | solution.py:339
  1448.2 12.1 multiply_reduce_fusion.2
  1460.9 9.7 psum.59
  1470.7 39.5 %psum.61 = f32[]{:T(128)} all-reduce(f32[]{:T(128)S(6)} %add.498), channel_id=1, replica_groups=mesh['dp'=4,'vocab'=8] {'dp','vocab'}, use_global_device_ids=true, to_apply=%region_56.57 | all-reduce | flops 1 | bytes 8 | tf_op jit(solution)/shard_map/psum | solution.py:407
  1511.1 42.4 %multiply_reduce_fusion.1 = (f32[]{:T(128)}, f32[]{:T(128)}, f32[6288,768]{1,0:T(8,128)}, f32[6288,768]{1,0:T(8,128)}) fusion(f32[6288,768]{1,0:T(8,128)} %param.33, f32[6288,768]{1,0:T(8,128)} %all-reduce.7.cloned.1.call-done, f32[]{:T(128)S(6)} %min.3, f32[6288,768]{1,0:T(8,128)} %param.40, f32[6288,768]{1,0:T(8,128)} %param.47), kind=kLoop, calls=%fused_computation.12 | loop fusion | flops 86925312 | bytes 115900432 | tf_op jit(solution)/shard_map/reduce_sum | solution.py:405
  1559.7 2.0 multiply_reduce_fusion.16
  1561.7 4.0 stack.77
  1565.7 2.0 multiply_reduce_fusion.25
  1567.7 3.9 stack.85
  1572.3 41.0 %all-reduce.2 = (f32[7]{0:T(128)S(1)}, f32[7]{0:T(128)S(1)}) all-reduce(f32[7]{0:T(128)S(1)} %stack.85, f32[7]{0:T(128)S(1)} %stack.77), channel_id=1, replica_groups=mesh['dp'=4,'vocab'=8] {'dp','vocab'}, use_global_device_ids=true, to_apply=%region_72.73 | all-reduce | flops 14 | bytes 112 | tf_op jit(solution)/shard_map/psum | solution.py:427
  1623.6 27.1 %multiply_subtract_fusion = f32[6288,768]{1,0:T(8,128)} fusion(f32[6288,768]{1,0:T(8,128)} %param.33, f32[]{:T(128)} %bitcast.57, f32[6288,768]{1,0:T(8,128)} %get-tuple-element.109, f32[6288,768]{1,0:T(8,128)} %get-tuple-element.108), kind=kLoop, calls=%fused_computation.8 | loop fusion | flops 38633472 | bytes 77266944 | tf_op jit(solution)/shard_map/sub | solution.py:430
  (329 shorter events, 68.3 us)
Async XLA Ops:
  7.2 163.9 %all-gather.10.cloned.1.call-start = ((), (), s32[]{:S(2)}) async-start(), calls=%async_computation.6 | async-start | bytes 3649536 | tf_op jit(solution)/shard_map/all_gather | solution.py:267
  8.9 166.3 %all-gather.12.cloned.1.call-start = ((), (), s32[]{:S(2)}) async-start(), calls=%async_computation.7 | async-start | bytes 1216512 | tf_op jit(solution)/shard_map/all_gather | solution.py:268
  10.4 197.0 %all-gather.14.cloned.1.call-start = ((), (), s32[]{:S(2)}) async-start(), calls=%async_computation.8 | async-start | bytes 4866048 | tf_op jit(solution)/shard_map/all_gather | solution.py:269
  12.2 261.2 %all-gather.16.cloned.1.call-start = ((), (), s32[]{:S(2)}) async-start(), calls=%async_computation.9 | async-start | bytes 4866048 | tf_op jit(solution)/shard_map/all_gather | solution.py:270
  43.7 72.7 %copy-start.85 = (s32[1,64]{1,0:T(1,128)S(1)}, s32[1,64]{1,0:T(1,128)}, u32[]{:S(2)}) copy-start(s32[1,64]{1,0:T(1,128)} %param.26) | copy-start | bytes 772
  52.2 117.5 %all-to-all-start = ((bf16[8,64,768]{2,1,0:T(8,128)(2,1)}), bf16[8,64,768]{2,1,0:T(8,128)(2,1)S(1)}, u32[]{:S(2)}, u32[]{:S(2)}) async-start(bf16[8,64,768]{2,1,0:T(8,128)(2,1)} %select_select_fusion), calls=%async_computation | async-start | bytes 1572864 | tf_op jit(solution)/shard_map/all_to_all | solution.py:294
  55.8 347.1 %reduce-scatter.7.cloned.1.call-start = ((), (), s32[]{:S(2)}) async-start(), calls=%async_computation.10 | async-start | bytes 1769472 | tf_op jit(solution)/shard_map/reduce_scatter | solution.py:323
  56.9 112.8 %copy-start.86 = (s32[64]{0:T(128)}, s32[64]{0:T(128)S(1)}, u32[]{:S(2)}) copy-start(s32[64]{0:T(128)S(1)} %fusion.38) | copy-start | bytes 772
  174.4 33.1 %copy-start.34 = (bf16[128,768]{0,1:T(8,128)(2,1)}, bf16[128,768]{0,1:T(8,128)(2,1)S(1)}, u32[]{:S(2)}) copy-start(bf16[128,768]{0,1:T(8,128)(2,1)S(1)} %copy.84) | copy-start | bytes 589828
  174.7 32.7 %copy-start.45 = (f32[12,128]{1,0:T(8,128)}, f32[12,128]{1,0:T(8,128)S(1)}, u32[]{:S(2)}) copy-start(f32[12,128]{1,0:T(8,128)S(1)} %get-tuple-element.163) | copy-start | bytes 18436
  174.9 35.8 %copy-start.51 = (f32[12,128]{1,0:T(8,128)}, f32[12,128]{1,0:T(8,128)S(1)}, u32[]{:S(2)}) copy-start(f32[12,128]{1,0:T(8,128)S(1)} %fusion.20) | copy-start | bytes 18436
  175.2 32.3 %copy-start.30 = (bf16[12,64,128]{2,1,0:T(8,128)(2,1)}, bf16[12,64,128]{2,1,0:T(8,128)(2,1)S(1)}, u32[]{:S(2)}) copy-start(bf16[12,64,128]{2,1,0:T(8,128)(2,1)S(1)} %convolution_convert_fusion.2) | copy-start | bytes 589828
  177.0 96.4 %copy-start.53 = (f32[128]{0:T(128)}, f32[128]{0:T(128)S(1)}, u32[]{:S(2)}) copy-start(f32[128]{0:T(128)S(1)} %broadcast_multiply_fusion.1) | copy-start | bytes 1540
  177.2 96.2 %copy-start.82 = (f32[128]{0:T(128)}, f32[128]{0:T(128)S(1)}, u32[]{:S(2)}) copy-start(f32[128]{0:T(128)S(1)} %multiply_reduce_fusion.11) | copy-start | bytes 1540
  177.2 96.2 %copy-start.67 = (f32[128]{0:T(128)}, f32[128]{0:T(128)S(1)}, u32[]{:S(2)}) copy-start(f32[128]{0:T(128)S(1)} %fusion.40) | copy-start | bytes 1540
  371.5 91.1 %all-gather.18.cloned.1.call-start = ((), (), s32[]{:S(2)}) async-start(), calls=%async_computation.15 | async-start | bytes 1769472 | tf_op jit(solution)/shard_map/all_gather | solution.py:337
  429.2 155.6 %all-reduce.9.cloned.1.call-start = ((), (), s32[]{:S(2)}) async-start(), calls=%async_computation.17 | async-start | bytes 786432
  429.9 259.1 %reduce-scatter.11.cloned.1.call-start = ((), (), s32[]{:S(2)}) async-start(), calls=%async_computation.12 | async-start | bytes 2433024 | tf_op jit(solution)/shard_map/reduce_scatter | solution.py:374
  431.9 381.0 %reduce-scatter.9.cloned.1.call-start = ((), (), s32[]{:S(2)}) async-start(), calls=%async_computation.11 | async-start | bytes 7299072 | tf_op jit(solution)/shard_map/reduce_scatter | solution.py:373
  436.8 518.1 %reduce-scatter.13.cloned.1.call-start = ((), (), s32[]{:S(2)}) async-start(), calls=%async_computation.13 | async-start | bytes 9732096 | tf_op jit(solution)/shard_map/reduce_scatter | solution.py:375
  443.2 653.0 %reduce-scatter.15.cloned.1.call-start = ((), (), s32[]{:S(2)}) async-start(), calls=%async_computation.14 | async-start | bytes 9732096 | tf_op jit(solution)/shard_map/reduce_scatter | solution.py:376
  449.4 998.8 %all-reduce.7.cloned.1.call-start = ((), (), s32[]{:S(2)}) async-start(), calls=%async_computation.16 | async-start | bytes 38633472 | tf_op jit(solution)/shard_map/psum | solution.py:339
  1510.9 43.9 %copy-start.47 = (f32[14,24]{1,0:T(8,128)S(1)}, f32[14,24]{1,0:T(8,128)}, u32[]{:S(2)}) copy-start(f32[14,24]{1,0:T(8,128)} %param.32) | copy-start | bytes 4036
  1510.9 43.9 %copy-start.73 = (f32[14,24]{1,0:T(8,128)S(1)}, f32[14,24]{1,0:T(8,128)}, u32[]{:S(2)}) copy-start(f32[14,24]{1,0:T(8,128)} %param.39) | copy-start | bytes 4036
  1511.0 43.9 %copy-start.74 = (f32[14,24]{1,0:T(8,128)S(1)}, f32[14,24]{1,0:T(8,128)}, u32[]{:S(2)}) copy-start(f32[14,24]{1,0:T(8,128)} %param.46) | copy-start | bytes 4036
  1511.0 45.2 %copy-start.35 = (f32[24,768]{1,0:T(8,128)S(1)}, f32[24,768]{1,0:T(8,128)}, u32[]{:S(2)}) copy-start(f32[24,768]{1,0:T(8,128)} %param.28) | copy-start | bytes 221188
  1511.0 45.2 %copy-start.39 = (f32[24,768]{1,0:T(8,128)S(1)}, f32[24,768]{1,0:T(8,128)}, u32[]{:S(2)}) copy-start(f32[24,768]{1,0:T(8,128)} %reduce-scatter.11.cloned.1.call-done) | copy-start | bytes 221188
  1511.0 45.2 %copy-start.48 = (f32[24,768]{1,0:T(8,128)S(1)}, f32[24,768]{1,0:T(8,128)}, u32[]{:S(2)}) copy-start(f32[24,768]{1,0:T(8,128)} %param.35) | copy-start | bytes 221188
  1511.0 45.2 %copy-start.49 = (f32[24,768]{1,0:T(8,128)S(1)}, f32[24,768]{1,0:T(8,128)}, u32[]{:S(2)}) copy-start(f32[24,768]{1,0:T(8,128)} %param.42) | copy-start | bytes 221188
  1511.0 45.9 %copy-start.7 = (f32[24,2304]{1,0:T(8,128)S(1)}, f32[24,2304]{1,0:T(8,128)}, u32[]{:S(2)}) copy-start(f32[24,2304]{1,0:T(8,128)} %param.27) | copy-start | bytes 663556
  1511.0 45.8 %copy-start.25 = (f32[24,2304]{1,0:T(8,128)S(1)}, f32[24,2304]{1,0:T(8,128)}, u32[]{:S(2)}) copy-start(f32[24,2304]{1,0:T(8,128)} %reduce-scatter.9.cloned.1.call-done) | copy-start | bytes 663556
  1511.0 45.8 %copy-start.42 = (f32[24,2304]{1,0:T(8,128)S(1)}, f32[24,2304]{1,0:T(8,128)}, u32[]{:S(2)}) copy-start(f32[24,2304]{1,0:T(8,128)} %param.34) | copy-start | bytes 663556
  1511.0 47.6 %copy-start.5 = (f32[96,768]{1,0:T(8,128)S(1)}, f32[96,768]{1,0:T(8,128)}, u32[]{:S(2)}) copy-start(f32[96,768]{1,0:T(8,128)} %param.30) | copy-start | bytes 884740
  1511.1 47.6 %copy-start.20 = (f32[96,768]{1,0:T(8,128)S(1)}, f32[96,768]{1,0:T(8,128)}, u32[]{:S(2)}) copy-start(f32[96,768]{1,0:T(8,128)} %reduce-scatter.15.cloned.1.call-done) | copy-start | bytes 884740
  1511.1 47.6 %copy-start.36 = (f32[96,768]{1,0:T(8,128)S(1)}, f32[96,768]{1,0:T(8,128)}, u32[]{:S(2)}) copy-start(f32[96,768]{1,0:T(8,128)} %param.37) | copy-start | bytes 884740
  1511.1 47.6 %copy-start.37 = (f32[96,768]{1,0:T(8,128)S(1)}, f32[96,768]{1,0:T(8,128)}, u32[]{:S(2)}) copy-start(f32[96,768]{1,0:T(8,128)} %param.44) | copy-start | bytes 884740
  1511.1 48.6 %copy-start.6 = (f32[24,3072]{1,0:T(8,128)S(1)}, f32[24,3072]{1,0:T(8,128)}, u32[]{:S(2)}) copy-start(f32[24,3072]{1,0:T(8,128)} %param.29) | copy-start | bytes 884740
  1511.1 48.6 %copy-start.19 = (f32[24,3072]{1,0:T(8,128)S(1)}, f32[24,3072]{1,0:T(8,128)}, u32[]{:S(2)}) copy-start(f32[24,3072]{1,0:T(8,128)} %reduce-scatter.13.cloned.1.call-done) | copy-start | bytes 884740
  1511.1 48.6 %copy-start.38 = (f32[24,3072]{1,0:T(8,128)S(1)}, f32[24,3072]{1,0:T(8,128)}, u32[]{:S(2)}) copy-start(f32[24,3072]{1,0:T(8,128)} %param.36) | copy-start | bytes 884740
  1556.9 93.9 %copy-start.40 = (f32[24,768]{1,0:T(8,128)}, f32[24,768]{1,0:T(8,128)S(1)}, u32[]{:S(2)}) copy-start(f32[24,768]{1,0:T(8,128)S(1)} %get-tuple-element.120) | copy-start | bytes 221188
  1556.9 93.9 %copy-start.41 = (f32[24,768]{1,0:T(8,128)}, f32[24,768]{1,0:T(8,128)S(1)}, u32[]{:S(2)}) copy-start(f32[24,768]{1,0:T(8,128)S(1)} %get-tuple-element.121) | copy-start | bytes 221188
  1558.7 92.1 %copy-start.26 = (f32[24,2304]{1,0:T(8,128)}, f32[24,2304]{1,0:T(8,128)S(1)}, u32[]{:S(2)}) copy-start(f32[24,2304]{1,0:T(8,128)S(1)} %get-tuple-element.122) | copy-start | bytes 663556
  1558.7 92.1 %copy-start.27 = (f32[24,2304]{1,0:T(8,128)}, f32[24,2304]{1,0:T(8,128)S(1)}, u32[]{:S(2)}) copy-start(f32[24,2304]{1,0:T(8,128)S(1)} %get-tuple-element.123) | copy-start | bytes 663556
  1559.7 91.1 %copy-start.21 = (f32[96,768]{1,0:T(8,128)}, f32[96,768]{1,0:T(8,128)S(1)}, u32[]{:S(2)}) copy-start(f32[96,768]{1,0:T(8,128)S(1)} %get-tuple-element.116) | copy-start | bytes 884740
  1559.7 91.1 %copy-start.22 = (f32[96,768]{1,0:T(8,128)}, f32[96,768]{1,0:T(8,128)S(1)}, u32[]{:S(2)}) copy-start(f32[96,768]{1,0:T(8,128)S(1)} %get-tuple-element.117) | copy-start | bytes 884740
  1561.7 89.1 %copy-start.23 = (f32[24,3072]{1,0:T(8,128)}, f32[24,3072]{1,0:T(8,128)S(1)}, u32[]{:S(2)}) copy-start(f32[24,3072]{1,0:T(8,128)S(1)} %get-tuple-element.118) | copy-start | bytes 884740
  1561.7 89.1 %copy-start.24 = (f32[24,3072]{1,0:T(8,128)}, f32[24,3072]{1,0:T(8,128)S(1)}, u32[]{:S(2)}) copy-start(f32[24,3072]{1,0:T(8,128)S(1)} %get-tuple-element.119) | copy-start | bytes 884740
  1613.2 37.6 %copy-start.52 = (f32[7]{0:T(128)}, f32[7]{0:T(128)S(1)}, u32[]{:S(2)}) copy-start(f32[7]{0:T(128)S(1)} %rsqrt_multiply_fusion) | copy-start | bytes 88
  (55 other events, 223.5 us)
Sparse Core Ops, SparseCore 0:
  11.6 72.7 all-gather.9
  88.0 53.1 all-gather.11
  144.9 62.5 all-gather.13
  210.9 62.4 all-gather.15
  371.6 31.2 reduce-scatter.6
  429.3 23.2 all-gather.17
  457.9 126.9 all-reduce.8
  591.0 98.0 reduce-scatter.10
  694.7 118.1 reduce-scatter.8
  820.2 134.6 reduce-scatter.12
  961.4 134.6 reduce-scatter.14
  1100.6 347.6 all-reduce.6
where the time goes:
time: 1670 us; the launch traced here: 1660 us
  waiting for transfers between devices  1040 us (62%)
  blocking collectives  296 us (18%)
  other arithmetic  181 us (11%)
  matrix products  76.9 us (5%)
  local copies, waits for them, and re-layouts  36.4 us (2%)
  between operations  29.9 us (2%)
    psum x1, waiting for transfers between devices, shards(): table_grad, loss_total = lax.psum((table_grad, jnp.sum(row_loss)), 'dp')  348 us
    reduce_scatter x1, waiting for transfers between devices, shards(): lax.psum_scatter(matrix_grads[2], ('dp', 'vocab'), scatter_dimension=0, t...  139 us
    reduce_scatter x1, waiting for transfers between devices, shards(): lax.psum_scatter(matrix_grads[3], ('dp', 'vocab'), scatter_dimension=0, t...  139 us
    reduce_scatter x1, waiting for transfers between devices, shards(): lax.psum_scatter(matrix_grads[0], ('dp', 'vocab'), scatter_dimension=0, t...  122 us
    reduce_scatter x1, waiting for transfers between devices, shards(): lax.psum_scatter(matrix_grads[1], ('dp', 'vocab'), scatter_dimension=0, t...  103 us
    all_gather x1, waiting for transfers between devices, shards(): lax.all_gather(mlp_out.astype(jnp.bfloat16), ('dp', 'vocab'), axis=0, til...  62.7 us
    unnamed x13, waiting for transfers between devices  61.1 us
    all_gather x1, blocking collectives, shards(): lax.all_gather(positions.astype(jnp.bfloat16), ('dp', 'vocab'), axis=0, t...  59.4 us
  transfers between devices with their start and end apart: 13, of which 9 were waited for; matrix products, arithmetic and copies ran while one was open for 6% of the time, Pallas kernels for 0%

commit v1 on v0

v1 whole, which is shorter than its diff:
```python
import jax
import jax.numpy as jnp
from jax import lax
from jax.sharding import PartitionSpec as P

HD = 64
V_REAL = 50257
STEP = 5


LN_EPS = 1e-05
SMOOTHING = 0.1
BETA_ONE = 0.9
BETA_TWO = 0.999
ADAM_EPS = 1e-12
DECAY = 0.01
RATE = 0.3
CLIP_AT = 0.01
MASKED = -1e30


def layer_norm(inputs, gain, shift):
    centre = jnp.mean(inputs, axis=-1, keepdims=True)
    centred = inputs - centre
    spread = jnp.mean(centred * centred, axis=-1, keepdims=True)
    return centred * lax.rsqrt(spread + LN_EPS) * gain + shift


def gelu_tanh(inputs):
    return (
        0.5
        * inputs
        * (1.0 + jnp.tanh(0.7978845608028654 * (inputs + 0.044715 * inputs * inputs * inputs)))
    )


def dot_plain(left_op, right_op):
    return jnp.dot(left_op, right_op, preferred_element_type=jnp.float32)


def dot_first(left_op, right_op):
    return lax.dot_general(
        left_op, right_op, (((0,), (0,)), ((), ())), preferred_element_type=jnp.float32
    )


def dot_second(left_op, right_op):
    return lax.dot_general(
        left_op, right_op, (((1,), (1,)), ((), ())), preferred_element_type=jnp.float32
    )


def block_scores(query_blk, keys_all, offset):
    scores = jnp.einsum(
        "qhd,khd->hqk", query_blk, keys_all, preferred_element_type=jnp.float32
    ) * HD ** (-0.5)
    places = offset + jnp.arange(query_blk.shape[0])[:, None]
    causal = jnp.arange(keys_all.shape[0])[None, :] <= places
    return jnp.where(causal[None], scores, MASKED)


def split_blocks(queries):
    seq_len = queries.shape[0]
    block_rows = min(512, seq_len)
    count_blocks = seq_len // block_rows
    starts = jnp.arange(count_blocks, dtype=jnp.int32) * block_rows
    return (block_rows, count_blocks, starts)


def attention_forward(queries, keys_all, values_all):
    block_rows, count_blocks, starts = split_blocks(queries)
    stacked = queries.reshape(count_blocks, block_rows, queries.shape[1], queries.shape[2])

    def one_block(inputs):
        query_blk, offset = inputs
        scores = block_scores(query_blk, keys_all, offset)
        row_top = jnp.max(scores, axis=-1, keepdims=True)
        exp_scores = jnp.exp(scores - row_top)
        totals = jnp.sum(exp_scores, axis=-1, keepdims=True)
        attn_probs = (exp_scores / totals).astype(jnp.bfloat16)
        mixed_out = jnp.einsum(
            "hqk,khd->qhd", attn_probs, values_all, preferred_element_type=jnp.float32
        )
        return (mixed_out, (row_top + jnp.log(totals))[..., 0])

    mixed_out, log_total = lax.map(one_block, (stacked, starts))
    return (mixed_out.reshape(queries.shape), log_total)


def attention_backward(queries, keys_all, values_all, log_total, grad_mixed):
    block_rows, count_blocks, starts = split_blocks(queries)
    shape_blk = (count_blocks, block_rows, queries.shape[1], queries.shape[2])

    def one_block(carry, inputs):
        query_blk, grad_blk, lse_blk, offset = inputs
        scores = block_scores(query_blk, keys_all, offset)
        soft = jnp.exp(scores - lse_blk[..., None])
        grad_p = jnp.einsum(
            "qhd,khd->hqk", grad_blk, values_all, preferred_element_type=jnp.float32
        )
        centre = jnp.sum(soft * grad_p, axis=-1, keepdims=True)
        grad_s = (soft * (grad_p - centre)).astype(jnp.bfloat16)
        grad_q = jnp.einsum(
            "hqk,khd->qhd", grad_s, keys_all, preferred_element_type=jnp.float32
        ) * HD ** (-0.5)
        grad_k = carry[0] + jnp.einsum(
            "hqk,qhd->khd", grad_s, query_blk, preferred_element_type=jnp.float32
        ) * HD ** (-0.5)
        grad_v = carry[1] + jnp.einsum(
            "hqk,qhd->khd", soft.astype(jnp.bfloat16), grad_blk, preferred_element_type=jnp.float32
        )
        return ((grad_k, grad_v), grad_q)

    zeros_kv = jnp.zeros(keys_all.shape, jnp.float32)
    (grad_k, grad_v), grad_q = lax.scan(
        one_block,
        (zeros_kv, zeros_kv),
        (queries.reshape(shape_blk), grad_mixed.reshape(shape_blk), log_total, starts),
    )
    return (grad_q.reshape(queries.shape), grad_k, grad_v)


def layer_forward(resid_in, w_qkv, w_proj, w_up, w_down, vec_rows):
    seq_len, width = resid_in.shape
    head_count = width // HD
    normed_one = layer_norm(resid_in, vec_rows[0], vec_rows[1]).astype(jnp.bfloat16)
    qkv_bias = jnp.concatenate([vec_rows[6], jnp.zeros_like(vec_rows[6]), vec_rows[7]])
    packed = (dot_plain(normed_one, w_qkv) + qkv_bias).astype(jnp.bfloat16)
    queries = packed[:, :width].reshape(seq_len, head_count, HD)
    keys_all = packed[:, width : 2 * width].reshape(seq_len, head_count, HD)
    values_all = packed[:, 2 * width :].reshape(seq_len, head_count, HD)
    attended, log_total = attention_forward(queries, keys_all, values_all)
    attended = attended.reshape(seq_len, width).astype(jnp.bfloat16)
    resid_mid = resid_in + dot_plain(attended, w_proj) + vec_rows[8]
    normed_two = layer_norm(resid_mid, vec_rows[2], vec_rows[3]).astype(jnp.bfloat16)
    hidden_pre = dot_plain(normed_two, w_up) + vec_rows[10:14].reshape(-1)
    hidden_act = gelu_tanh(hidden_pre).astype(jnp.bfloat16)
    resid_out = resid_mid + dot_plain(hidden_act, w_down) + vec_rows[9]
    kept = (
        resid_in,
        resid_mid,
        normed_one,
        normed_two,
        queries,
        keys_all,
        values_all,
        log_total,
        attended,
        hidden_pre,
        hidden_act,
    )
    return (resid_out, kept)


def layer_backward(grad_out, kept, w_qkv, w_proj, w_up, w_down, vec_rows):
    (
        resid_in,
        resid_mid,
        normed_one,
        normed_two,
        queries,
        keys_all,
        values_all,
        log_total,
        attended,
        hidden_pre,
        hidden_act,
    ) = kept
    seq_len, width = resid_in.shape
    devices = lax.axis_size("dp") * lax.axis_size("vocab")
    grad_branch = grad_out.astype(jnp.bfloat16)
    grad_down = grad_shard(hidden_act, grad_branch, hidden_act.shape[1] // devices, halves(width))
    bias_down = jnp.sum(grad_branch.astype(jnp.float32), axis=0)
    grad_act = dot_second(grad_branch, w_down)
    grad_pre = jax.vjp(gelu_tanh, hidden_pre)[1](grad_act)[0].astype(jnp.bfloat16)
    grad_up = grad_shard(normed_two, grad_pre, width // devices, halves(grad_pre.shape[1]))
    bias_up = jnp.sum(grad_pre.astype(jnp.float32), axis=0)
    grad_two = dot_second(grad_pre, w_up)
    grad_mid, gain_two, shift_two = jax.vjp(layer_norm, resid_mid, vec_rows[2], vec_rows[3])[1](
        grad_two
    )
    grad_mid = grad_mid + grad_out
    grad_attn = grad_mid.astype(jnp.bfloat16)
    grad_proj = grad_shard(attended, grad_attn, width // devices, halves(width))
    bias_proj = jnp.sum(grad_attn.astype(jnp.float32), axis=0)
    grad_mixed = dot_second(grad_attn, w_proj).astype(jnp.bfloat16).reshape(queries.shape)
    grad_q, grad_k, grad_v = attention_backward(
        queries, keys_all, values_all, log_total, grad_mixed
    )
    grad_packed = jnp.concatenate(
        [
            grad_q.reshape(seq_len, width),
            grad_k.reshape(seq_len, width),
            grad_v.reshape(seq_len, width),
        ],
        axis=1,
    ).astype(jnp.bfloat16)
    grad_qkv = grad_shard(normed_one, grad_packed, width // devices, halves(3 * width))
    bias_qkv = jnp.sum(grad_packed.astype(jnp.float32), axis=0)
    grad_one = dot_second(grad_packed, w_qkv)
    grad_in, gain_one, shift_one = jax.vjp(layer_norm, resid_in, vec_rows[0], vec_rows[1])[1](
        grad_one
    )
    grad_in = grad_in + grad_mid
    vec_grads = (
        gain_one,
        shift_one,
        gain_two,
        shift_two,
        bias_qkv[:width],
        bias_qkv[2 * width :],
        bias_proj,
        bias_down,
        bias_up.reshape(4, width),
    )
    return (grad_in, (grad_qkv, grad_proj, grad_up, grad_down), vec_grads)


def bit_of(index, level):
    return (index >> level) & 1


def xor_order(parts, index):
    level = 0
    while (1 << level) < len(parts):
        odd = bit_of(index, level) == 1
        step = 1 << level
        placed = list(parts)
        for place in range(len(parts)):
            if not place & step:
                low, high = parts[place], parts[place | step]
                placed[place] = jnp.where(odd, high, low)
                placed[place | step] = jnp.where(odd, low, high)
        parts = placed
        level += 1
    return parts


def tree_sum(parts):
    while len(parts) > 1:
        parts = [parts[place] + parts[place + 1] for place in range(0, len(parts), 2)]
    return parts[0]


def swap_core(value):
    count = lax.axis_size("vocab")
    return lax.ppermute(value, "vocab", [(i, i ^ 1) for i in range(count)])


def swap_outer(value, step):
    count = lax.axis_size("vocab")
    return lax.ppermute(value, "vocab", [(i, i ^ (2 * step)) for i in range(count)])


def swap_dp(value, step):
    count = lax.axis_size("dp")
    return lax.ppermute(value, "dp", [(i, i ^ step) for i in range(count)])


def places():
    vocab_index = lax.axis_index("vocab")
    return (lax.axis_index("dp"), vocab_index // 2, vocab_index % 2)


def gather_vocab(value):
    _, outer, core = places()
    pair = jnp.stack(xor_order([value, swap_core(value)], core))
    count = lax.axis_size("vocab") // 2
    parts = [pair] + [swap_outer(pair, step) for step in range(1, count)]
    return jnp.concatenate(xor_order(parts, outer), axis=0)


def gather_dp(value):
    dp_index, _, _ = places()
    parts = [value] + [swap_dp(value, step) for step in range(1, lax.axis_size("dp"))]
    return jnp.stack(xor_order(parts, dp_index))


def sum_all(value):
    value = value + swap_core(value)
    value = tree_sum([value] + [swap_dp(value, step) for step in range(1, lax.axis_size("dp"))])
    count = lax.axis_size("vocab") // 2
    return tree_sum([value] + [swap_outer(value, step) for step in range(1, count)])


def gather_all(value, flip):
    dp_index, outer, core = places()
    count = lax.axis_size("vocab") // 2
    parts = [value] + [swap_outer(value, step) for step in range(1, count)]
    held = jnp.stack(xor_order(parts, outer))
    held = held[None, None]
    for bit in (0, 1) if flip else (1, 0):
        other = swap_dp(held, 1 << bit)
        held = jnp.concatenate(xor_order([held, other], bit_of(dp_index, bit)), axis=1 - bit)
    held = held.reshape((-1,) + value.shape)
    return jnp.stack(xor_order([held, swap_core(held)], core), axis=1).reshape(
        (-1,) + value.shape[1:]
    )


def pick_half(value, index, axis):
    return lax.dynamic_index_in_dim(value, index, axis, keepdims=False)


def scatter_sum(keep, sent, flip):
    dp_index, outer, _ = places()
    count = lax.axis_size("vocab") // 2
    held = keep + swap_core(sent.astype(jnp.bfloat16)).astype(jnp.float32)
    held = held.reshape((2, 2, count) + keep.shape[1:])
    first, second = (0, 1) if flip else (1, 0)
    own = bit_of(dp_index, first)
    axis = 1 - first
    out = pick_half(held, 1 - own, axis).astype(jnp.bfloat16)
    held = pick_half(held, own, axis) + swap_dp(out, 1 << first).astype(jnp.float32)
    own = bit_of(dp_index, second)
    out = pick_half(held, 1 - own, 0).astype(jnp.bfloat16)
    held = pick_half(held, own, 0) + swap_dp(out, 1 << second).astype(jnp.float32)
    terms = [pick_half(held, outer, 0)]
    for step in range(1, count):
        out = pick_half(held, outer ^ step, 0).astype(jnp.bfloat16)
        terms.append(swap_outer(out, step).astype(jnp.float32))
    return tree_sum(terms)


def core_split(value, rows):
    _, _, core = places()
    tokens = value.shape[0]
    grouped = value.reshape(tokens, -1, 2, rows)
    keep = pick_half(grouped, core, 2).reshape(tokens, -1)
    sent = pick_half(grouped, 1 - core, 2).reshape(tokens, -1)
    return (keep, sent)


def grad_shard(left, right, rows, cuts):
    keep_cols, sent_cols = core_split(left, rows)
    made = []
    for place, (start, stop) in enumerate(cuts):
        piece = right[:, start:stop]
        sent = dot_first(sent_cols, piece).astype(jnp.bfloat16)
        keep = dot_first(keep_cols, piece)
        shape = (-1, rows, stop - start)
        made.append(scatter_sum(keep.reshape(shape), sent.reshape(shape), place % 2 == 1))
    return jnp.concatenate(made, axis=1)


def halves(width):
    return ((0, width // 2), (width // 2, width))


def shards(
    token_ids,
    pick_rows,
    target_ids,
    attn_in,
    attn_out,
    mlp_in,
    mlp_out,
    positions,
    vectors,
    table,
    *moments,
):
    low = jnp.bfloat16
    dp_index, outer, core = places()
    dp_count = lax.axis_size("dp")
    shard_count = lax.axis_size("vocab")
    device_count = dp_count * shard_count
    outer_count = shard_count // 2
    vocab_rows, width = table.shape
    seq_len = token_ids.shape[1]
    pick_count = pick_rows.shape[1]
    vocab_start = lax.axis_index("vocab") * vocab_rows

    packed_ids = jnp.concatenate([token_ids, target_ids], axis=1)
    group_packed = gather_vocab(packed_ids).reshape(shard_count, -1)
    group_ids = group_packed[:, :seq_len]
    group_targets = group_packed[:, seq_len:]

    small_rows = positions.shape[0]
    vec_flat = vectors.astype(low).reshape(-1)
    vec_pad = -vec_flat.size % width
    small = jnp.concatenate(
        [positions.astype(low), jnp.pad(vec_flat, (0, vec_pad)).reshape(-1, width)], axis=0
    )
    small_all = gather_all(small, False).reshape((device_count,) + small.shape)
    pos_low = small_all[:, :small_rows].reshape(-1, width)
    vec_low = small_all[:, small_rows:].reshape(device_count, -1)[:, : vec_flat.size]
    vec_low = vec_low.reshape((device_count,) + vectors.shape)
    vec_rows = jnp.moveaxis(vec_low, 0, 1).reshape(vectors.shape[0], width).astype(jnp.float32)

    def gather_weight(weight):
        return jnp.concatenate(
            [
                gather_all(weight[:, start:stop].astype(low), place % 2 == 1)
                for place, (start, stop) in enumerate(halves(weight.shape[1]))
            ],
            axis=1,
        )

    w_qkv = gather_weight(attn_in)
    w_proj = gather_weight(attn_out)
    w_up = gather_weight(mlp_in)
    w_down = gather_weight(mlp_out)
    table_low = table.astype(low)

    group_local = group_ids - vocab_start
    mine = (group_local >= 0) & (group_local < vocab_rows)
    served = jnp.take(table, jnp.where(mine, group_local, 0).reshape(-1), axis=0)
    served = jnp.where(mine.reshape(-1)[:, None], served, 0.0).astype(low)
    served = served.reshape(outer_count, 2, seq_len, width)
    held = pick_half(served, core, 1) + swap_core(pick_half(served, 1 - core, 1))
    terms = [pick_half(held, outer, 0)]
    for step in range(1, outer_count):
        terms.append(swap_outer(pick_half(held, outer ^ step, 0), step))
    resid_in = tree_sum(terms).astype(jnp.float32) + pos_low.astype(jnp.float32)

    resid_out, kept = layer_forward(resid_in, w_qkv, w_proj, w_up, w_down, vec_rows)
    final_low = layer_norm(resid_out, vec_rows[4], vec_rows[5]).astype(low)
    own_picks = pick_rows.reshape(-1)
    pick_hot = own_picks[:, None] == jnp.arange(seq_len, dtype=jnp.int32)[None, :]
    picked = dot_plain(pick_hot.astype(low), final_low).astype(low)

    _parts = [picked] + [swap_outer(picked, step) for step in range(1, outer_count)]
    same_core = jnp.stack(xor_order(_parts, outer))
    head_in = jnp.stack(xor_order([same_core, swap_core(same_core)], core), axis=1)
    head_in = head_in.reshape(-1, width)
    columns = vocab_start + jnp.arange(vocab_rows, dtype=jnp.int32)
    is_real = columns < V_REAL
    flat_targets = group_targets.reshape(-1)
    logits = jnp.where(is_real[None, :], dot_second(head_in, table_low), MASKED)
    is_target = columns[None, :] == flat_targets[:, None]
    target_part = jnp.sum(jnp.where(is_target, logits, 0.0), axis=1)
    logit_part = jnp.sum(jnp.where(is_real[None, :], logits, 0.0), axis=1)
    top_part = jnp.max(logits, axis=1)
    exp_part = jnp.sum(jnp.exp(logits - top_part[:, None]), axis=1)
    stats = gather_vocab(jnp.stack([top_part, exp_part, target_part, logit_part]))
    stats = stats.reshape(shard_count, 4, -1)
    row_top = jnp.max(stats[:, 0], axis=0)
    exp_total = jnp.sum(stats[:, 1] * jnp.exp(stats[:, 0] - row_top[None]), axis=0)
    target_logit = jnp.sum(stats[:, 2], axis=0)
    logit_total = jnp.sum(stats[:, 3], axis=0)
    log_norm = row_top + jnp.log(exp_total)
    row_loss = (1.0 - SMOOTHING) * (log_norm - target_logit) + SMOOTHING * (
        log_norm - logit_total / V_REAL
    )
    token_count = device_count * pick_count

    def logit_grad(values, norms, targets):
        soft = jnp.exp(values - norms[:, None])
        hit = columns[None, :] == targets[:, None]
        return (
            (soft - (1.0 - SMOOTHING) * hit - SMOOTHING / V_REAL * is_real[None, :]) / token_count
        ).astype(low)

    partial = dot_plain(logit_grad(logits, log_norm, flat_targets), table_low)
    partial = partial.reshape(outer_count, 2, pick_count, width)
    held = pick_half(partial, core, 1) + swap_core(
        pick_half(partial, 1 - core, 1).astype(low)
    ).astype(jnp.float32)
    terms = [pick_half(held, outer, 0)]
    for step in range(1, outer_count):
        out = pick_half(held, outer ^ step, 0).astype(low)
        terms.append(swap_outer(out, step).astype(jnp.float32))
    picked_grad = tree_sum(terms)
    final_grad = lax.dot_general(
        pick_hot.astype(jnp.float32),
        picked_grad,
        (((0,), (0,)), ((), ())),
        precision=lax.Precision.HIGHEST,
        preferred_element_type=jnp.float32,
    )

    half = lax.dynamic_slice_in_dim(head_in, core * (width // 2), width // 2, axis=1)
    half_all = half[None]
    for bit in (0, 1):
        half_all = jnp.concatenate(
            xor_order([half_all, swap_dp(half_all, 1 << bit)], bit_of(dp_index, bit)), axis=0
        )
    head_all = jnp.concatenate(xor_order([half_all, swap_core(half_all)], core), axis=2)
    head_all = head_all.reshape(-1, width)
    norm_all = gather_dp(log_norm).reshape(-1)
    packed_all = gather_dp(group_packed).reshape(device_count, -1)
    ids_all = packed_all[:, :seq_len].reshape(-1)
    targets_all = packed_all[:, seq_len:].reshape(-1)

    grad_top, gain_final, shift_final = jax.vjp(layer_norm, resid_out, vec_rows[4], vec_rows[5])[1](
        final_grad
    )
    grad_in, matrix_grads, vec_grads = layer_backward(
        grad_top, kept, w_qkv, w_proj, w_up, w_down, vec_rows
    )
    grad_rows = grad_in.astype(low)
    rows_all = jnp.concatenate(
        [
            gather_all(grad_rows[:, start:stop], place % 2 == 1)
            for place, (start, stop) in enumerate(halves(width))
        ],
        axis=1,
    )

    all_logits = jnp.where(is_real[None, :], dot_second(head_all, table_low), MASKED)
    table_grad = dot_first(logit_grad(all_logits, norm_all, targets_all), head_all)
    local_all = ids_all - vocab_start
    inside = (local_all >= 0) & (local_all < vocab_rows)
    table_grad = table_grad.at[jnp.where(inside, local_all, vocab_rows)].add(
        rows_all.astype(jnp.float32), mode="drop"
    )
    loss = tree_sum(
        [jnp.sum(row_loss)[None]]
        + [swap_dp(jnp.sum(row_loss)[None], step) for step in range(1, dp_count)]
    )[0] / token_count
    (
        gain_one,
        shift_one,
        gain_two,
        shift_two,
        bias_query,
        bias_value,
        bias_proj,
        bias_down,
        bias_up,
    ) = vec_grads
    vec_grad = jnp.concatenate(
        [
            jnp.stack(
                [
                    gain_one,
                    shift_one,
                    gain_two,
                    shift_two,
                    gain_final,
                    shift_final,
                    bias_query,
                    bias_value,
                    bias_proj,
                    bias_down,
                ]
            ),
            bias_up,
        ],
        axis=0,
    )
    vec_total = sum_all(vec_grad)
    vec_width = vectors.shape[1]
    device_index = lax.axis_index(("dp", "vocab"))
    vec_own = lax.dynamic_slice_in_dim(vec_total, device_index * vec_width, vec_width, axis=1)
    grad_blocks = grad_in.reshape(-1, 2, small_rows, width)
    pos_own = scatter_sum(
        pick_half(grad_blocks, core, 1), pick_half(grad_blocks, 1 - core, 1), False
    )
    gradients = tuple(matrix_grads) + (pos_own, vec_own, table_grad)
    masters = (attn_in, attn_out, mlp_in, mlp_out, positions, vectors, table)
    firsts = moments[:7]
    seconds = moments[7:]
    shares = (1.0, 1.0, 1.0, 1.0, 1.0, 1.0, 1.0 / dp_count)
    clip_term = sum(
        (jnp.sum(gradient * gradient) * share for gradient, share in zip(gradients, shares))
    )
    weight_terms = [jnp.sum(weight * weight) * share for weight, share in zip(masters, shares)]
    sums = sum_all(jnp.stack([clip_term] + weight_terms))
    clip_total, weight_total = sums[0], sums[1:]
    grad_norm = jnp.sqrt(clip_total)
    factor = jnp.minimum(1.0, CLIP_AT / grad_norm)
    new_firsts, new_seconds, updates, update_terms = ([], [], [], [])
    for weight, gradient, moment_one, moment_two, share in zip(
        masters, gradients, firsts, seconds, shares
    ):
        clipped = gradient * factor
        moment_one = BETA_ONE * moment_one + (1.0 - BETA_ONE) * clipped
        moment_two = BETA_TWO * moment_two + (1.0 - BETA_TWO) * clipped * clipped
        update = (
            moment_one
            / (1.0 - BETA_ONE**STEP)
            / (jnp.sqrt(moment_two / (1.0 - BETA_TWO**STEP)) + ADAM_EPS)
            + DECAY * weight
        )
        new_firsts.append(moment_one)
        new_seconds.append(moment_two)
        updates.append(update)
        update_terms.append(jnp.sum(update * update) * share)
    update_total = sum_all(jnp.stack(update_terms))
    ratios = jnp.sqrt(weight_total) / jnp.sqrt(update_total)
    new_weights = [
        weight - RATE * ratios[index] * update
        for index, (weight, update) in enumerate(zip(masters, updates))
    ]
    return (loss, grad_norm, ratios, *new_weights, *new_firsts, *new_seconds)


def solution(mesh):
    rows = P(("dp", "vocab"), None)
    weights = (rows, rows, rows, rows, rows, P(None, ("dp", "vocab")), P("vocab", None))
    return jax.shard_map(
        shards,
        mesh=mesh,
        in_specs=(rows, rows, rows) + weights * 3,
        out_specs=(P(), P(), P()) + weights * 3,
        check_vma=False,
    )
```

time: 1670 us -> 833 us (0.50)
  waiting for transfers between devices: 1040 us -> 195 us
  blocking collectives: 296 us -> 0 us
  starting transfers between devices: 4.25 us -> 181 us
  other arithmetic: 181 us -> 248 us
  matrix products: 76.9 us -> 124 us
  local copies, waits for them, and re-layouts: 36.4 us -> 62.7 us
    reduce_scatter x5 -> x0, waiting for transfers between devices: 533 us -> none  [the longest x1 139 us: shards(): lax.psum_scatter(matrix_grads[2], ('dp', 'vocab'), scatter_dimension=0, t...]
    psum x1 -> x0, waiting for transfers between devices: 348 us -> none  [shards(): table_grad, loss_total = lax.psum((table_grad, jnp.sum(row_loss)), 'dp')]
    ppermute x0 -> x173, waiting for transfers between devices: none -> 195 us  [the longest x60 125 us: swap_dp(): return lax.ppermute(value, 'dp', [(i, i ^ step) for i in range(count)])]
    ppermute x0 -> x173, starting transfers between devices: none -> 181 us  [the longest x84 112 us: swap_outer(): lax.ppermute(value, 'vocab', [(i, i ^ 2 * step) for i in range(count)])]
    all_gather x5 -> x0, blocking collectives: 136 us -> none  [the longest x1 59.4 us: shards(): lax.all_gather(positions.astype(jnp.bfloat16), ('dp', 'vocab'), axis=0, t...]
    psum x4 -> x0, blocking collectives: 105 us -> none  [the longest x1 41 us: shards(): update_total = lax.psum(jnp.stack(update_terms), ('dp', 'vocab'))]
    all_gather x5 -> x0, waiting for transfers between devices: 93 us -> none  [the longest x1 62.7 us: shards(): lax.all_gather(mlp_out.astype(jnp.bfloat16), ('dp', 'vocab'), axis=0, til...]
    unnamed x13 -> x0, waiting for transfers between devices: 61.1 us -> none
  transfers between devices with their start and end apart: 13 -> 173, of which waited for: 9 -> 72; matrix products, arithmetic and copies ran while one was open for 6% -> 29% of each run, Pallas kernels for 0% -> 0%
where the time goes in v1:
time: 833 us
  other arithmetic  248 us (30%)
  waiting for transfers between devices  195 us (23%)
  starting transfers between devices  181 us (22%)
  matrix products  124 us (15%)
  local copies, waits for them, and re-layouts  62.7 us (8%)
  between operations  20.6 us (2%)
    ppermute x60, waiting for transfers between devices, swap_dp(): return lax.ppermute(value, 'dp', [(i, i ^ step) for i in range(count)])  125 us
    ppermute x84, starting transfers between devices, swap_outer(): lax.ppermute(value, 'vocab', [(i, i ^ 2 * step) for i in range(count)])  112 us
    ppermute x84, waiting for transfers between devices, swap_outer(): lax.ppermute(value, 'vocab', [(i, i ^ 2 * step) for i in range(count)])  65.9 us
    ppermute x60, starting transfers between devices, swap_dp(): return lax.ppermute(value, 'dp', [(i, i ^ step) for i in range(count)])  64.5 us
    dot_general x6, matrix products, dot_second(): lax.dot_general(left_op, right_op, (((1,), (1,)), ((), ())), preferred_el...  60 us
    reduce_sum x7, other arithmetic, shards(): update_terms.append(jnp.sum(update * update) * share)  48.9 us
    scatter-add x1, other arithmetic, shards(): table_grad.at[jnp.where(inside, local_all, vocab_rows)]  41.4 us
    dot_general x17, matrix products, dot_first(): lax.dot_general(left_op, right_op, (((0,), (0,)), ((), ())), preferred_el...  39.9 us
  transfers between devices with their start and end apart: 173, of which 72 were waited for; matrix products, arithmetic and copies ran while one was open for 29% of the time, Pallas kernels for 0%

profile of v1, /device:TPU:0, one launch (start us, length us, event | category | flops | bytes accessed | tf_op | source)
XLA Modules:
  0.0 832.6 jit_solution(9884648860558957398)
XLA Ops:
  4.8 3.0 collective-permute-start.10
  14.1 12.1 %multiply_reduce_fusion.1 = f32[]{:T(128)} fusion(f32[6288,768]{1,0:T(8,128)} %param.33), kind=kLoop, calls=%fused_computation.9 | loop fusion | flops 9658367 | bytes 19316740 | tf_op jit(solution)/shard_map/reduce_sum | solution.py:559
  29.7 3.9 collective-permute-start.1
  36.9 4.3 collective-permute-start.27
  42.5 11.0 %gather_fusion = bf16[1024,768]{1,0:T(8,128)(2,1)S(1)} fusion(f32[6288,768]{1,0:T(8,128)} %param.33, s32[1024]{0:T(1024)S(1)} %broadcast_clamp_fusion), kind=kCustom, calls=%fused_computation | custom fusion | bytes 3149824 | tf_op jit(solution)/shard_map/jit(_take)/gather | solution.py:408
  78.8 3.1 collective-permute-done.11
  109.9 3.3 collective-permute-done.45
  138.1 4.1 collective-permute-done.36
  146.5 4.3 collective-permute-done.23
  157.7 5.7 collective-permute-done.59
  168.9 4.0 collective-permute-done.18
  178.6 6.9 collective-permute-done.42
  187.4 9.1 %collective-permute-done.54 = bf16[2,1,4,96,384]{4,3,2,1,0:T(8,128)(2,1)S(1)} collective-permute-done((bf16[2,1,4,96,384]{4,3,2,1,0:T(8,128)(2,1)S(1)}, bf16[2,1,4,96,384]{4,3,2,1,0:T(8,128)(2,1)S(1)}, u32[]{:S(2)}, u32[]{:S(2)}) %collective-permute-start.54) | collective-permute-done | bytes 589856 | tf_op jit(solution)/shard_map/ppermute | solution.py:257
  199.9 7.1 collective-permute-done.6
  211.7 12.5 %select_bitcast_fusion.13 = (bf16[16,1,24,1152]{3,2,0,1:T(8,128)(2,1)S(1)}, bf16[16,1,24,1152]{3,2,0,1:T(8,128)(2,1)S(1)}) fusion(bf16[16,24,1152]{2,1,0:T(8,128)(2,1)S(1)} %collective-permute-done.25, pred[]{:T(512)S(6)} %eq.59, bf16[2,2,4,24,1152]{4,3,2,1,0:T(8,128)(2,1)S(1)} %pad_maximum_fusion.33), kind=kLoop, calls=%fused_computation.126 | loop fusion | flops 884736 | bytes 3538945 | tf_op jit(solution)/shard_map/stack | solution.py:296
  232.5 3.3 select_bitcast_fusion.5
  240.1 3.5 multiply_convert_fusion.1
  251.2 5.0 collective-permute-done.63
  261.7 13.2 %fusion.246 = (f32[512]{0:T(512)S(1)}, f32[512,6288]{0,1:T(8,128)}) fusion(bf16[512,768]{1,0:T(8,128)(2,1)S(1)} %bitcast.733, f32[6288,768]{1,0:T(8,128)} %param.33, pred[6288]{0:T(1024)(128)(4,1)S(1)} %copy-done.153), kind=kOutput, calls=%fused_computation.757 | convolution fusion | flops 4956352000 | bytes 32989328 | tf_op jit(solution)/shard_map/dot_general | solution.py:48
  275.0 8.1 exponential_reduce_fusion
  296.7 14.8 %fusion.9 = f32[512,768]{1,0:T(8,128)S(1)} fusion(f32[512,6288]{0,1:T(8,128)S(1)} %copy-done, f32[6288]{0:T(1024)S(1)} %copy-done.170, f32[512]{0:T(512)S(1)} %get-tuple-element.133, s32[512]{0:T(512)S(1)} %copy-done.189, s32[6288]{0:T(1024)S(1)} %copy-done.138, f32[6288,768]{1,0:T(8,128)} %param.33), kind=kOutput, calls=%fused_computation.24 | convolution fusion | flops 4972449792 | bytes 33821824 | tf_op jit(solution)/shard_map/dot_general | solution.py:38
  312.3 3.0 collective-permute-done.70
  333.7 4.8 collective-permute-done.75
  340.7 3.4 convert_reduce_fusion
  352.8 4.9 multiply_reduce_fusion.6
  382.8 4.2 collective-permute-done.148
  388.1 3.0 collective-permute-done.126
  391.9 3.2 collective-permute-done.127
  395.0 3.2 collective-permute-start.135
  417.0 7.5 collective-permute-done.90
  437.4 2.9 collective-permute-done.100
  459.1 8.6 %collective-permute-done.151 = bf16[2,1,4,128,384]{4,3,2,1,0:T(8,128)(2,1)S(1)} collective-permute-done((bf16[2,1,4,128,384]{4,3,2,1,0:T(8,128)(2,1)S(1)}, bf16[2,1,4,128,384]{4,3,2,1,0:T(8,128)(2,1)S(1)}, u32[]{:S(2)}, u32[]{:S(2)}) %collective-permute-start.151) | collective-permute-done | bytes 786464 | tf_op jit(solution)/shard_map/ppermute | solution.py:257
  470.3 5.9 collective-permute-done.84
  481.6 13.0 %collective-permute-done.85 = bf16[4,24,1152]{2,1,0:T(8,128)(2,1)S(1)} collective-permute-done((bf16[4,24,1152]{2,1,0:T(8,128)(2,1)S(1)}, bf16[4,24,1152]{2,1,0:T(8,128)(2,1)S(1)}, u32[]{:S(2)}, u32[]{:S(2)}) %collective-permute-start.85) | collective-permute-done | bytes 221216 | tf_op jit(solution)/shard_map/ppermute | solution.py:257
  514.5 6.7 collective-permute-done.120
  526.2 7.6 collective-permute-done.108
  536.3 5.3 collective-permute-done.103
  544.7 3.6 collective-permute-done.109
  559.3 3.5 collective-permute-start.116
  563.8 3.7 collective-permute-done.111
  583.3 35.7 %multiply_convert_fusion.clone.4 = bf16[2048,6288]{0,1:T(8,128)(2,1)} fusion(bf16[2048,768]{1,0:T(8,128)(2,1)S(1)} %bitcast.750, f32[6288]{0:T(1024)S(1)} %copy-done.171, s32[2048]{0:T(1024)S(1)} %copy-done.187, f32[2048]{0:T(1024)S(1)} %bitcast.834, s32[6288]{0:T(1024)S(1)} %copy-done.139, pred[6288]{0:T(1024)(128)(4,1)S(1)} %copy-done.153, ...), kind=kOutput, calls=%fused_computation.2.clone.clone.clone.1 | convolution fusion | flops 19888189440 | bytes 48291088 | tf_op jit(solution)/shard_map/dot_general | solution.py:48
  619.0 26.8 %fusion.8 = f32[6288,768]{1,0:T(8,128)} fusion(bf16[2048,768]{1,0:T(8,128)(2,1)S(1)} %bitcast.751, bf16[2048,6288]{0,1:T(8,128)(2,1)} %multiply_convert_fusion.clone.4), kind=kOutput, calls=%fused_computation.23 | convolution fusion | flops 19780337664 | bytes 48218112 | tf_op jit(solution)/shard_map/dot_general | solution.py:42
  653.0 41.4 %scatter_custom_fusion = f32[6288,768]{1,0:T(8,128)} fusion(f32[6288,768]{1,0:T(8,128)} %fusion.8, s32[4096]{0:T(1024)} %bitcast.832, bf16[4096,384]{1,0:T(8,128)(2,1)} %bitcast.724, bf16[]{:T(256)} %constant.618, bf16[4096,384]{1,0:T(8,128)(2,1)S(1)} %bitcast.723), kind=kCustom, calls=%fused_computation.20 | custom fusion | flops 15728640 | bytes 25608704 | tf_op jit(solution)/shard_map/scatter-add | solution.py:505
  694.4 12.1 %multiply_reduce_fusion.2 = f32[]{:T(128)} fusion(f32[6288,768]{1,0:T(8,128)} %scatter_custom_fusion), kind=kLoop, calls=%fused_computation.10 | loop fusion | flops 9658367 | bytes 19316740 | tf_op jit(solution)/shard_map/reduce_sum | solution.py:557
  707.1 4.0 stack.549
  725.2 41.7 %multiply_reduce_fusion = (f32[]{:T(128)}, f32[6288,768]{1,0:T(8,128)}, f32[6288,768]{1,0:T(8,128)}) fusion(f32[6288,768]{1,0:T(8,128)} %param.33, f32[6288,768]{1,0:T(8,128)} %scatter_custom_fusion, f32[]{:T(128)S(6)} %min.3, f32[6288,768]{1,0:T(8,128)} %param.40, f32[6288,768]{1,0:T(8,128)} %param.47), kind=kLoop, calls=%fused_computation.6 | loop fusion | flops 77266944 | bytes 115900424 | tf_op jit(solution)/shard_map/reduce_sum | solution.py:580
  775.1 4.0 stack.557
  803.0 27.2 %multiply_subtract_fusion = f32[6288,768]{1,0:T(8,128)} fusion(f32[6288,768]{1,0:T(8,128)} %param.33, f32[]{:T(128)} %bitcast.319, f32[6288,768]{1,0:T(8,128)} %get-tuple-element.96, f32[6288,768]{1,0:T(8,128)} %get-tuple-element.95), kind=kLoop, calls=%fused_computation.5 | loop fusion | flops 38633472 | bytes 77266944 | tf_op jit(solution)/shard_map/sub | solution.py:584
  (1115 shorter events, 379.1 us)
Async XLA Ops:
  4.8 52.1 %collective-permute-start.10 = (bf16[5,768]{1,0:T(8,128)(2,1)}, bf16[5,768]{1,0:T(8,128)(2,1)}, u32[]{:S(2)}, u32[]{:S(2)}) collective-permute-start(bf16[5,768]{1,0:T(8,128)(2,1)} %pad_maximum_fusion.70), channel_id=1, source_target_pairs={{0,2},{1,3},{2,0},{3,1},{4,6},{5,7},{6,4},{7,5},{8,10},{9,11},{10,... | collective-permute-start | bytes 23048 | tf_op jit(solution)/shard_map/ppermute | solution.py:252
  7.8 50.6 %collective-permute-start.9 = (bf16[5,768]{1,0:T(8,128)(2,1)}, bf16[5,768]{1,0:T(8,128)(2,1)}, u32[]{:S(2)}, u32[]{:S(2)}) collective-permute-start(bf16[5,768]{1,0:T(8,128)(2,1)} %pad_maximum_fusion.70), channel_id=1, source_target_pairs={{0,4},{1,5},{2,6},{3,7},{4,0},{5,1},{6,2},{7,3},{8,12},{9,13},{10,... | collective-permute-start | bytes 23048 | tf_op jit(solution)/shard_map/ppermute | solution.py:252
  11.7 17.4 %collective-permute-start = (s32[1,192]{1,0:T(1,128)S(1)}, s32[1,192]{1,0:T(1,128)S(1)}, u32[]{:S(2)}, u32[]{:S(2)}) collective-permute-start(s32[1,192]{1,0:T(1,128)S(1)} %constant_dynamic-update-slice_fusion), channel_id=1, source_target_pairs={{0,1},{1,0},{2,3},{3,2},{4,5},{5,4},{6,7},{7,6},{8,9},{9,8},{10,11... | collective-permute-start | bytes 2312 | tf_op jit(solution)/shard_map/ppermute | solution.py:247
  36.8 23.1 %collective-permute-start.8 = (bf16[5,768]{1,0:T(8,128)(2,1)}, bf16[5,768]{1,0:T(8,128)(2,1)}, u32[]{:S(2)}, u32[]{:S(2)}) collective-permute-start(bf16[5,768]{1,0:T(8,128)(2,1)} %pad_maximum_fusion.70), channel_id=1, source_target_pairs={{0,6},{1,7},{2,4},{3,5},{4,2},{5,3},{6,0},{7,1},{8,14},{9,15},{10,... | collective-permute-start | bytes 23048 | tf_op jit(solution)/shard_map/ppermute | solution.py:252
  36.9 32.4 %collective-permute-start.28 = (bf16[24,384]{1,0:T(8,128)(2,1)}, bf16[24,384]{1,0:T(8,128)(2,1)}, u32[]{:S(2)}, u32[]{:S(2)}) collective-permute-start(bf16[24,384]{1,0:T(8,128)(2,1)} %slice.256), channel_id=1, source_target_pairs={{0,2},{1,3},{2,0},{3,1},{4,6},{5,7},{6,4},{7,5},{8,10},{9,11},{10,... | collective-permute-start | bytes 55304 | tf_op jit(solution)/shard_map/ppermute | solution.py:252
  36.9 32.3 %collective-permute-start.27 = (bf16[24,384]{1,0:T(8,128)(2,1)}, bf16[24,384]{1,0:T(8,128)(2,1)}, u32[]{:S(2)}, u32[]{:S(2)}) collective-permute-start(bf16[24,384]{1,0:T(8,128)(2,1)} %slice.256), channel_id=1, source_target_pairs={{0,4},{1,5},{2,6},{3,7},{4,0},{5,1},{6,2},{7,3},{8,12},{9,13},{10,... | collective-permute-start | bytes 55304 | tf_op jit(solution)/shard_map/ppermute | solution.py:252
  62.2 20.9 %collective-permute-start.16 = (bf16[24,1152]{1,0:T(8,128)(2,1)}, bf16[24,1152]{1,0:T(8,128)(2,1)S(1)}, u32[]{:S(2)}, u32[]{:S(2)}) collective-permute-start(bf16[24,1152]{1,0:T(8,128)(2,1)} %slice.249), channel_id=1, source_target_pairs={{0,2},{1,3},{2,0},{3,1},{4,6},{5,7},{6,4},{7,5},{8,10},{9,11},{10,... | collective-permute-start | bytes 165896 | tf_op jit(solution)/shard_map/ppermute | solution.py:252
  64.7 20.0 %collective-permute-start.15 = (bf16[24,1152]{1,0:T(8,128)(2,1)}, bf16[24,1152]{1,0:T(8,128)(2,1)S(1)}, u32[]{:S(2)}, u32[]{:S(2)}) collective-permute-start(bf16[24,1152]{1,0:T(8,128)(2,1)} %slice.249), channel_id=1, source_target_pairs={{0,4},{1,5},{2,6},{3,7},{4,0},{5,1},{6,2},{7,3},{8,12},{9,13},{10,... | collective-permute-start | bytes 165896 | tf_op jit(solution)/shard_map/ppermute | solution.py:252
  89.9 85.5 %collective-permute-start.4 = (bf16[4,128,768]{2,1,0:T(8,128)(2,1)}, bf16[4,128,768]{2,1,0:T(8,128)(2,1)}, u32[]{:S(2)}, u32[]{:S(2)}) collective-permute-start(bf16[4,128,768]{2,1,0:T(8,128)(2,1)} %dynamic-slice_bitcast_fusion), channel_id=1, source_target_pairs={{0,1},{1,0},{2,3},{3,2},{4,5},{5,4},{6,7},{7,6},{8,9},{9,8},{10,11... | collective-permute-start | bytes 2359304 | tf_op jit(solution)/shard_map/ppermute | solution.py:247
  101.3 42.5 %collective-permute-start.17 = (bf16[1,1,4,24,1152]{4,3,2,1,0:T(8,128)(2,1)}, bf16[1,1,4,24,1152]{4,3,2,1,0:T(8,128)(2,1)}, u32[]{:S(2)}, u32[]{:S(2)}) collective-permute-start(bf16[1,1,4,24,1152]{4,3,2,1,0:T(8,128)(2,1)} %maximum_bitcast_fusion.6), channel_id=1, source_target_pairs={{0,16},{8,24},{16,0},{24,8},{1,17},{9,25},{17,1},{25,9},{2,18},{10... | collective-permute-start | bytes 663560 | tf_op jit(solution)/shard_map/ppermute | solution.py:257
  114.9 36.6 %collective-permute-start.41 = (bf16[1,1,4,24,1536]{4,3,2,1,0:T(8,128)(2,1)}, bf16[1,1,4,24,1536]{4,3,2,1,0:T(8,128)(2,1)}, u32[]{:S(2)}, u32[]{:S(2)}) collective-permute-start(bf16[1,1,4,24,1536]{4,3,2,1,0:T(8,128)(2,1)} %maximum_bitcast_fusion.2), channel_id=1, source_target_pairs={{0,16},{8,24},{16,0},{24,8},{1,17},{9,25},{17,1},{25,9},{2,18},{10... | collective-permute-start | bytes 884744 | tf_op jit(solution)/shard_map/ppermute | solution.py:257
  118.5 34.1 %collective-permute-start.53 = (bf16[1,1,4,96,384]{4,3,2,1,0:T(8,128)(2,1)}, bf16[1,1,4,96,384]{4,3,2,1,0:T(8,128)(2,1)}, u32[]{:S(2)}, u32[]{:S(2)}) collective-permute-start(bf16[1,1,4,96,384]{4,3,2,1,0:T(8,128)(2,1)} %maximum_bitcast_fusion.4), channel_id=1, source_target_pairs={{0,16},{8,24},{16,0},{24,8},{1,17},{9,25},{17,1},{25,9},{2,18},{10... | collective-permute-start | bytes 884744 | tf_op jit(solution)/shard_map/ppermute | solution.py:257
  121.2 14.8 %collective-permute-start.30 = (bf16[2,1,4,24,384]{4,3,2,1,0:T(8,128)(2,1)}, bf16[2,1,4,24,384]{4,3,2,1,0:T(8,128)(2,1)}, u32[]{:S(2)}, u32[]{:S(2)}) collective-permute-start(bf16[2,1,4,24,384]{4,3,2,1,0:T(8,128)(2,1)} %pad_maximum_fusion.60), channel_id=1, source_target_pairs={{0,8},{8,0},{16,24},{24,16},{1,9},{9,1},{17,25},{25,17},{2,10},{10... | collective-permute-start | bytes 442376 | tf_op jit(solution)/shard_map/ppermute | solution.py:257
  157.1 15.8 %collective-permute-start.18 = (bf16[2,1,4,24,1152]{4,3,2,1,0:T(8,128)(2,1)S(1)}, bf16[2,1,4,24,1152]{4,3,2,1,0:T(8,128)(2,1)S(1)}, u32[]{:S(2)}, u32[]{:S(2)}) collective-permute-start(bf16[2,1,4,24,1152]{4,3,2,1,0:T(8,128)(2,1)S(1)} %pad_maximum_fusion.47), channel_id=1, source_target_pairs={{0,8},{8,0},{16,24},{24,16},{1,9},{9,1},{17,25},{25,17},{2,10},{10... | collective-permute-start | bytes 1327112 | tf_op jit(solution)/shard_map/ppermute | solution.py:257
  164.8 20.8 %collective-permute-start.42 = (bf16[2,1,4,24,1536]{4,3,2,1,0:T(8,128)(2,1)S(1)}, bf16[2,1,4,24,1536]{4,3,2,1,0:T(8,128)(2,1)S(1)}, u32[]{:S(2)}, u32[]{:S(2)}) collective-permute-start(bf16[2,1,4,24,1536]{4,3,2,1,0:T(8,128)(2,1)S(1)} %pad_maximum_fusion.42), channel_id=1, source_target_pairs={{0,8},{8,0},{16,24},{24,16},{1,9},{9,1},{17,25},{25,17},{2,10},{10... | collective-permute-start | bytes 1769480 | tf_op jit(solution)/shard_map/ppermute | solution.py:257
  166.4 30.2 %collective-permute-start.54 = (bf16[2,1,4,96,384]{4,3,2,1,0:T(8,128)(2,1)S(1)}, bf16[2,1,4,96,384]{4,3,2,1,0:T(8,128)(2,1)S(1)}, u32[]{:S(2)}, u32[]{:S(2)}) collective-permute-start(bf16[2,1,4,96,384]{4,3,2,1,0:T(8,128)(2,1)S(1)} %pad_maximum_fusion.44), channel_id=1, source_target_pairs={{0,8},{8,0},{16,24},{24,16},{1,9},{9,1},{17,25},{25,17},{2,10},{10... | collective-permute-start | bytes 1769480 | tf_op jit(solution)/shard_map/ppermute | solution.py:257
  172.9 36.6 %collective-permute-start.48 = (bf16[1,2,4,24,1536]{4,3,2,1,0:T(8,128)(2,1)S(1)}, bf16[1,2,4,24,1536]{4,3,2,1,0:T(8,128)(2,1)S(1)}, u32[]{:S(2)}, u32[]{:S(2)}) collective-permute-start(bf16[1,2,4,24,1536]{4,3,2,1,0:T(8,128)(2,1)S(1)} %pad_maximum_fusion.43), channel_id=1, source_target_pairs={{0,16},{8,24},{16,0},{24,8},{1,17},{9,25},{17,1},{25,9},{2,18},{10... | collective-permute-start | bytes 1769480 | tf_op jit(solution)/shard_map/ppermute | solution.py:257
  174.2 33.3 %collective-permute-start.60 = (bf16[1,2,4,96,384]{4,3,2,1,0:T(8,128)(2,1)S(1)}, bf16[1,2,4,96,384]{4,3,2,1,0:T(8,128)(2,1)S(1)}, u32[]{:S(2)}, u32[]{:S(2)}) collective-permute-start(bf16[1,2,4,96,384]{4,3,2,1,0:T(8,128)(2,1)S(1)} %pad_maximum_fusion.45), channel_id=1, source_target_pairs={{0,16},{8,24},{16,0},{24,8},{1,17},{9,25},{17,1},{25,9},{2,18},{10... | collective-permute-start | bytes 1769480 | tf_op jit(solution)/shard_map/ppermute | solution.py:257
  176.7 22.6 %collective-permute-start.5 = (bf16[128,768]{1,0:T(8,128)(2,1)S(1)}, bf16[128,768]{1,0:T(8,128)(2,1)S(1)}, u32[]{:S(2)}, u32[]{:S(2)}) collective-permute-start(bf16[128,768]{1,0:T(8,128)(2,1)S(1)} %get-tuple-element.185), channel_id=1, source_target_pairs={{0,2},{1,3},{2,0},{3,1},{4,6},{5,7},{6,4},{7,5},{8,10},{9,11},{10,... | collective-permute-start | bytes 589832 | tf_op jit(solution)/shard_map/ppermute | solution.py:252
  185.5 13.8 %collective-permute-start.7 = (bf16[128,768]{1,0:T(8,128)(2,1)S(1)}, bf16[128,768]{1,0:T(8,128)(2,1)S(1)}, u32[]{:S(2)}, u32[]{:S(2)}) collective-permute-start(bf16[128,768]{1,0:T(8,128)(2,1)S(1)} %get-tuple-element.186), channel_id=1, source_target_pairs={{0,6},{1,7},{2,4},{3,5},{4,2},{5,3},{6,0},{7,1},{8,14},{9,15},{10,... | collective-permute-start | bytes 589832 | tf_op jit(solution)/shard_map/ppermute | solution.py:252
  206.9 23.6 %collective-permute-start.55 = (bf16[16,96,384]{2,1,0:T(8,128)(2,1)S(1)}, bf16[16,96,384]{2,1,0:T(8,128)(2,1)}, u32[]{:S(2)}, u32[]{:S(2)}) collective-permute-start(bf16[16,96,384]{2,1,0:T(8,128)(2,1)S(1)} %bitcast.745), channel_id=1, source_target_pairs={{0,1},{1,0},{2,3},{3,2},{4,5},{5,4},{6,7},{7,6},{8,9},{9,8},{10,11... | collective-permute-start | bytes 3538952 | tf_op jit(solution)/shard_map/ppermute | solution.py:247
  207.5 21.1 %collective-permute-start.43 = (bf16[16,24,1536]{2,1,0:T(8,128)(2,1)}, bf16[16,24,1536]{2,1,0:T(8,128)(2,1)}, u32[]{:S(2)}, u32[]{:S(2)}) collective-permute-start(bf16[16,24,1536]{2,1,0:T(8,128)(2,1)} %bitcast.72), channel_id=1, source_target_pairs={{0,1},{1,0},{2,3},{3,2},{4,5},{5,4},{6,7},{7,6},{8,9},{9,8},{10,11... | collective-permute-start | bytes 3538952 | tf_op jit(solution)/shard_map/ppermute | solution.py:247
  209.5 23.0 %collective-permute-start.61 = (bf16[16,96,384]{2,1,0:T(8,128)(2,1)}, bf16[16,96,384]{2,1,0:T(8,128)(2,1)}, u32[]{:S(2)}, u32[]{:S(2)}) collective-permute-start(bf16[16,96,384]{2,1,0:T(8,128)(2,1)} %bitcast.101), channel_id=1, source_target_pairs={{0,1},{1,0},{2,3},{3,2},{4,5},{5,4},{6,7},{7,6},{8,9},{9,8},{10,11... | collective-permute-start | bytes 3538952 | tf_op jit(solution)/shard_map/ppermute | solution.py:247
  210.8 25.7 %collective-permute-start.49 = (bf16[16,24,1536]{2,1,0:T(8,128)(2,1)}, bf16[16,24,1536]{2,1,0:T(8,128)(2,1)}, u32[]{:S(2)}, u32[]{:S(2)}) collective-permute-start(bf16[16,24,1536]{2,1,0:T(8,128)(2,1)} %bitcast.82), channel_id=1, source_target_pairs={{0,1},{1,0},{2,3},{3,2},{4,5},{5,4},{6,7},{7,6},{8,9},{9,8},{10,11... | collective-permute-start | bytes 3538952 | tf_op jit(solution)/shard_map/ppermute | solution.py:247
  289.0 36.3 %collective-permute-start.138 = (bf16[1,512,384]{2,1,0:T(8,128)(2,1)S(1)}, bf16[1,512,384]{2,1,0:T(8,128)(2,1)S(1)}, u32[]{:S(2)}, u32[]{:S(2)}) collective-permute-start(bf16[1,512,384]{2,1,0:T(8,128)(2,1)S(1)} %dynamic-slice_bitcast_fusion.1), channel_id=1, source_target_pairs={{0,8},{8,0},{16,24},{24,16},{1,9},{9,1},{17,25},{25,17},{2,10},{10... | collective-permute-start | bytes 1179656 | tf_op jit(solution)/shard_map/ppermute | solution.py:257
  293.2 31.4 %collective-permute-start.142 = (f32[512]{0:T(512)S(1)}, f32[512]{0:T(512)S(1)}, u32[]{:S(2)}, u32[]{:S(2)}) collective-permute-start(f32[512]{0:T(512)S(1)} %get-tuple-element.133), channel_id=1, source_target_pairs={{0,16},{8,24},{16,0},{24,8},{1,17},{9,25},{17,1},{25,9},{2,18},{10... | collective-permute-start | bytes 6152 | tf_op jit(solution)/shard_map/ppermute | solution.py:257
  294.3 30.4 %collective-permute-start.141 = (f32[512]{0:T(512)S(1)}, f32[512]{0:T(512)S(1)}, u32[]{:S(2)}, u32[]{:S(2)}) collective-permute-start(f32[512]{0:T(512)S(1)} %get-tuple-element.133), channel_id=1, source_target_pairs={{0,24},{8,16},{16,8},{24,0},{1,25},{9,17},{17,9},{25,1},{2,26},{10... | collective-permute-start | bytes 6152 | tf_op jit(solution)/shard_map/ppermute | solution.py:257
  295.3 29.3 %collective-permute-start.143 = (f32[512]{0:T(512)S(1)}, f32[512]{0:T(512)S(1)}, u32[]{:S(2)}, u32[]{:S(2)}) collective-permute-start(f32[512]{0:T(512)S(1)} %get-tuple-element.133), channel_id=1, source_target_pairs={{0,8},{8,0},{16,24},{24,16},{1,9},{9,1},{17,25},{25,17},{2,10},{10... | collective-permute-start | bytes 6152 | tf_op jit(solution)/shard_map/ppermute | solution.py:257
  330.3 112.4 %collective-permute-start.139 = (bf16[2,512,384]{2,1,0:T(8,128)(2,1)}, bf16[2,512,384]{2,1,0:T(8,128)(2,1)}, u32[]{:S(2)}, u32[]{:S(2)}) collective-permute-start(bf16[2,512,384]{2,1,0:T(8,128)(2,1)} %pad_maximum_fusion.35), channel_id=1, source_target_pairs={{0,16},{8,24},{16,0},{24,8},{1,17},{9,25},{17,1},{25,9},{2,18},{10... | collective-permute-start | bytes 2359304 | tf_op jit(solution)/shard_map/ppermute | solution.py:257
  380.4 33.5 %collective-permute-start.89 = (bf16[16,24,384]{2,1,0:T(8,128)(2,1)S(1)}, bf16[16,24,384]{2,1,0:T(8,128)(2,1)S(1)}, u32[]{:S(2)}, u32[]{:S(2)}) collective-permute-start(bf16[16,24,384]{2,1,0:T(8,128)(2,1)S(1)} %bitcast.820), channel_id=1, source_target_pairs={{0,1},{1,0},{2,3},{3,2},{4,5},{5,4},{6,7},{7,6},{8,9},{9,8},{10,11... | collective-permute-start | bytes 884744 | tf_op jit(solution)/shard_map/ppermute | solution.py:247
  380.6 17.6 %collective-permute-start.137 = (f32[14,768]{1,0:T(8,128)S(1)}, f32[14,768]{1,0:T(8,128)S(1)}, u32[]{:S(2)}, u32[]{:S(2)}) collective-permute-start(f32[14,768]{1,0:T(8,128)S(1)} %add_add_fusion.5), channel_id=1, source_target_pairs={{0,6},{1,7},{2,4},{3,5},{4,2},{5,3},{6,0},{7,1},{8,14},{9,15},{10,... | collective-permute-start | bytes 129032 | tf_op jit(solution)/shard_map/ppermute | solution.py:252
  409.9 16.7 %collective-permute-start.150 = (bf16[1,1,4,128,384]{4,3,2,1,0:T(8,128)(2,1)S(1)}, bf16[1,1,4,128,384]{4,3,2,1,0:T(8,128)(2,1)S(1)}, u32[]{:S(2)}, u32[]{:S(2)}) collective-permute-start(bf16[1,1,4,128,384]{4,3,2,1,0:T(8,128)(2,1)S(1)} %maximum_bitcast_fusion), channel_id=1, source_target_pairs={{0,16},{8,24},{16,0},{24,8},{1,17},{9,25},{17,1},{25,9},{2,18},{10... | collective-permute-start | bytes 1179656 | tf_op jit(solution)/shard_map/ppermute | solution.py:257
  413.2 28.6 %collective-permute-start.156 = (bf16[1,1,4,128,384]{4,3,2,1,0:T(8,128)(2,1)S(1)}, bf16[1,1,4,128,384]{4,3,2,1,0:T(8,128)(2,1)S(1)}, u32[]{:S(2)}, u32[]{:S(2)}) collective-permute-start(bf16[1,1,4,128,384]{4,3,2,1,0:T(8,128)(2,1)S(1)} %maximum_bitcast_fusion.1), channel_id=1, source_target_pairs={{0,8},{8,0},{16,24},{24,16},{1,9},{9,1},{17,25},{25,17},{2,10},{10... | collective-permute-start | bytes 1179656 | tf_op jit(solution)/shard_map/ppermute | solution.py:257
  447.2 20.5 %collective-permute-start.151 = (bf16[2,1,4,128,384]{4,3,2,1,0:T(8,128)(2,1)S(1)}, bf16[2,1,4,128,384]{4,3,2,1,0:T(8,128)(2,1)S(1)}, u32[]{:S(2)}, u32[]{:S(2)}) collective-permute-start(bf16[2,1,4,128,384]{4,3,2,1,0:T(8,128)(2,1)S(1)} %pad_maximum_fusion.36), channel_id=1, source_target_pairs={{0,8},{8,0},{16,24},{24,16},{1,9},{9,1},{17,25},{25,17},{2,10},{10... | collective-permute-start | bytes 2359304 | tf_op jit(solution)/shard_map/ppermute | solution.py:257
  448.5 31.6 %collective-permute-start.157 = (bf16[1,2,4,128,384]{4,3,2,1,0:T(8,128)(2,1)S(1)}, bf16[1,2,4,128,384]{4,3,2,1,0:T(8,128)(2,1)S(1)}, u32[]{:S(2)}, u32[]{:S(2)}) collective-permute-start(bf16[1,2,4,128,384]{4,3,2,1,0:T(8,128)(2,1)S(1)} %pad_maximum_fusion.37), channel_id=1, source_target_pairs={{0,16},{8,24},{16,0},{24,8},{1,17},{9,25},{17,1},{25,9},{2,18},{10... | collective-permute-start | bytes 2359304 | tf_op jit(solution)/shard_map/ppermute | solution.py:257
  451.0 129.7 %collective-permute-start.140 = (bf16[4,512,384]{2,1,0:T(8,128)(2,1)}, bf16[4,512,384]{2,1,0:T(8,128)(2,1)}, u32[]{:S(2)}, u32[]{:S(2)}) collective-permute-start(bf16[4,512,384]{2,1,0:T(8,128)(2,1)} %pad_maximum_fusion.18), channel_id=1, source_target_pairs={{0,1},{1,0},{2,3},{3,2},{4,5},{5,4},{6,7},{7,6},{8,9},{9,8},{10,11... | collective-permute-start | bytes 4718600 | tf_op jit(solution)/shard_map/ppermute | solution.py:247
  451.4 24.8 %collective-permute-start.84 = (bf16[2,4,24,1152]{3,2,1,0:T(8,128)(2,1)S(1)}, bf16[2,4,24,1152]{3,2,1,0:T(8,128)(2,1)S(1)}, u32[]{:S(2)}, u32[]{:S(2)}) collective-permute-start(bf16[2,4,24,1152]{3,2,1,0:T(8,128)(2,1)S(1)} %fusion.38), channel_id=1, source_target_pairs={{0,8},{8,0},{16,24},{24,16},{1,9},{9,1},{17,25},{25,17},{2,10},{10... | collective-permute-start | bytes 1327112 | tf_op jit(solution)/shard_map/ppermute | solution.py:257
  455.4 23.0 %collective-permute-start.78 = (bf16[2,4,24,1152]{3,2,1,0:T(8,128)(2,1)S(1)}, bf16[2,4,24,1152]{3,2,1,0:T(8,128)(2,1)S(1)}, u32[]{:S(2)}, u32[]{:S(2)}) collective-permute-start(bf16[2,4,24,1152]{3,2,1,0:T(8,128)(2,1)S(1)} %fusion.37), channel_id=1, source_target_pairs={{0,16},{8,24},{16,0},{24,8},{1,17},{9,25},{17,1},{25,9},{2,18},{10... | collective-permute-start | bytes 1327112 | tf_op jit(solution)/shard_map/ppermute | solution.py:257
  467.7 44.9 %collective-permute-start.114 = (bf16[2,4,96,384]{3,2,1,0:T(8,128)(2,1)}, bf16[2,4,96,384]{3,2,1,0:T(8,128)(2,1)}, u32[]{:S(2)}, u32[]{:S(2)}) collective-permute-start(bf16[2,4,96,384]{3,2,1,0:T(8,128)(2,1)} %fusion.34), channel_id=1, source_target_pairs={{0,16},{8,24},{16,0},{24,8},{1,17},{9,25},{17,1},{25,9},{2,18},{10... | collective-permute-start | bytes 1769480 | tf_op jit(solution)/shard_map/ppermute | solution.py:257
  476.4 18.2 %collective-permute-start.85 = (bf16[4,24,1152]{2,1,0:T(8,128)(2,1)S(1)}, bf16[4,24,1152]{2,1,0:T(8,128)(2,1)S(1)}, u32[]{:S(2)}, u32[]{:S(2)}) collective-permute-start(bf16[4,24,1152]{2,1,0:T(8,128)(2,1)S(1)} %fusion.80), channel_id=1, source_target_pairs={{0,16},{8,24},{16,0},{24,8},{1,17},{9,25},{17,1},{25,9},{2,18},{10... | collective-permute-start | bytes 663560 | tf_op jit(solution)/shard_map/ppermute | solution.py:257
  478.6 18.3 %collective-permute-start.79 = (bf16[4,24,1152]{2,1,0:T(8,128)(2,1)S(1)}, bf16[4,24,1152]{2,1,0:T(8,128)(2,1)S(1)}, u32[]{:S(2)}, u32[]{:S(2)}) collective-permute-start(bf16[4,24,1152]{2,1,0:T(8,128)(2,1)S(1)} %fusion.79), channel_id=1, source_target_pairs={{0,8},{8,0},{16,24},{24,16},{1,9},{9,1},{17,25},{25,17},{2,10},{10... | collective-permute-start | bytes 663560 | tf_op jit(solution)/shard_map/ppermute | solution.py:257
  504.6 16.6 %collective-permute-start.120 = (bf16[2,4,96,384]{3,2,1,0:T(8,128)(2,1)}, bf16[2,4,96,384]{3,2,1,0:T(8,128)(2,1)}, u32[]{:S(2)}, u32[]{:S(2)}) collective-permute-start(bf16[2,4,96,384]{3,2,1,0:T(8,128)(2,1)} %fusion.36), channel_id=1, source_target_pairs={{0,8},{8,0},{16,24},{24,16},{1,9},{9,1},{17,25},{25,17},{2,10},{10... | collective-permute-start | bytes 1769480 | tf_op jit(solution)/shard_map/ppermute | solution.py:257
  507.4 16.2 %collective-permute-start.102 = (bf16[2,4,24,1536]{3,2,1,0:T(8,128)(2,1)}, bf16[2,4,24,1536]{3,2,1,0:T(8,128)(2,1)}, u32[]{:S(2)}, u32[]{:S(2)}) collective-permute-start(bf16[2,4,24,1536]{3,2,1,0:T(8,128)(2,1)} %fusion.33), channel_id=1, source_target_pairs={{0,16},{8,24},{16,0},{24,8},{1,17},{9,25},{17,1},{25,9},{2,18},{10... | collective-permute-start | bytes 1769480 | tf_op jit(solution)/shard_map/ppermute | solution.py:257
  508.6 25.3 %collective-permute-start.108 = (bf16[2,4,24,1536]{3,2,1,0:T(8,128)(2,1)}, bf16[2,4,24,1536]{3,2,1,0:T(8,128)(2,1)}, u32[]{:S(2)}, u32[]{:S(2)}) collective-permute-start(bf16[2,4,24,1536]{3,2,1,0:T(8,128)(2,1)} %fusion.35), channel_id=1, source_target_pairs={{0,8},{8,0},{16,24},{24,16},{1,9},{9,1},{17,25},{25,17},{2,10},{10... | collective-permute-start | bytes 1769480 | tf_op jit(solution)/shard_map/ppermute | solution.py:257
  512.6 133.2 %collective-permute-start.152 = (bf16[16,128,384]{2,1,0:T(8,128)(2,1)}, bf16[16,128,384]{2,1,0:T(8,128)(2,1)}, u32[]{:S(2)}, u32[]{:S(2)}) collective-permute-start(bf16[16,128,384]{2,1,0:T(8,128)(2,1)} %bitcast.736), channel_id=1, source_target_pairs={{0,1},{1,0},{2,3},{3,2},{4,5},{5,4},{6,7},{7,6},{8,9},{9,8},{10,11... | collective-permute-start | bytes 4718600 | tf_op jit(solution)/shard_map/ppermute | solution.py:247
  521.2 21.7 %collective-permute-start.115 = (bf16[4,96,384]{2,1,0:T(8,128)(2,1)S(1)}, bf16[4,96,384]{2,1,0:T(8,128)(2,1)S(1)}, u32[]{:S(2)}, u32[]{:S(2)}) collective-permute-start(bf16[4,96,384]{2,1,0:T(8,128)(2,1)S(1)} %fusion.68), channel_id=1, source_target_pairs={{0,8},{8,0},{16,24},{24,16},{1,9},{9,1},{17,25},{25,17},{2,10},{10... | collective-permute-start | bytes 884744 | tf_op jit(solution)/shard_map/ppermute | solution.py:257
  523.6 26.8 %collective-permute-start.121 = (bf16[4,96,384]{2,1,0:T(8,128)(2,1)S(1)}, bf16[4,96,384]{2,1,0:T(8,128)(2,1)S(1)}, u32[]{:S(2)}, u32[]{:S(2)}) collective-permute-start(bf16[4,96,384]{2,1,0:T(8,128)(2,1)S(1)} %fusion.69), channel_id=1, source_target_pairs={{0,16},{8,24},{16,0},{24,8},{1,17},{9,25},{17,1},{25,9},{2,18},{10... | collective-permute-start | bytes 884744 | tf_op jit(solution)/shard_map/ppermute | solution.py:257
  574.2 74.0 %collective-permute-start.158 = (bf16[16,128,384]{2,1,0:T(8,128)(2,1)}, bf16[16,128,384]{2,1,0:T(8,128)(2,1)}, u32[]{:S(2)}, u32[]{:S(2)}) collective-permute-start(bf16[16,128,384]{2,1,0:T(8,128)(2,1)} %bitcast.293), channel_id=1, source_target_pairs={{0,1},{1,0},{2,3},{3,2},{4,5},{5,4},{6,7},{7,6},{8,9},{9,8},{10,11... | collective-permute-start | bytes 4718600 | tf_op jit(solution)/shard_map/ppermute | solution.py:247
  (346 other events, 3700.5 us)

commit v2 on v1

v2 whole, which is shorter than its diff:
```python
import functools
import math

import jax
import jax.numpy as jnp
from jax import lax
from jax.experimental import pallas as pl
from jax.experimental.pallas import tpu as pltpu
from jax.sharding import PartitionSpec as P

HD = 64
V_REAL = 50257
STEP = 5


LN_EPS = 1e-05
SMOOTHING = 0.1
BETA_ONE = 0.9
BETA_TWO = 0.999
ADAM_EPS = 1e-12
DECAY = 0.01
RATE = 0.3
CLIP_AT = 0.01
MASKED = -1e30
CHUNK = 1280
PIECE = 640
VMEM_BYTES = 58 * 2**20


def layer_norm(inputs, gain, shift):
    centre = jnp.mean(inputs, axis=-1, keepdims=True)
    centred = inputs - centre
    spread = jnp.mean(centred * centred, axis=-1, keepdims=True)
    return centred * lax.rsqrt(spread + LN_EPS) * gain + shift


def gelu_tanh(inputs):
    return (
        0.5
        * inputs
        * (1.0 + jnp.tanh(0.7978845608028654 * (inputs + 0.044715 * inputs * inputs * inputs)))
    )


def dot_plain(left_op, right_op):
    return jnp.dot(left_op, right_op, preferred_element_type=jnp.float32)


def dot_first(left_op, right_op):
    return lax.dot_general(
        left_op, right_op, (((0,), (0,)), ((), ())), preferred_element_type=jnp.float32
    )


def dot_second(left_op, right_op):
    return lax.dot_general(
        left_op, right_op, (((1,), (1,)), ((), ())), preferred_element_type=jnp.float32
    )


def params():
    return pltpu.CompilerParams(vmem_limit_bytes=VMEM_BYTES)


def cost(flops, bytes_accessed):
    return pl.CostEstimate(
        flops=int(flops), bytes_accessed=int(bytes_accessed), transcendentals=0
    )


def whole_block():
    return pl.BlockSpec(memory_space=pltpu.VMEM)


def shape_of(shape, dtype):
    return jax.ShapeDtypeStruct(tuple(shape), dtype)


def causal_scores(queries, keys, causal):
    return jnp.where(causal, dot_second(queries, keys) * HD ** (-0.5), MASKED)


def causal_mask(count):
    query = lax.broadcasted_iota(jnp.int32, (count, count), 0)
    key = lax.broadcasted_iota(jnp.int32, (count, count), 1)
    return key <= query


def head_span(head):
    return slice(head * HD, (head + 1) * HD)


def attention_forward(embedded, positions, vec_rows, w_qkv, w_proj):
    count, width = embedded.shape
    low = jnp.bfloat16

    def body(e_ref, p_ref, v_ref, qkv_ref, proj_ref, x0_ref, h1_ref, packed_ref, o_ref, x1_ref, h2_ref):
        x0 = e_ref[...] + p_ref[...].astype(jnp.float32)
        x0_ref[...] = x0
        h1 = layer_norm(x0, v_ref[0:1, :], v_ref[1:2, :]).astype(low)
        h1_ref[...] = h1
        parts = []
        for place, bias in enumerate((6, None, 7)):
            span = slice(place * width, (place + 1) * width)
            part = dot_plain(h1, qkv_ref[:, span])
            if bias is not None:
                part = part + v_ref[bias : bias + 1, :]
            parts.append(part.astype(low))
            packed_ref[:, span] = parts[-1]
        queries, keys, values = parts
        causal = causal_mask(count)
        for head in range(0, width // HD, 2):
            mixed = []
            for one in (head, head + 1):
                span = head_span(one)
                scores = causal_scores(queries[:, span], keys[:, span], causal)
                grown = jnp.exp(scores - jnp.max(scores, axis=-1, keepdims=True))
                probs = (grown / jnp.sum(grown, axis=-1, keepdims=True)).astype(low)
                mixed.append(dot_plain(probs, values[:, span]))
            o_ref[:, head * HD : (head + 2) * HD] = jnp.concatenate(mixed, axis=1).astype(low)
        x1 = x0 + dot_plain(o_ref[...], proj_ref[...]) + v_ref[8:9, :]
        x1_ref[...] = x1
        h2_ref[...] = layer_norm(x1, v_ref[2:3, :], v_ref[3:4, :]).astype(low)

    shape = (count, width)
    return pl.pallas_call(
        body,
        out_shape=[
            shape_of(shape, jnp.float32),
            shape_of(shape, low),
            shape_of((count, 3 * width), low),
            shape_of(shape, low),
            shape_of(shape, jnp.float32),
            shape_of(shape, low),
        ],
        in_specs=[whole_block()] * 5,
        out_specs=[whole_block()] * 6,
        compiler_params=params(),
        cost_estimate=cost(16 * count * width * width, 8 * width * width),
    )(embedded, positions, vec_rows, w_qkv, w_proj)


def hidden_forward(normed, vec_rows, w_up):
    count, width = normed.shape
    hidden = w_up.shape[1]

    def body(h_ref, v_ref, w_ref, pre_ref, act_ref):
        for place in range(hidden // width):
            span = slice(place * width, (place + 1) * width)
            pre = dot_plain(h_ref[...], w_ref[:, span]) + v_ref[10 + place : 11 + place, :]
            pre_ref[:, span] = pre
            act_ref[:, span] = gelu_tanh(pre).astype(jnp.bfloat16)

    return pl.pallas_call(
        body,
        out_shape=[
            shape_of((count, hidden), jnp.float32),
            shape_of((count, hidden), jnp.bfloat16),
        ],
        in_specs=[whole_block()] * 3,
        out_specs=[whole_block()] * 2,
        compiler_params=params(),
        cost_estimate=cost(2 * count * width * hidden, 2 * width * hidden),
    )(normed, vec_rows, w_up)


def output_forward(act, w_down, resid_mid, vec_rows, picks):
    count, width = resid_mid.shape
    number = picks.shape[0]

    def body(act_ref, w_ref, x1_ref, v_ref, pick_ref, x2_ref, out_ref):
        x2 = x1_ref[...] + dot_plain(act_ref[...], w_ref[...]) + v_ref[9:10, :]
        x2_ref[...] = x2
        final = layer_norm(x2, v_ref[4:5, :], v_ref[5:6, :]).astype(jnp.bfloat16)
        hot = pick_ref[...] == lax.broadcasted_iota(jnp.int32, (number, count), 1)
        hot = jnp.where(hot, 1.0, 0.0).astype(jnp.bfloat16)
        out_ref[...] = dot_plain(hot, final).astype(jnp.bfloat16)

    return pl.pallas_call(
        body,
        out_shape=[
            shape_of((count, width), jnp.float32),
            shape_of((number, width), jnp.bfloat16),
        ],
        in_specs=[whole_block()] * 5,
        out_specs=[whole_block()] * 2,
        compiler_params=params(),
        cost_estimate=cost(2 * act.size * width, 2 * w_down.size),
    )(act, w_down, resid_mid, vec_rows, picks)


def norm_backward(grad, inputs, gain):
    centred = inputs - jnp.mean(inputs, axis=-1, keepdims=True)
    scale = lax.rsqrt(jnp.mean(centred * centred, axis=-1, keepdims=True) + LN_EPS)
    normed = centred * scale
    scaled = grad * gain
    back = scale * (
        scaled
        - jnp.mean(scaled, axis=-1, keepdims=True)
        - normed * jnp.mean(scaled * normed, axis=-1, keepdims=True)
    )
    return (
        back,
        jnp.sum(grad * normed, axis=0, keepdims=True),
        jnp.sum(grad, axis=0, keepdims=True),
    )


def column_sum(value):
    return jnp.sum(value.astype(jnp.float32), axis=0, keepdims=True)


def select_columns(value, chooser):
    unit = chooser.shape[0]
    parts = [
        dot_plain(value[:, start : start + unit], chooser).astype(jnp.bfloat16)
        for start in range(0, value.shape[1], unit)
    ]
    return parts[0] if len(parts) == 1 else jnp.concatenate(parts, axis=1)


def choosers(width, rows, core):
    column = jnp.arange(width, dtype=jnp.int32)
    target = jnp.arange(width // 2, dtype=jnp.int32)
    made = []
    for side in (core, 1 - core):
        source = (target // rows * 2 + side) * rows + target % rows
        made.append((column[:, None] == source[None, :]).astype(jnp.bfloat16))
    return jnp.stack(made)


def output_backward(picked_grad, picks, resid_out, vec_rows, act, chooser):
    count, width = resid_out.shape
    number = picks.shape[0]
    half = act.shape[1] // 2
    low = jnp.bfloat16

    def body(g_ref, pick_ref, x_ref, v_ref, act_ref, c_ref, dx_ref, dy_ref, keep_ref, sent_ref, vec_ref):
        hot = pick_ref[...] == lax.broadcasted_iota(jnp.int32, (number, count), 1)
        final_grad = lax.dot_general(
            jnp.where(hot, 1.0, 0.0),
            g_ref[...],
            (((0,), (0,)), ((), ())),
            precision=lax.Precision.HIGHEST,
            preferred_element_type=jnp.float32,
        )
        back, gain, shift = norm_backward(final_grad, x_ref[...], v_ref[4:5, :])
        dx_ref[...] = back
        dy = back.astype(low)
        dy_ref[...] = dy
        vec_ref[0:1, :] = gain
        vec_ref[1:2, :] = shift
        vec_ref[2:3, :] = column_sum(dy)
        vec_ref[3:8, :] = jnp.zeros((5, width), jnp.float32)
        sent_ref[...] = dot_first(select_columns(act_ref[...], c_ref[1]), dy).astype(low)
        keep_ref[...] = dot_first(select_columns(act_ref[...], c_ref[0]), dy)

    return pl.pallas_call(
        body,
        out_shape=[
            shape_of((count, width), jnp.float32),
            shape_of((count, width), low),
            shape_of((half, width), jnp.float32),
            shape_of((half, width), low),
            shape_of((8, width), jnp.float32),
        ],
        in_specs=[whole_block()] * 6,
        out_specs=[whole_block()] * 5,
        compiler_params=params(),
        cost_estimate=cost(4 * act.size * width, 6 * half * width),
    )(picked_grad, picks, resid_out, vec_rows, act, chooser)


def hidden_backward(dy, w_down, pre, normed, chooser):
    count, width = dy.shape
    hidden = pre.shape[1]
    half = width // 2
    low = jnp.bfloat16

    def body(dy_ref, w_ref, pre_ref, h_ref, c_ref, dpre_ref, keep_ref, sent_ref, vec_ref):
        keep_cols = select_columns(h_ref[...], c_ref[0])
        sent_cols = select_columns(h_ref[...], c_ref[1])
        vec_ref[...] = jnp.zeros_like(vec_ref)
        for place in range(hidden // width):
            span = slice(place * width, (place + 1) * width)
            grad = dot_second(dy_ref[...], w_ref[span, :])
            u = pre_ref[:, span]
            bent = jnp.tanh(0.7978845608028654 * (u + 0.044715 * u * u * u))
            slope = 0.5 * (1.0 + bent) + 0.5 * u * (1.0 - bent * bent) * (
                0.7978845608028654 * (1.0 + 3.0 * 0.044715 * u * u)
            )
            dpre = (grad * slope).astype(low)
            dpre_ref[:, span] = dpre
            vec_ref[place : place + 1, :] = column_sum(dpre)
            sent_ref[:, span] = dot_first(sent_cols, dpre).astype(low)
            keep_ref[:, span] = dot_first(keep_cols, dpre)

    return pl.pallas_call(
        body,
        out_shape=[
            shape_of((count, hidden), low),
            shape_of((half, hidden), jnp.float32),
            shape_of((half, hidden), low),
            shape_of((8, width), jnp.float32),
        ],
        in_specs=[whole_block()] * 5,
        out_specs=[whole_block()] * 4,
        compiler_params=params(),
        cost_estimate=cost(6 * count * width * hidden, 8 * width * hidden),
    )(dy, w_down, pre, normed, chooser)


def middle_backward(dpre, w_up, dx2, x1, attended, w_proj, vec_rows, chooser):
    count, width = x1.shape
    half = width // 2
    low = jnp.bfloat16

    def body(dpre_ref, up_ref, dx2_ref, x1_ref, o_ref, proj_ref, v_ref, c_ref, dx1_ref, mixed_ref, keep_ref, sent_ref, vec_ref):
        dh2 = dot_second(dpre_ref[...], up_ref[...])
        back, gain, shift = norm_backward(dh2, x1_ref[...], v_ref[2:3, :])
        dx1 = back + dx2_ref[...]
        dx1_ref[...] = dx1
        da = dx1.astype(low)
        vec_ref[0:1, :] = gain
        vec_ref[1:2, :] = shift
        vec_ref[2:3, :] = column_sum(da)
        vec_ref[3:8, :] = jnp.zeros((5, width), jnp.float32)
        sent_ref[...] = dot_first(select_columns(o_ref[...], c_ref[1]), da).astype(low)
        keep_ref[...] = dot_first(select_columns(o_ref[...], c_ref[0]), da)
        mixed_ref[...] = dot_second(da, proj_ref[...]).astype(low)

    return pl.pallas_call(
        body,
        out_shape=[
            shape_of((count, width), jnp.float32),
            shape_of((count, width), low),
            shape_of((half, width), jnp.float32),
            shape_of((half, width), low),
            shape_of((8, width), jnp.float32),
        ],
        in_specs=[whole_block()] * 8,
        out_specs=[whole_block()] * 5,
        compiler_params=params(),
        cost_estimate=cost(12 * count * width * width, 12 * width * width),
    )(dpre, w_up, dx2, x1, attended, w_proj, vec_rows, chooser)


def attention_backward(mixed, dx1, packed, x0, normed, w_qkv, vec_rows, chooser, proj_keep, proj_sent, extra):
    count, width = x0.shape
    half = width // 2
    low = jnp.bfloat16

    def body(mixed_ref, dx1_ref, packed_ref, x0_ref, h1_ref, qkv_ref, v_ref, c_ref, pk_ref, ps_ref,
             dx0_ref, rows_ref, keep_ref, sent_ref, vec_ref, grad_ref):
        causal = causal_mask(count)
        for head in range(0, width // HD, 2):
            sides = ([], [], [])
            for one in (head, head + 1):
                queries = packed_ref[:, one * HD : (one + 1) * HD]
                keys = packed_ref[:, width + one * HD : width + (one + 1) * HD]
                values = packed_ref[:, 2 * width + one * HD : 2 * width + (one + 1) * HD]
                scores = causal_scores(queries, keys, causal)
                grown = jnp.exp(scores - jnp.max(scores, axis=-1, keepdims=True))
                probs = grown / jnp.sum(grown, axis=-1, keepdims=True)
                out_grad = mixed_ref[:, one * HD : (one + 1) * HD]
                grad_p = dot_second(out_grad, values)
                centre = jnp.sum(probs * grad_p, axis=-1, keepdims=True)
                grad_s = (probs * (grad_p - centre)).astype(low)
                sides[0].append(dot_plain(grad_s, keys) * HD ** (-0.5))
                sides[1].append(dot_first(grad_s, queries) * HD ** (-0.5))
                sides[2].append(dot_first(probs.astype(low), out_grad))
            for place, side in enumerate(sides):
                start = place * width + head * HD
                grad_ref[:, start : start + 2 * HD] = jnp.concatenate(side, axis=1).astype(low)
        dh1 = dot_second(grad_ref[...], qkv_ref[...])
        back, gain, shift = norm_backward(dh1, x0_ref[...], v_ref[0:1, :])
        vec_ref[0:1, :] = gain
        vec_ref[1:2, :] = shift
        vec_ref[2:3, :] = column_sum(grad_ref[:, :width])
        vec_ref[3:4, :] = column_sum(grad_ref[:, 2 * width :])
        vec_ref[4:8, :] = jnp.zeros((4, width), jnp.float32)
        dx0 = back + dx1_ref[...]
        dx0_ref[...] = dx0
        rows_ref[...] = dx0.astype(low)
        keep_cols = select_columns(h1_ref[...], c_ref[0])
        sent_cols = select_columns(h1_ref[...], c_ref[1])
        for place in range(3):
            span = slice(place * width, (place + 1) * width)
            sent_ref[:, span] = dot_first(sent_cols, grad_ref[:, span]).astype(low)
            keep_ref[:, span] = dot_first(keep_cols, grad_ref[:, span])
        sent_ref[:, 3 * width : 4 * width] = ps_ref[...]
        keep_ref[:, 3 * width : 4 * width] = pk_ref[...]

    return pl.pallas_call(
        body,
        out_shape=[
            shape_of((count, width), jnp.float32),
            shape_of((count, width), low),
            shape_of((half, 4 * width + extra), jnp.float32),
            shape_of((half, 4 * width + extra), low),
            shape_of((8, width), jnp.float32),
        ],
        in_specs=[whole_block()] * 10,
        out_specs=[whole_block()] * 5,
        scratch_shapes=[pltpu.VMEM((count, 3 * width), low)],
        compiler_params=params(),
        cost_estimate=cost(20 * count * width * width, 16 * width * width),
    )(mixed, dx1, packed, x0, normed, w_qkv, vec_rows, chooser, proj_keep, proj_sent)


def bit_of(index, level):
    return (index >> level) & 1


def xor_order(parts, index):
    level = 0
    while (1 << level) < len(parts):
        odd = bit_of(index, level) == 1
        step = 1 << level
        placed = list(parts)
        for place in range(len(parts)):
            if not place & step:
                low, high = parts[place], parts[place | step]
                placed[place] = jnp.where(odd, high, low)
                placed[place | step] = jnp.where(odd, low, high)
        parts = placed
        level += 1
    return parts


def tree_sum(parts):
    while len(parts) > 1:
        parts = [parts[place] + parts[place + 1] for place in range(0, len(parts), 2)]
    return parts[0]


def swap_core(value):
    count = lax.axis_size("vocab")
    return lax.ppermute(value, "vocab", [(i, i ^ 1) for i in range(count)])


def swap_outer(value, step):
    count = lax.axis_size("vocab")
    return lax.ppermute(value, "vocab", [(i, i ^ (2 * step)) for i in range(count)])


def swap_dp(value, step):
    count = lax.axis_size("dp")
    return lax.ppermute(value, "dp", [(i, i ^ step) for i in range(count)])


def places():
    vocab_index = lax.axis_index("vocab")
    return (lax.axis_index("dp"), vocab_index // 2, vocab_index % 2)


def gather_vocab(value):
    _, outer, core = places()
    pair = jnp.stack(xor_order([value, swap_core(value)], core))
    count = lax.axis_size("vocab") // 2
    parts = [pair] + [swap_outer(pair, step) for step in range(1, count)]
    return jnp.concatenate(xor_order(parts, outer), axis=0)


def gather_dp(value):
    dp_index, _, _ = places()
    parts = [value] + [swap_dp(value, step) for step in range(1, lax.axis_size("dp"))]
    return jnp.stack(xor_order(parts, dp_index))


def sum_all(value):
    value = value + swap_core(value)
    value = tree_sum([value] + [swap_dp(value, step) for step in range(1, lax.axis_size("dp"))])
    count = lax.axis_size("vocab") // 2
    return tree_sum([value] + [swap_outer(value, step) for step in range(1, count)])


def outer_parts(value):
    count = lax.axis_size("vocab") // 2
    return [value] + [swap_outer(value, step) for step in range(1, count)]


def behind(value, *others):
    return lax.optimization_barrier((value, others))[0]


class Slots:
    def __init__(self):
        self.last = None

    def open(self, value):
        return value if self.last is None else behind(value, self.last)

    def close(self, *results):
        self.last = results


class OuterGather:
    def __init__(self, value):
        self.held = value[None]

    def advance(self, slots):
        count = lax.axis_size("vocab") // 2
        step = count // (2 * self.held.shape[0])
        if step:
            shape = (-1,) + self.held.shape[1:]
            held = slots.open(self.held)
            self.held = jnp.stack([held, swap_outer(held, step)], axis=1).reshape(shape)

    def finish(self, slots):
        while self.held.shape[0] < lax.axis_size("vocab") // 2:
            self.advance(slots)
        return self.held


def ring_first(held, slots):
    held = slots.open(held)
    return (held, swap_dp(held, 1), swap_dp(held, 2))


def ring_second(parts, slots):
    held, from_one, from_two = parts
    half = held.shape[0] // 2
    low, high = slots.open((from_two[:half], from_one[half:]))
    return jnp.concatenate([held, from_one, from_two, swap_dp(low, 1), swap_dp(high, 2)], axis=0)


def place_blocks(held, other, cuts):
    dp_index, outer, core = places()
    count = held.shape[0]
    outer_count = lax.axis_size("vocab") // 2
    here = jnp.stack([dp_index, outer, core]).astype(jnp.int32)
    spans = []
    for width in cuts:
        spans.append((sum(w for _, w in spans), width))

    def body(here_ref, held_ref, other_ref, *refs):
        out_refs, sems = refs[: len(cuts)], refs[len(cuts)]

        def copies(block):
            dp_place = (block // outer_count) ^ here_ref[0]
            outer_place = (block % outer_count) ^ here_ref[1]
            target = (dp_place * outer_count + outer_place) * 2
            made = []
            for side, ref in enumerate((held_ref, other_ref)):
                place = target + (here_ref[2] ^ side)
                for index, (start, width) in enumerate(spans):
                    made.append(
                        pltpu.make_async_copy(
                            ref.at[block, :, pl.ds(start, width)],
                            out_refs[index].at[place],
                            sems.at[index, side, block],
                        )
                    )
            return made

        def start(block, carry):
            for copy in copies(block):
                copy.start()
            return carry

        def wait(block, carry):
            for copy in copies(block):
                copy.wait()
            return carry

        lax.fori_loop(0, count, start, 0)
        lax.fori_loop(0, count, wait, 0)

    any_space = pl.BlockSpec(memory_space=pl.ANY)
    return pl.pallas_call(
        body,
        out_shape=[
            jax.ShapeDtypeStruct((2 * count, held.shape[1], width), held.dtype) for width in cuts
        ],
        in_specs=[pl.BlockSpec(memory_space=pltpu.SMEM), any_space, any_space],
        out_specs=[pl.BlockSpec(memory_space=pltpu.VMEM) for _ in cuts],
        scratch_shapes=[pltpu.SemaphoreType.DMA((len(cuts), 2, count))],
        compiler_params=pltpu.CompilerParams(vmem_limit_bytes=VMEM_BYTES),
        cost_estimate=pl.CostEstimate(
            flops=0, bytes_accessed=4 * held.size * held.dtype.itemsize, transcendentals=0
        ),
    )(here, held, other)


def tile_of(values):
    row = lax.broadcasted_iota(jnp.int32, (8, 128), 0)
    lane = lax.broadcasted_iota(jnp.int32, (8, 128), 1)
    tile = jnp.zeros((8, 128), jnp.float32)
    for place, value in enumerate(values):
        if value is not None:
            tile = jnp.where((row == 0) & (lane == place), value, tile)
    return tile


def total_of(value):
    return jnp.sum(jnp.sum(value, axis=1, keepdims=True), axis=0, keepdims=True)


def fold_rows(value):
    return jnp.sum(value.reshape(-1, 8, value.shape[1]), axis=0)


def prepare_table(table, smalls, dp_count):
    rows, width = table.shape
    chunks = -(-rows // CHUNK)
    per = max(n for n in range(1, 9) if chunks % n == 0 and n * CHUNK <= rows)
    tile = per * CHUNK
    steps = chunks // per

    def body(table_ref, *refs):
        small_refs, (low_ref, sum_ref, acc_ref) = refs[: len(smalls)], refs[len(smalls) :]
        step = pl.program_id(0)
        row = lax.broadcasted_iota(jnp.int32, (tile, 1), 0) + step * tile
        value = jnp.where(row < rows, table_ref[...], 0.0)
        low_ref[...] = value.astype(jnp.bfloat16)
        part = fold_rows(value * value)

        @pl.when(step == 0)
        def _():
            acc_ref[...] = part

        @pl.when(step > 0)
        def _():
            acc_ref[...] += part

        @pl.when(step == steps - 1)
        def _():
            terms = [None] + [total_of(ref[...] * ref[...]) for ref in small_refs]
            terms.append(total_of(acc_ref[...]) / dp_count)
            sum_ref[...] = tile_of(terms)

    return pl.pallas_call(
        body,
        grid=(steps,),
        out_shape=[
            jax.ShapeDtypeStruct((chunks * CHUNK, width), jnp.bfloat16),
            jax.ShapeDtypeStruct((8, 128), jnp.float32),
        ],
        in_specs=[pl.BlockSpec((tile, width), lambda i: (i, 0))] + [whole_block() for _ in smalls],
        out_specs=[pl.BlockSpec((tile, width), lambda i: (i, 0)), whole_block()],
        scratch_shapes=[pltpu.VMEM((8, width), jnp.float32)],
        compiler_params=pltpu.CompilerParams(vmem_limit_bytes=VMEM_BYTES),
        cost_estimate=pl.CostEstimate(
            flops=4 * table.size, bytes_accessed=6 * table.size, transcendentals=0
        ),
    )(table, *smalls)


def head_stats(head_in, table_low, targets, first, rows):
    count = head_in.shape[0]
    chunks = table_low.shape[0] // CHUNK

    def body(first_ref, head_ref, table_ref, target_ref, out_ref):
        head = head_ref[...]
        target = target_ref[...]
        real = jnp.minimum(rows, V_REAL - first_ref[0])

        def step(index, carry, masked):
            top, total, hit, plain = carry
            begin = pl.multiple_of(index * CHUNK, CHUNK)
            values = dot_second(table_ref[pl.ds(begin, CHUNK), :], head)
            local = lax.broadcasted_iota(jnp.int32, (CHUNK, 1), 0) + begin
            columns = local + first_ref[0]
            if masked:
                columns = jnp.where(local < real, columns, -1)
                plain = plain + fold_rows(jnp.where(local < real, values, 0.0))
                values = jnp.where(local < real, values, MASKED)
            else:
                plain = plain + fold_rows(values)
            blocks = values.reshape(-1, 8, count)
            higher = jnp.maximum(top, jnp.max(blocks, axis=0))
            total = total * jnp.exp(top - higher) + jnp.sum(jnp.exp(blocks - higher[None]), axis=0)
            hit = hit + fold_rows(jnp.where(columns == target, values, 0.0))
            return (higher, total, hit, plain)

        zeros = jnp.zeros((8, count), jnp.float32)
        carry = (jnp.full((8, count), MASKED, jnp.float32), zeros, zeros, zeros)
        unmasked = jnp.maximum(real, 0) // CHUNK
        carry = lax.fori_loop(0, unmasked, functools.partial(step, masked=False), carry)
        carry = lax.fori_loop(unmasked, chunks, functools.partial(step, masked=True), carry)
        top, total, hit, plain = carry
        highest = jnp.max(top, axis=0, keepdims=True)
        out_ref[0:1, :] = highest
        out_ref[1:2, :] = jnp.sum(total * jnp.exp(top - highest), axis=0, keepdims=True)
        out_ref[2:3, :] = jnp.sum(hit, axis=0, keepdims=True)
        out_ref[3:4, :] = jnp.sum(plain, axis=0, keepdims=True)
        out_ref[4:8, :] = jnp.zeros((4, count), jnp.float32)

    return pl.pallas_call(
        body,
        out_shape=jax.ShapeDtypeStruct((8, count), jnp.float32),
        in_specs=[pl.BlockSpec(memory_space=pltpu.SMEM)] + [whole_block()] * 3,
        out_specs=whole_block(),
        compiler_params=pltpu.CompilerParams(vmem_limit_bytes=VMEM_BYTES),
        cost_estimate=pl.CostEstimate(
            flops=2 * table_low.size * count,
            bytes_accessed=2 * table_low.size,
            transcendentals=table_low.shape[0] * count,
        ),
    )(first, head_in, table_low, targets)


def logit_grad(values, columns, norms, targets, scale):
    drop = jnp.where(
        columns == targets,
        scale * (1.0 - SMOOTHING + SMOOTHING / V_REAL),
        scale * (SMOOTHING / V_REAL),
    )
    return jnp.exp(values - norms) - drop


def head_back(head_in, table_low, targets, norms, first, rows, scale):
    count, width = head_in.shape
    chunks = table_low.shape[0] // CHUNK

    def body(first_ref, head_ref, table_ref, target_ref, norm_ref, out_ref):
        head = head_ref[...]
        target = target_ref[...]
        norm = norm_ref[...]
        real = jnp.minimum(rows, V_REAL - first_ref[0])
        out_ref[...] = jnp.zeros_like(out_ref)

        def step(index, carry, masked):
            begin = pl.multiple_of(index * CHUNK, CHUNK)
            part = table_ref[pl.ds(begin, CHUNK), :]
            local = lax.broadcasted_iota(jnp.int32, (1, CHUNK), 1) + begin
            grad = logit_grad(
                dot_second(head, part), local + first_ref[0], norm, target, scale
            )
            if masked:
                grad = jnp.where(local < real, grad, 0.0)
            out_ref[...] += dot_plain(grad.astype(jnp.bfloat16), part)
            return carry

        unmasked = jnp.maximum(real, 0) // CHUNK
        lax.fori_loop(0, unmasked, functools.partial(step, masked=False), 0)
        lax.fori_loop(unmasked, chunks, functools.partial(step, masked=True), 0)

    return pl.pallas_call(
        body,
        out_shape=jax.ShapeDtypeStruct((count, width), jnp.float32),
        in_specs=[pl.BlockSpec(memory_space=pltpu.SMEM)] + [whole_block()] * 4,
        out_specs=whole_block(),
        compiler_params=pltpu.CompilerParams(vmem_limit_bytes=VMEM_BYTES),
        cost_estimate=pl.CostEstimate(
            flops=4 * table_low.size * count,
            bytes_accessed=2 * table_low.size,
            transcendentals=table_low.shape[0] * count,
        ),
    )(first, head_in, table_low, targets, norms)


def table_part(earlier, head_all, table_low, targets, norms, first, rows, scale, start, stop):
    count, width = head_all.shape
    block = min(512, count)

    def body(first_ref, head_ref, table_ref, target_ref, norm_ref, *refs):
        out_ref, done_ref = refs[-2:]
        done_ref[...] = jnp.zeros_like(done_ref)
        begin = (pl.program_id(0) + start) * PIECE
        real = jnp.minimum(rows, V_REAL - first_ref[0])
        part = table_ref[...]
        local = lax.broadcasted_iota(jnp.int32, (PIECE, 1), 0) + begin
        columns = local + first_ref[0]

        def total_of_blocks(masked):
            total = jnp.zeros((PIECE, width), jnp.float32)
            for place in range(0, count, block):
                span = slice(place, place + block)
                head = head_ref[span, :]
                grad = logit_grad(
                    dot_second(part, head), columns, norm_ref[:, span], target_ref[:, span], scale
                )
                if masked:
                    grad = jnp.where(local < real, grad, 0.0)
                total = total + dot_plain(grad.astype(jnp.bfloat16), head)
            return total

        @pl.when(begin + PIECE <= real)
        def _():
            out_ref[...] = total_of_blocks(False)

        @pl.when(begin + PIECE > real)
        def _():
            out_ref[...] = total_of_blocks(True)

    args = [first, head_all, table_low, targets, norms]
    specs = [
        pl.BlockSpec(memory_space=pltpu.SMEM),
        whole_block(),
        pl.BlockSpec((PIECE, width), lambda i: (i + start, 0)),
        whole_block(),
        whole_block(),
    ]
    aliases = {}
    if earlier is not None:
        aliases = {len(args): 0}
        args.append(earlier)
        specs.append(pl.BlockSpec(memory_space=pl.ANY))
    size = (stop - start) * PIECE
    return pl.pallas_call(
        body,
        grid=(stop - start,),
        out_shape=[
            jax.ShapeDtypeStruct(table_low.shape, jnp.float32),
            jax.ShapeDtypeStruct((8, 128), jnp.float32),
        ],
        in_specs=specs,
        out_specs=[pl.BlockSpec((PIECE, width), lambda i: (i + start, 0)), whole_block()],
        input_output_aliases=aliases,
        compiler_params=pltpu.CompilerParams(vmem_limit_bytes=VMEM_BYTES),
        cost_estimate=pl.CostEstimate(
            flops=4 * size * width * count,
            bytes_accessed=6 * size * width,
            transcendentals=size * count,
        ),
    )(*args)


def token_lists(ids, first, rows, cap):
    local = ids - first
    mine = (local >= 0) & (local < rows)
    tokens = jnp.arange(ids.shape[1], dtype=jnp.int32)
    before = (tokens[:, None] < tokens[None, :]).astype(jnp.float32)
    slot = dot_plain(mine.astype(jnp.float32), before).astype(jnp.int32)
    slots = jnp.arange(cap, dtype=jnp.int32)
    hot = (slot[:, None, :] == slots[None, :, None]) & mine[:, None, :]
    row = jnp.sum(jnp.where(hot, local[:, None, :], 0), axis=2)
    token = jnp.sum(jnp.where(hot, tokens[None, None, :], 0), axis=2)
    return (jnp.sum(mine.astype(jnp.int32), axis=1), row, token)


def add_rows(table_grad, held, other, counts, row_list, token_list, gradients, weight_sums, dp_count):
    padded, width = table_grad.shape
    dp_index, outer, core = places()
    here = jnp.stack([dp_index, outer, core]).astype(jnp.int32)
    outer_count = lax.axis_size("vocab") // 2
    sequences = counts.shape[0]
    cap = row_list.shape[1]
    chunks = padded // CHUNK

    def body(here_ref, count_ref, row_ref, token_ref, grad_in_ref, held_ref, other_ref, sums_ref, *refs):
        small_refs = refs[: len(gradients)]
        grad_out_ref, total_ref, grad_ref, rows_ref, in_sems, out_sems = refs[len(gradients) :]

        def in_copy(index):
            span = pl.ds(pl.multiple_of(index * CHUNK, CHUNK), CHUNK)
            return pltpu.make_async_copy(grad_in_ref.at[span], grad_ref.at[span], in_sems.at[index])

        def out_copy(index):
            span = pl.ds(pl.multiple_of(index * CHUNK, CHUNK), CHUNK)
            return pltpu.make_async_copy(grad_ref.at[span], grad_out_ref.at[span], out_sems.at[index])

        def start_in(index, carry):
            in_copy(index).start()
            return carry

        def wait_in(index, carry):
            in_copy(index).wait()
            return carry

        lax.fori_loop(0, chunks, start_in, 0)
        terms = [total_of(ref[...] * ref[...]) for ref in small_refs]
        lax.fori_loop(0, chunks, wait_in, 0)

        def sequence(index, carry):
            dp_place = (index // 2) // outer_count
            outer_place = (index // 2) % outer_count
            block = (dp_place ^ here_ref[0]) * outer_count + (outer_place ^ here_ref[1])

            @pl.when(index % 2 == here_ref[2])
            def _():
                rows_ref[...] = held_ref[block].astype(jnp.float32)

            @pl.when(index % 2 != here_ref[2])
            def _():
                rows_ref[...] = other_ref[block].astype(jnp.float32)

            def one(slot, carry):
                row = row_ref[index * cap + slot]
                token = token_ref[index * cap + slot]
                grad_ref[pl.ds(row, 1), :] += rows_ref[pl.ds(token, 1), :]
                return carry

            lax.fori_loop(0, count_ref[index], one, 0)
            return carry

        lax.fori_loop(0, sequences, sequence, 0)

        def square(index, acc):
            span = pl.ds(pl.multiple_of(index * CHUNK, CHUNK), CHUNK)
            out_copy(index).start()
            value = grad_ref[span, :]
            return acc + fold_rows(value * value)

        acc = lax.fori_loop(0, chunks, square, jnp.zeros((8, width), jnp.float32))
        clip = total_of(acc) / dp_count
        for term in terms:
            clip = clip + term
        total_ref[...] = sums_ref[...] + tile_of([clip])

        def wait_out(index, carry):
            out_copy(index).wait()
            return carry

        lax.fori_loop(0, chunks, wait_out, 0)

    smem = pl.BlockSpec(memory_space=pltpu.SMEM)
    any_space = pl.BlockSpec(memory_space=pl.ANY)
    return pl.pallas_call(
        body,
        out_shape=[
            jax.ShapeDtypeStruct(table_grad.shape, jnp.float32),
            jax.ShapeDtypeStruct((8, 128), jnp.float32),
        ],
        in_specs=[smem, smem, smem, smem, any_space, whole_block(), whole_block(), whole_block()]
        + [whole_block() for _ in gradients],
        out_specs=[any_space, whole_block()],
        scratch_shapes=[
            pltpu.VMEM((padded, width), jnp.float32),
            pltpu.VMEM(held.shape[1:], jnp.float32),
            pltpu.SemaphoreType.DMA((chunks,)),
            pltpu.SemaphoreType.DMA((chunks,)),
        ],
        input_output_aliases={4: 0},
        compiler_params=pltpu.CompilerParams(vmem_limit_bytes=VMEM_BYTES),
        cost_estimate=pl.CostEstimate(
            flops=2 * table_grad.size, bytes_accessed=8 * table_grad.size, transcendentals=0
        ),
    )(here, counts, row_list.reshape(-1), token_list.reshape(-1), table_grad, held, other, weight_sums, *gradients)


def moments_of(gradient, first, second, factor):
    clipped = gradient * factor
    first = BETA_ONE * first + (1.0 - BETA_ONE) * clipped
    second = BETA_TWO * second + (1.0 - BETA_TWO) * clipped * clipped
    return (first, second)


def update_of(weight, first, second):
    scaled = second * (1.0 / (1.0 - BETA_TWO**STEP))
    root = scaled * lax.rsqrt(scaled) + ADAM_EPS
    return first * (1.0 / (1.0 - BETA_ONE**STEP)) / root + DECAY * weight


def clip_factor(sums):
    return jnp.minimum(1.0, CLIP_AT / jnp.sqrt(sums[0:1, 0:1]))


def table_tile(rows, dp_count):
    return -(-rows // (3 * dp_count * 8)) * 8


def update_norms(sums, smalls, table_set, dp_count):
    weight, gradient, first, second = table_set
    rows, width = weight.shape
    tile = table_tile(rows, dp_count)
    here = lax.axis_index("dp").astype(jnp.int32).reshape(1)
    number = len(smalls)

    def body(here_ref, sums_ref, w_ref, g_ref, m_ref, s_ref, *refs):
        small_refs = refs[: 4 * number]
        out_refs = refs[4 * number : 7 * number]
        norm_ref, acc_ref, term_ref = refs[7 * number :]
        step = pl.program_id(0)
        factor = clip_factor(sums_ref[...])

        @pl.when(step == 0)
        def _():
            acc_ref[...] = jnp.zeros_like(acc_ref)
            terms = [None]
            for place in range(number):
                w, g, m, s = (ref[...] for ref in small_refs[4 * place : 4 * place + 4])
                m, s = moments_of(g, m, s, factor)
                u = update_of(w, m, s)
                out_refs[3 * place][...] = m
                out_refs[3 * place + 1][...] = s
                out_refs[3 * place + 2][...] = u
                terms.append(total_of(u * u))
            term_ref[...] = tile_of(terms)

        row = (here_ref[0] * 3 + step) * tile + lax.broadcasted_iota(jnp.int32, (tile, 1), 0)
        m, s = moments_of(g_ref[...], m_ref[...], s_ref[...], factor)
        u = jnp.where(row < rows, update_of(w_ref[...], m, s), 0.0)
        acc_ref[...] += fold_rows(u * u)

        @pl.when(step == 2)
        def _():
            norm_ref[...] = term_ref[...] + tile_of([None] * (number + 1) + [total_of(acc_ref[...])])

    block = pl.BlockSpec((tile, width), lambda i, here_ref: (here_ref[0] * 3 + i, 0))
    flat = [value for group in smalls for value in group]
    outs = [jax.ShapeDtypeStruct(group[0].shape, jnp.float32) for group in smalls for _ in range(3)]
    made = pl.pallas_call(
        body,
        grid_spec=pltpu.PrefetchScalarGridSpec(
            num_scalar_prefetch=1,
            grid=(3,),
            in_specs=[whole_block()] + [block] * 4 + [whole_block() for _ in flat],
            out_specs=[whole_block() for _ in outs] + [whole_block()],
            scratch_shapes=[pltpu.VMEM((8, width), jnp.float32), pltpu.VMEM((8, 128), jnp.float32)],
        ),
        out_shape=outs + [jax.ShapeDtypeStruct((8, 128), jnp.float32)],
        compiler_params=pltpu.CompilerParams(vmem_limit_bytes=VMEM_BYTES),
        cost_estimate=pl.CostEstimate(
            flops=20 * tile * 3 * width, bytes_accessed=16 * tile * 3 * width, transcendentals=2 * tile * 3 * width
        ),
    )(here, sums, weight, gradient, first, second, *flat)
    return ([made[3 * place : 3 * place + 3] for place in range(number)], made[-1])


def write_updates(sums, norms, smalls, table_set):
    weight, gradient, first, second = table_set
    rows, width = weight.shape
    tile = table_tile(rows, lax.axis_size("dp"))
    steps = -(-rows // tile)
    number = len(smalls)

    def body(sums_ref, norms_ref, w_ref, g_ref, m_ref, s_ref, *refs):
        small_refs = refs[: 2 * number]
        out_w, out_m, out_s = refs[2 * number : 2 * number + 3]
        small_outs = refs[2 * number + 3 :]
        sums = sums_ref[...]
        pace = RATE * jnp.sqrt(sums) / jnp.sqrt(norms_ref[...])

        @pl.when(pl.program_id(0) == 0)
        def _():
            for place in range(number):
                w, u = (ref[...] for ref in small_refs[2 * place : 2 * place + 2])
                small_outs[place][...] = w - pace[0:1, place + 1 : place + 2] * u

        m, s = moments_of(g_ref[...], m_ref[...], s_ref[...], clip_factor(sums))
        w = w_ref[...]
        out_m[...] = m
        out_s[...] = s
        out_w[...] = w - pace[0:1, number + 1 : number + 2] * update_of(w, m, s)

    block = pl.BlockSpec((tile, width), lambda i: (i, 0))
    flat = [value for group in smalls for value in group]
    outs = [jax.ShapeDtypeStruct(weight.shape, jnp.float32)] * 3
    outs += [jax.ShapeDtypeStruct(group[0].shape, jnp.float32) for group in smalls]
    return pl.pallas_call(
        body,
        grid=(steps,),
        out_shape=outs,
        in_specs=[whole_block(), whole_block()] + [block] * 4 + [whole_block() for _ in flat],
        out_specs=[block] * 3 + [whole_block() for _ in smalls],
        compiler_params=pltpu.CompilerParams(vmem_limit_bytes=VMEM_BYTES),
        cost_estimate=pl.CostEstimate(
            flops=20 * weight.size, bytes_accessed=28 * weight.size, transcendentals=2 * weight.size
        ),
    )(sums, norms, weight, gradient, first, second, *flat)


def pick_half(value, index, axis):
    return lax.dynamic_index_in_dim(value, index, axis, keepdims=False)


class OuterSum:
    def __init__(self, held):
        self.held = held
        self.step = 1

    def advance(self, slots):
        held = self.held
        if held.shape[0] > 1:
            _, outer, _ = places()
            pairs = held.reshape((-1, 2) + held.shape[1:])
            own = (outer // self.step) % 2
            out = slots.open(pick_half(pairs, 1 - own, 1).astype(jnp.bfloat16))
            self.held = pick_half(pairs, own, 1) + swap_outer(out, self.step).astype(jnp.float32)
            self.step *= 2

    def finish(self, slots):
        while self.held.shape[0] > 1:
            self.advance(slots)
        return self.held.reshape(self.held.shape[1:])


def scatter_core(keep, sent, slots):
    held = keep + swap_core(slots.open(sent)).astype(jnp.float32)
    return held.reshape((4, -1) + keep.shape[1:])


def scatter_first(held, slots):
    dp_index, _, _ = places()
    half = held.shape[1] // 2
    low = jnp.bfloat16
    own, one, two, three = [pick_half(held, dp_index ^ step, 0) for step in range(4)]
    three = slots.open(three.astype(low))
    into_two = swap_dp(three[:half], 1)
    into_one = swap_dp(three[half:], 2)
    one = jnp.concatenate(
        [one[:half].astype(low), (one[half:] + into_one.astype(jnp.float32)).astype(low)], axis=0
    )
    two = jnp.concatenate(
        [(two[:half] + into_two.astype(jnp.float32)).astype(low), two[half:].astype(low)], axis=0
    )
    return (own, one, two)


def scatter_second(parts, slots):
    own, one, two = parts
    one, two = slots.open((one, two))
    return own + (swap_dp(one, 1).astype(jnp.float32) + swap_dp(two, 2).astype(jnp.float32))


def shards(
    token_ids,
    pick_rows,
    target_ids,
    attn_in,
    attn_out,
    mlp_in,
    mlp_out,
    positions,
    vectors,
    table,
    *moments,
):
    low = jnp.bfloat16
    dp_index, outer, core = places()
    dp_count = lax.axis_size("dp")
    shard_count = lax.axis_size("vocab")
    device_count = dp_count * shard_count
    outer_count = shard_count // 2
    vocab_rows, width = table.shape
    seq_len = token_ids.shape[1]
    pick_count = pick_rows.shape[1]
    vocab_start = lax.axis_index("vocab") * vocab_rows

    slots = Slots()
    unit_rows = attn_in.shape[0]
    small_count = positions.size + vectors.size
    small_width = -(-small_count // (unit_rows * 128)) * 128
    small = jnp.concatenate([positions.astype(low).reshape(-1), vectors.astype(low).reshape(-1)])
    small = jnp.pad(small, (0, unit_rows * small_width - small_count))
    first = OuterGather(
        jnp.concatenate(
            [attn_in.astype(low), attn_out.astype(low), small.reshape(unit_rows, small_width)], axis=1
        )
    )
    up = OuterGather(mlp_in.astype(low))
    down = OuterGather(mlp_out.astype(low))
    small_masters = (attn_in, attn_out, mlp_in, mlp_out, positions, vectors)

    first.advance(slots)
    packed_ids = jnp.concatenate([token_ids, target_ids], axis=1)
    ids_pair = jnp.stack(xor_order([packed_ids, swap_core(packed_ids)], core))
    slots.close(first.held, ids_pair)

    first.finish(slots)
    ids_parts = outer_parts(slots.open(ids_pair))
    group_packed = jnp.concatenate(xor_order(ids_parts, outer), axis=0).reshape(shard_count, -1)
    group_ids = group_packed[:, :seq_len]
    group_targets = group_packed[:, seq_len:]
    slots.close(first.held, group_packed)

    first_ring = ring_first(first.held, slots)
    up.advance(slots)
    table_low, weight_sums = prepare_table(slots.open(table), small_masters, dp_count)
    slots.close(first_ring, up.held, table_low)

    first_held = ring_second(first_ring, slots)
    up.finish(slots)
    slots.close(first_held, up.held)

    up_ring = ring_first(up.held, slots)
    first_other = swap_core(slots.open(first_held))
    down.advance(slots)
    group_local = slots.open(group_ids) - vocab_start
    mine = (group_local >= 0) & (group_local < vocab_rows)
    served = jnp.take(table, jnp.where(mine, group_local, 0).reshape(-1), axis=0)
    served = jnp.where(mine.reshape(-1)[:, None], served, 0.0).astype(low)
    served = served.reshape(outer_count, 2, seq_len, width)
    slots.close(up_ring, first_other, down.held, served)

    up_held = ring_second(up_ring, slots)
    down.finish(slots)
    served = slots.open(served)
    embedded = pick_half(served, core, 1) + swap_core(pick_half(served, 1 - core, 1))
    embedded = OuterSum(embedded.astype(jnp.float32))
    w_qkv, w_proj, small_all = place_blocks(
        slots.open(first_held), first_other, (3 * width, width, small_width)
    )
    slots.close(up_held, down.held, embedded.held, w_qkv)

    down_ring = ring_first(down.held, slots)
    up_other = swap_core(slots.open(up_held))
    embedded = embedded.finish(slots)
    w_qkv = w_qkv.reshape(width, 3 * width)
    w_proj = w_proj.reshape(width, width)
    small_all = small_all.reshape(device_count, -1)
    pos_low = small_all[:, : positions.size].reshape(seq_len, width)
    vec_low = small_all[:, positions.size : small_count].reshape((device_count,) + vectors.shape)
    vec_rows = jnp.moveaxis(vec_low, 0, 1).reshape(vectors.shape[0], width).astype(jnp.float32)
    resid_in, normed_one, packed, attended, resid_mid, normed_two = attention_forward(
        embedded, pos_low, vec_rows, w_qkv, w_proj
    )
    slots.close(down_ring, up_other, embedded, vec_rows)

    down_held = ring_second(down_ring, slots)
    w_up = place_blocks(slots.open(up_held), up_other, (mlp_in.shape[1],))[0].reshape(width, -1)
    slots.close(down_held, w_up, normed_two)

    down_other = swap_core(slots.open(down_held))
    hidden_pre, hidden_act = hidden_forward(slots.open(normed_two), vec_rows, w_up)
    w_down = place_blocks(down_held, down_other, (width,))[0].reshape(-1, width)
    picks = pick_rows.reshape(-1, 1)
    resid_out, picked = output_forward(hidden_act, w_down, resid_mid, vec_rows, picks)

    same_core = jnp.stack(outer_parts(picked))
    ordered = jnp.stack(xor_order([same_core[step] for step in range(outer_count)], outer))
    head_in = jnp.stack(xor_order([ordered, swap_core(ordered)], core), axis=1)
    head_in = head_in.reshape(-1, width)
    first_column = vocab_start.astype(jnp.int32).reshape(1)
    flat_targets = group_targets.reshape(1, -1)
    stats = gather_vocab(head_stats(head_in, table_low, flat_targets, first_column, vocab_rows))
    stats = stats.reshape(shard_count, 8, -1)
    row_top = jnp.max(stats[:, 0], axis=0)
    exp_total = jnp.sum(stats[:, 1] * jnp.exp(stats[:, 0] - row_top[None]), axis=0)
    target_logit = jnp.sum(stats[:, 2], axis=0)
    logit_total = jnp.sum(stats[:, 3], axis=0)
    log_norm = row_top + jnp.log(exp_total)
    row_loss = (1.0 - SMOOTHING) * (log_norm - target_logit) + SMOOTHING * (
        log_norm - logit_total / V_REAL
    )
    token_count = device_count * pick_count

    partial = head_back(
        head_in,
        table_low,
        flat_targets.reshape(-1, 1),
        (log_norm + math.log(token_count)).reshape(-1, 1),
        first_column,
        vocab_rows,
        1.0 / token_count,
    )
    partial = partial.reshape(outer_count, 2, pick_count, width)
    held = pick_half(partial, core, 1) + swap_core(
        pick_half(partial, 1 - core, 1).astype(low)
    ).astype(jnp.float32)
    terms = [pick_half(held, outer, 0)]
    for step in range(1, outer_count):
        out = pick_half(held, outer ^ step, 0).astype(low)
        terms.append(swap_outer(out, step).astype(jnp.float32))
    picked_grad = tree_sum(terms)
    ring = ring_second(ring_first(same_core, Slots()), Slots())
    head_all = place_blocks(ring, swap_core(ring), (width,))[0].reshape(-1, width)
    rows_stats = gather_dp(jnp.stack([log_norm, row_loss]))
    norm_all = (rows_stats[:, 0] + math.log(token_count)).reshape(1, -1)
    loss = jnp.sum(rows_stats[:, 1]) / token_count
    packed_all = gather_dp(behind(group_packed, same_core)).reshape(device_count, -1)
    targets_all = packed_all[:, seq_len:].reshape(1, -1)
    counts, row_list, token_list = token_lists(
        packed_all[:, :seq_len], vocab_start, vocab_rows, 4 * seq_len // shard_count
    )

    slots = Slots()
    blocks = (-1, unit_rows)
    unit_choosers = choosers(width, unit_rows, core)
    grad_top, grad_branch, down_keep, down_sent, vec_down = output_backward(
        picked_grad, picks, resid_out, vec_rows, hidden_act, choosers(width, mlp_out.shape[0], core)
    )
    down_shape = (-1,) + mlp_out.shape
    down = scatter_core(down_keep.reshape(down_shape), down_sent.reshape(down_shape), slots)
    grad_pre, up_keep, up_sent, vec_up = hidden_backward(
        grad_branch, w_down, hidden_pre, normed_two, unit_choosers
    )
    slots.close(down, grad_pre)

    down = scatter_first(down, slots)
    up_shape = blocks + up_keep.shape[1:]
    up = scatter_core(up_keep.reshape(up_shape), up_sent.reshape(up_shape), slots)
    grad_mid, grad_mixed, proj_keep, proj_sent, vec_middle = middle_backward(
        slots.open(grad_pre),
        w_up,
        grad_top,
        resid_mid,
        attended,
        w_proj,
        vec_rows,
        unit_choosers,
    )
    slots.close(down, up, grad_mid)

    down = OuterSum(scatter_second(down, slots))
    grad_in, grad_rows, first_keep, first_sent, vec_first = attention_backward(
        grad_mixed,
        slots.open(grad_mid),
        packed,
        resid_in,
        normed_one,
        w_qkv,
        vec_rows,
        unit_choosers,
        proj_keep,
        proj_sent,
        small_width,
    )
    slots.close(down.held, grad_in)

    vec_grad = jnp.concatenate(
        [
            vec_first[0:2],
            vec_middle[0:2],
            vec_down[0:2],
            vec_first[2:4],
            vec_middle[2:3],
            vec_down[2:3],
            vec_up[0:4],
        ],
        axis=0,
    )
    vec_width = vectors.shape[1]
    vec_blocks = jnp.moveaxis(vec_grad.reshape(-1, device_count, vec_width), 1, 0)
    small_grad = jnp.concatenate(
        [grad_in.reshape(device_count, -1), vec_blocks.reshape(device_count, -1)], axis=1
    )
    small_grad = jnp.pad(small_grad, ((0, 0), (0, unit_rows * small_width - small_count)))
    small_grad = small_grad.reshape(-1, 2, unit_rows, small_width)
    first_keep = first_keep.reshape(blocks + first_keep.shape[1:])
    first_keep = first_keep.at[:, :, 4 * width :].set(pick_half(small_grad, core, 1))
    first_sent = first_sent.reshape(blocks + first_sent.shape[1:])
    first_sent = first_sent.at[:, :, 4 * width :].set(pick_half(small_grad, 1 - core, 1).astype(low))

    pieces = table_low.shape[0] // PIECE
    parts = 5 if pieces % 5 == 0 else 1

    def head_part(earlier, part, mark):
        if part >= parts:
            return (earlier, mark)
        return table_part(
            earlier,
            head_all,
            table_low,
            targets_all,
            behind(norm_all, mark),
            first_column,
            vocab_rows,
            1.0 / token_count,
            part * pieces // parts,
            (part + 1) * pieces // parts,
        )

    up = scatter_first(up, slots)
    down.advance(slots)
    rows = OuterGather(slots.open(grad_rows))
    slots.close(up, down.held, first_sent)

    up = OuterSum(scatter_second(up, slots))
    first = scatter_core(first_keep, first_sent, slots)
    rows.advance(slots)
    down_own = down.finish(slots)
    table_grad, mark = head_part(None, 0, slots.last)
    slots.close(up.held, first, rows.held, down_own, mark)

    first = scatter_first(first, slots)
    rows_outer = rows.finish(slots)
    up.advance(slots)
    table_grad, mark = head_part(table_grad, 1, slots.last)
    slots.close(first, rows_outer, up.held, mark)

    first = OuterSum(scatter_second(first, slots))
    up_own = up.finish(slots)
    table_grad, mark = head_part(table_grad, 2, slots.last)
    slots.close(first.held, up_own, mark)

    rows_ring = ring_first(rows_outer, slots)
    first.advance(slots)
    table_grad, mark = head_part(table_grad, 3, slots.last)
    slots.close(rows_ring, first.held, mark)

    rows_held = ring_second(rows_ring, slots)
    first_own = first.finish(slots)
    table_grad, mark = head_part(table_grad, 4, slots.last)
    slots.close(rows_held, first_own, mark)

    rows_other = swap_core(slots.open(rows_held))
    small_own = first_own[:, 4 * width :].reshape(-1)
    gradients = (
        first_own[:, : 3 * width],
        first_own[:, 3 * width : 4 * width],
        up_own,
        down_own,
        small_own[: positions.size].reshape(positions.shape),
        small_own[positions.size : small_count].reshape(vectors.shape),
    )
    table_grad, sums = add_rows(
        table_grad, rows_held, rows_other, counts, row_list, token_list, gradients, weight_sums, dp_count
    )
    sums = sum_all(sums)
    grad_norm = jnp.sqrt(sums[0, 0])
    firsts, seconds = moments[:7], moments[7:]
    smalls = list(zip(small_masters, gradients, firsts, seconds))
    table_set = (table, table_grad, firsts[6], seconds[6])
    made, norms = update_norms(sums, smalls, table_set, dp_count)
    norms = sum_all(norms)
    ratios = jnp.sqrt(sums[0, 1:8]) / jnp.sqrt(norms[0, 1:8])
    written = write_updates(
        sums, norms, [(weight, group[2]) for weight, group in zip(small_masters, made)], table_set
    )
    new_weights = list(written[3:]) + [written[0]]
    new_firsts = [group[0] for group in made] + [written[1]]
    new_seconds = [group[1] for group in made] + [written[2]]
    return (loss, grad_norm, ratios, *new_weights, *new_firsts, *new_seconds)


def solution(mesh):
    rows = P(("dp", "vocab"), None)
    weights = (rows, rows, rows, rows, rows, P(None, ("dp", "vocab")), P("vocab", None))
    return jax.shard_map(
        shards,
        mesh=mesh,
        in_specs=(rows, rows, rows) + weights * 3,
        out_specs=(P(), P(), P()) + weights * 3,
        check_vma=False,
    )
```

time: 833 us -> 617 us (0.74); the launches traced: 833 us -> 606 us
  Pallas kernels: 0 us -> 284 us
  other arithmetic: 248 us -> 48.9 us
  matrix products: 124 us -> 0.14 us
  waiting for transfers between devices: 195 us -> 94.1 us
  starting transfers between devices: 181 us -> 102 us
  between operations: 20.6 us -> 5.87 us
    pallas_call x0 -> x22, Pallas kernels: none -> 284 us  [the longest x5 67.7 us: table_part(): pl.pallas_call(body, grid=(stop - start,), out_shape=[jax.ShapeDtypeStruc...]
    dot_general x30 -> x0, matrix products: 104 us -> none  [the longest x6 60 us: dot_second(): lax.dot_general(left_op, right_op, (((1,), (1,)), ((), ())), preferred_el...]
    reduce_sum x34 -> x2, other arithmetic: 97.3 us -> 1.95 us  [the longest x1 1.16 us: token_lists(): token = jnp.sum(jnp.where(hot, tokens[None, None, :], 0), axis=2)]
    ppermute x60 -> x44, waiting for transfers between devices: 125 us -> 40.5 us  [swap_dp(): return lax.ppermute(value, 'dp', [(i, i ^ step) for i in range(count)])]
    ppermute x84 -> x34, starting transfers between devices: 112 us -> 50.4 us  [swap_outer(): lax.ppermute(value, 'vocab', [(i, i ^ 2 * step) for i in range(count)])]
    scatter-add x1 -> x0, other arithmetic: 41.4 us -> none  [shards(): table_grad.at[jnp.where(inside, local_all, vocab_rows)]]
    sub x8 -> x0, other arithmetic: 32.9 us -> none  [the longest x7 32.3 us: shards(): weight - RATE * ratios[index] * update]
    another operation x38 -> x16, other arithmetic: 33.4 us -> 6.47 us  [the longest x2 2.64 us: choosers(): return jnp.stack(made)]
  transfers between devices with their start and end apart: 173 -> 93, of which waited for: 72 -> 41; matrix products, arithmetic and copies ran while one was open for 29% -> 16% of each run, Pallas kernels for 0% -> 24%
where the time goes in v2:
time: 617 us; the launch traced here: 606 us
  Pallas kernels  284 us (46%)
  starting transfers between devices  102 us (17%)
  waiting for transfers between devices  94.1 us (15%)
  local copies, waits for them, and re-layouts  69.8 us (11%)
  other arithmetic  48.9 us (8%)
    pallas_call x5, Pallas kernels, table_part(): pl.pallas_call(body, grid=(stop - start,), out_shape=[jax.ShapeDtypeStruc...  67.7 us
    pallas_call x1, Pallas kernels, write_updates(): pl.pallas_call(body, grid=(steps,), out_shape=outs, in_specs=[whole_block...  54.8 us
    ppermute x34, starting transfers between devices, swap_outer(): lax.ppermute(value, 'vocab', [(i, i ^ 2 * step) for i in range(count)])  50.4 us
    ppermute x34, waiting for transfers between devices, swap_outer(): lax.ppermute(value, 'vocab', [(i, i ^ 2 * step) for i in range(count)])  47.6 us
    ppermute x44, starting transfers between devices, swap_dp(): return lax.ppermute(value, 'dp', [(i, i ^ step) for i in range(count)])  47.3 us
    ppermute x44, waiting for transfers between devices, swap_dp(): return lax.ppermute(value, 'dp', [(i, i ^ step) for i in range(count)])  40.5 us
    unnamed x63, local copies, waits for them, and re-layouts  24.7 us
    pallas_call x1, Pallas kernels, add_rows(): pl.pallas_call(body, out_shape=[jax.ShapeDtypeStruct(table_grad.shape, jn...  23.7 us
  transfers between devices with their start and end apart: 93, of which 41 were waited for; matrix products, arithmetic and copies ran while one was open for 16% of the time, Pallas kernels for 24%

profile of v2, /device:TPU:0, one launch (start us, length us, event | category | flops | bytes accessed | tf_op | source)
XLA Modules:
  0.0 605.5 jit_solution(15666922770735567655)
XLA Ops:
  5.9 3.7 collective-permute-start.1
  10.5 7.2 %collective-permute-done.1 = bf16[1,24,3328]{2,1,0:T(8,128)(2,1)S(1)} collective-permute-done((bf16[1,24,3328]{2,1,0:T(8,128)(2,1)S(1)}, bf16[1,24,3328]{2,1,0:T(8,128)(2,1)S(1)}, u32[]{:S(2)}, u32[]{:S(2)}) %collective-permute-start.1) | collective-permute-done | bytes 159776 | tf_op jit(solution)/shard_map/ppermute | solution.py:444
  17.7 3.6 collective-permute-start.2
  23.4 2.6 collective-permute-done.3
  26.0 5.0 collective-permute-done.5
  34.2 2.3 collective-permute-start.8
  37.3 12.6 %shard_map.415 = (bf16[6400,768]{1,0:T(8,128)(2,1)}, f32[8,128]{1,0:T(8,128)}) custom-call(f32[6288,768]{1,0:T(8,128)} %w_ref.3, f32[24,2304]{1,0:T(8,128)} %refs_0_.5, f32[24,768]{1,0:T(8,128)} %refs_2_.5, f32[24,3072]{1,0:T(8,128)} %refs_4_.5, f32[96,768]{1,0:T(8,128)} %refs_6_.3, f32[4,768]{1,0:T(4,128)} %refs_8_.3, f32[14,24]{1,0:T(8,128)} %refs_10_.3), custom_call_target="tpu_custom_call" | custom-call | flops 19316736 | bytes 28975104 | tf_op jit(solution)/shard_map/pallas_call | solution.py:633
  63.7 11.0 %gather_fusion = bf16[1024,768]{1,0:T(8,128)(2,1)S(1)} fusion(f32[6288,768]{1,0:T(8,128)} %w_ref.3, s32[1024]{0:T(1024)S(1)} %broadcast_clamp_fusion), kind=kCustom, calls=%fused_computation | custom fusion | bytes 3149824 | tf_op jit(solution)/shard_map/jit(_take)/gather | solution.py:1174
  82.0 6.5 %shard_map.416 = (bf16[32,24,2304]{2,1,0:T(8,128)(2,1)}, bf16[32,24,768]{2,1,0:T(8,128)(2,1)}, bf16[32,24,256]{2,1,0:T(8,128)(2,1)}) custom-call(s32[3]{0:T(128)} %pad_add_fusion.1.here_ref, bf16[16,24,3328]{2,1,0:T(8,128)(2,1)} %constant_dynamic-update-slice_fusion.2.held_ref, bf16[16,24,3328]{2,1,0:T(8,128)(2,1)} %collective-permute-done.14.other_ref), custom_call_target="tpu_custom_call" | custom-call | bytes 10223616 | tf_op jit(solution)/shard_map/pallas_call | solution.py:571
  96.2 6.6 %collective-permute-done.20 = bf16[2,128,768]{2,1,0:T(8,128)(2,1)S(1)} collective-permute-done((bf16[2,128,768]{2,1,0:T(8,128)(2,1)S(1)}, bf16[2,128,768]{2,1,0:T(8,128)(2,1)S(1)}, u32[]{:S(2)}, u32[]{:S(2)}) %collective-permute-start.20) | collective-permute-done | bytes 393248 | tf_op jit(solution)/shard_map/ppermute | solution.py:444
  102.9 2.3 collective-permute-start.21
  111.7 2.5 collective-permute-done.21
  119.9 8.0 %shard_map.417 = (f32[128,768]{1,0:T(8,128)}, bf16[128,768]{1,0:T(8,128)(2,1)}, bf16[128,2304]{1,0:T(8,128)(2,1)}, bf16[128,768]{1,0:T(8,128)(2,1)}, f32[128,768]{1,0:T(8,128)}, /*index=5*/bf16[128,768]{1,0:T(8,128)(2,1)}) custom-call(f32[128,768]{1,0:T(8,128)} %add_bitcast_fusion.e_ref, bf16[128,768]{1,0:T(8,128)(2,1)} %reshape.678.p_ref, ...), custom_call_target="tpu_custom_call" | custom-call | flops 1207959552 | bytes 4718592 | tf_op jit(solution)/shard_map/pallas_call | solution.py:126
  127.9 5.7 shard_map.418
  134.8 5.0 shard_map.419
  139.8 5.6 shard_map.420
  145.4 4.5 shard_map.421
  149.9 2.3 collective-permute-start.28
  154.3 3.3 collective-permute-done.28
  157.6 3.4 collective-permute-done.29
  164.9 14.2 %shard_map.422 = f32[8,512]{1,0:T(8,128)} custom-call(s32[1]{0:T(128)} %bitcast.first_ref, bf16[512,768]{1,0:T(8,128)(2,1)} %bitcast.341, bf16[6400,768]{1,0:T(8,128)(2,1)} %get-tuple-element.184.table_ref, s32[1,512]{1,0:T(1,128)} %reshape.685.target_ref), custom_call_target="tpu_custom_call" | custom-call | flops 5033164800 | bytes 9830400 | tf_op jit(solution)/shard_map/pallas_call | solution.py:690
  181.3 2.3 collective-permute-start.33
  189.4 17.8 %shard_map.424 = f32[512,768]{1,0:T(8,128)} custom-call(s32[1]{0:T(128)} %bitcast.first_ref, bf16[512,768]{1,0:T(8,128)(2,1)} %bitcast.342, bf16[6400,768]{1,0:T(8,128)(2,1)} %get-tuple-element.184.table_ref, s32[512,1]{1,0:T(8,128)} %reshape_reshape.4.target_ref, f32[512,1]{1,0:T(8,128)} %copy.97.norm_ref), custom_call_target="tpu_custom_call" | custom-call | flops 10066329600 | bytes 9830400 | tf_op jit(solution)/shard_map/pallas_call | solution.py:740
  217.4 6.0 collective-permute-done.49
  224.1 7.0 %shard_map.425 = (f32[128,768]{1,0:T(8,128)}, bf16[128,768]{1,0:T(8,128)(2,1)}, f32[1536,768]{1,0:T(8,128)}, bf16[1536,768]{1,0:T(8,128)(2,1)}, f32[8,768]{1,0:T(8,128)}) custom-call(f32[64,768]{1,0:T(8,128)} %fusion.30.g_ref, s32[64,1]{1,0:T(8,128)} %copy.90.pick_ref, f32[128,768]{1,0:T(8,128)} %get-tuple-element.214.x_ref, f32[14,768]{1,0:T(8,128)} %reshape.715.v_ref, ...), custom_call_target="tpu_custom_call" | custom-call | flops 1207959552 | bytes 7077888 | tf_op jit(solution)/shard_map/pallas_call | solution.py:258
  241.0 5.3 collective-permute-done.40
  248.5 9.8 %shard_map.426 = (bf16[128,3072]{1,0:T(8,128)(2,1)}, f32[384,3072]{1,0:T(8,128)}, bf16[384,3072]{1,0:T(8,128)(2,1)}, f32[8,768]{1,0:T(8,128)}) custom-call(bf16[128,768]{1,0:T(8,128)(2,1)} %get-tuple-element.215.dy_ref, bf16[3072,768]{1,0:T(8,128)(2,1)} %bitcast.287, f32[128,3072]{1,0:T(8,128)} %get-tuple-element.216.pre_ref, ...), custom_call_target="tpu_custom_call" | custom-call | flops 1811939328 | bytes 18874368 | tf_op jit(solution)/shard_map/pallas_call | solution.py:298
  259.7 3.6 convert_add_fusion.2
  271.7 3.9 collective-permute-done.45
  279.8 8.1 %shard_map.427 = (f32[128,768]{1,0:T(8,128)}, bf16[128,768]{1,0:T(8,128)(2,1)}, f32[384,768]{1,0:T(8,128)}, bf16[384,768]{1,0:T(8,128)(2,1)}, f32[8,768]{1,0:T(8,128)}) custom-call(bf16[128,3072]{1,0:T(8,128)(2,1)} %get-tuple-element.220.dpre_ref, bf16[768,3072]{1,0:T(8,128)(2,1)} %bitcast.285, f32[128,768]{1,0:T(8,128)} %get-tuple-element.221.dx2_ref, ...), custom_call_target="tpu_custom_call" | custom-call | flops 905969664 | bytes 7077888 | tf_op jit(solution)/shard_map/pallas_call | solution.py:332
  291.5 3.7 convert_add_fusion.1
  295.2 2.2 copy-done.1
  297.5 14.5 %shard_map.428 = (f32[128,768]{1,0:T(8,128)}, bf16[128,768]{1,0:T(8,128)(2,1)}, f32[384,3328]{1,0:T(8,128)}, bf16[384,3328]{1,0:T(8,128)(2,1)}, f32[8,768]{1,0:T(8,128)}) custom-call(bf16[128,768]{1,0:T(8,128)(2,1)} %get-tuple-element.223.mixed_ref, f32[128,768]{1,0:T(8,128)} %get-tuple-element.229.dx1_ref, bf16[128,2304]{1,0:T(8,128)(2,1)} %get-tuple-element.230.packed_ref, ...), custom_call_target="tpu_custom_call" | custom-call | flops 1509949440 | bytes 9437184 | tf_op jit(solution)/shard_map/pallas_call | solution.py:394
  318.2 11.9 %collective-permute-done.55 = bf16[4,96,768]{2,1,0:T(8,128)(2,1)S(1)} collective-permute-done((bf16[4,96,768]{2,1,0:T(8,128)(2,1)}, bf16[4,96,768]{2,1,0:T(8,128)(2,1)S(1)}, u32[]{:S(2)}, u32[]{:S(2)}) %collective-permute-start.55) | collective-permute-done | bytes 589856 | tf_op jit(solution)/shard_map/ppermute | solution.py:449
  337.3 2.6 collective-permute-done.59
  345.6 4.8 shard_map.423
  356.8 13.3 %shard_map.429 = (f32[6400,768]{1,0:T(8,128)}, f32[8,128]{1,0:T(8,128)}) custom-call(s32[1]{0:T(128)} %bitcast.first_ref, bf16[2048,768]{1,0:T(8,128)(2,1)} %bitcast.279, bf16[6400,768]{1,0:T(8,128)(2,1)} %get-tuple-element.184.table_ref, s32[1,2048]{1,0:T(1,128)} %reshape.690.target_ref, f32[1,2048]{1,0:T(1,128)} %bitcast.348), custom_call_target="tpu_custom_call" | custom-call | flops 8053063680 | bytes 5898240 | tf_op jit(solution)/shard_map/pallas_call | solution.py:802
  375.2 2.3 convert_add_fusion
  382.6 13.6 %shard_map.430 = (f32[6400,768]{1,0:T(8,128)}, f32[8,128]{1,0:T(8,128)}) custom-call(s32[1]{0:T(128)} %bitcast.first_ref, bf16[2048,768]{1,0:T(8,128)(2,1)} %bitcast.280, bf16[6400,768]{1,0:T(8,128)(2,1)} %get-tuple-element.184.table_ref, s32[1,2048]{1,0:T(1,128)} %reshape.690.target_ref, f32[1,2048]{1,0:T(1,128)} %bitcast.349, ...), custom_call_target="tpu_custom_call", output_to_operand_aliasing={{0}: (5, {})} | custom-call | flops 8053063680 | bytes 5898240 | tf_op jit(solution)/shard_map/pallas_call | solution.py:802
  406.5 13.8 %shard_map.431 = (f32[6400,768]{1,0:T(8,128)}, f32[8,128]{1,0:T(8,128)}) custom-call(s32[1]{0:T(128)} %bitcast.first_ref, bf16[2048,768]{1,0:T(8,128)(2,1)} %bitcast.281, bf16[6400,768]{1,0:T(8,128)(2,1)} %get-tuple-element.184.table_ref, s32[1,2048]{1,0:T(1,128)} %reshape.690.target_ref, f32[1,2048]{1,0:T(1,128)} %bitcast.350, ...), custom_call_target="tpu_custom_call", output_to_operand_aliasing={{0}: (5, {})} | custom-call | flops 8053063680 | bytes 5898240 | tf_op jit(solution)/shard_map/pallas_call | solution.py:802
  426.2 13.5 %shard_map.432 = (f32[6400,768]{1,0:T(8,128)}, f32[8,128]{1,0:T(8,128)}) custom-call(s32[1]{0:T(128)} %bitcast.first_ref, bf16[2048,768]{1,0:T(8,128)(2,1)} %bitcast.282, bf16[6400,768]{1,0:T(8,128)(2,1)} %get-tuple-element.184.table_ref, s32[1,2048]{1,0:T(1,128)} %reshape.690.target_ref, f32[1,2048]{1,0:T(1,128)} %bitcast.351, ...), custom_call_target="tpu_custom_call", output_to_operand_aliasing={{0}: (5, {})} | custom-call | flops 8053063680 | bytes 5898240 | tf_op jit(solution)/shard_map/pallas_call | solution.py:802
  449.0 2.7 collective-permute-done.75
  456.6 13.5 %shard_map.433 = (f32[6400,768]{1,0:T(8,128)}, f32[8,128]{1,0:T(8,128)}) custom-call(s32[1]{0:T(128)} %bitcast.first_ref, bf16[2048,768]{1,0:T(8,128)(2,1)} %bitcast.283, bf16[6400,768]{1,0:T(8,128)(2,1)} %get-tuple-element.184.table_ref, s32[1,2048]{1,0:T(1,128)} %reshape.690.target_ref, f32[1,2048]{1,0:T(1,128)} %bitcast.352, ...), custom_call_target="tpu_custom_call", output_to_operand_aliasing={{0}: (5, {})} | custom-call | flops 8053063680 | bytes 5898240 | tf_op jit(solution)/shard_map/pallas_call | solution.py:802
  472.8 23.7 %shard_map.434 = (f32[6400,768]{1,0:T(8,128)}, f32[8,128]{1,0:T(8,128)}) custom-call(s32[3]{0:T(128)} %pad_add_fusion.1.here_ref, s32[32]{0:T(128)} %get-tuple-element.316.count_ref, s32[2048]{0:T(1024)} %reshape.687.row_ref, s32[2048]{0:T(1024)} %reshape.688.token_ref, f32[6400,768]{1,0:T(8,128)} %get-tuple-element.274.grad_in_ref, ...), custom_call_target="tpu_custom_call", output_to_operand_aliasing={{0}: (4, {})} | custom-call | flops 9830400 | bytes 39321600 | tf_op jit(solution)/shard_map/pallas_call | solution.py:911
  496.4 3.0 collective-permute-start.79
  516.0 14.1 %shard_map.435 = (f32[24,2304]{1,0:T(8,128)}, f32[24,2304]{1,0:T(8,128)}, f32[24,2304]{1,0:T(8,128)}, f32[24,768]{1,0:T(8,128)}, f32[24,768]{1,0:T(8,128)}, /*in...) custom-call(s32[1]{0:T(128)} %bitcast.34.here_ref, ...), custom_call_target="tpu_custom_call" | custom-call | flops 24330240 | bytes 19464192 | tf_op jit(solution)/shard_map/pallas_call | solution.py:995
  539.1 2.2 collective-permute-start.91
  548.0 54.8 %shard_map.436 = (f32[6288,768]{1,0:T(8,128)}, f32[6288,768]{1,0:T(8,128)}, f32[6288,768]{1,0:T(8,128)}, f32[24,2304]{1,0:T(8,128)}, f32[24,768]{1,0:T(8,128)}, ...) custom-call(f32[8,128]{1,0:T(8,128)} %add_add_fusion.5.sums_ref, ...), custom_call_target="tpu_custom_call" | custom-call | flops 96583680 | bytes 135217152 | tf_op jit(solution)/shard_map/pallas_call | solution.py:1043
  (401 shorter events, 207.8 us)
Async XLA Ops:
  5.9 11.9 %collective-permute-start.1 = (bf16[1,24,3328]{2,1,0:T(8,128)(2,1)S(1)}, bf16[1,24,3328]{2,1,0:T(8,128)(2,1)S(1)}, u32[]{:S(2)}, u32[]{:S(2)}) collective-permute-start(bf16[1,24,3328]{2,1,0:T(8,128)(2,1)S(1)} %get-tuple-element.349), channel_id=1, source_target_pairs={{0,4},{1,5},{2,6},{3,7},{4,0},{5,1},{6,2},{7,3},{8,12},{9,13},{10,... | collective-permute-start | bytes 479240 | tf_op jit(solution)/shard_map/ppermute | solution.py:444
  31.1 18.8 %collective-permute-start.6 = (bf16[4,24,3328]{2,1,0:T(8,128)(2,1)S(1)}, bf16[4,24,3328]{2,1,0:T(8,128)(2,1)S(1)}, u32[]{:S(2)}, u32[]{:S(2)}) collective-permute-start(bf16[4,24,3328]{2,1,0:T(8,128)(2,1)S(1)} %bitcast.319), channel_id=1, source_target_pairs={{0,8},{8,0},{16,24},{24,16},{1,9},{9,1},{17,25},{25,17},{2,10},{10... | collective-permute-start | bytes 1916936 | tf_op jit(solution)/shard_map/ppermute | solution.py:449
  32.7 17.3 %collective-permute-start.7 = (bf16[4,24,3328]{2,1,0:T(8,128)(2,1)S(1)}, bf16[4,24,3328]{2,1,0:T(8,128)(2,1)S(1)}, u32[]{:S(2)}, u32[]{:S(2)}) collective-permute-start(bf16[4,24,3328]{2,1,0:T(8,128)(2,1)S(1)} %bitcast.320), channel_id=1, source_target_pairs={{0,16},{8,24},{16,0},{24,8},{1,17},{9,25},{17,1},{25,9},{2,18},{10... | collective-permute-start | bytes 1916936 | tf_op jit(solution)/shard_map/ppermute | solution.py:449
  34.2 15.7 %collective-permute-start.8 = (bf16[1,24,3072]{2,1,0:T(8,128)(2,1)S(1)}, bf16[1,24,3072]{2,1,0:T(8,128)(2,1)S(1)}, u32[]{:S(2)}, u32[]{:S(2)}) collective-permute-start(bf16[1,24,3072]{2,1,0:T(8,128)(2,1)S(1)} %convert_bitcast_fusion.1), channel_id=1, source_target_pairs={{0,4},{1,5},{2,6},{3,7},{4,0},{5,1},{6,2},{7,3},{8,12},{9,13},{10,... | collective-permute-start | bytes 442376 | tf_op jit(solution)/shard_map/ppermute | solution.py:444
  60.3 18.9 %collective-permute-start.14 = (bf16[16,24,3328]{2,1,0:T(8,128)(2,1)}, bf16[16,24,3328]{2,1,0:T(8,128)(2,1)}, u32[]{:S(2)}, u32[]{:S(2)}) collective-permute-start(bf16[16,24,3328]{2,1,0:T(8,128)(2,1)} %constant_dynamic-update-slice_fusion.2.held_ref), channel_id=1, source_target_pairs={{0,1},{1,0},{2,3},{3,2},{4,5},{5,4},{6,7},{7,6},{8,9},{9,8},{10,11... | collective-permute-start | bytes 7667720 | tf_op jit(solution)/shard_map/ppermute | solution.py:439
  61.6 16.8 %collective-permute-start.12 = (bf16[4,24,3072]{2,1,0:T(8,128)(2,1)S(1)}, bf16[4,24,3072]{2,1,0:T(8,128)(2,1)S(1)}, u32[]{:S(2)}, u32[]{:S(2)}) collective-permute-start(bf16[4,24,3072]{2,1,0:T(8,128)(2,1)S(1)} %bitcast.324), channel_id=1, source_target_pairs={{0,8},{8,0},{16,24},{24,16},{1,9},{9,1},{17,25},{25,17},{2,10},{10... | collective-permute-start | bytes 1769480 | tf_op jit(solution)/shard_map/ppermute | solution.py:449
  62.9 15.5 %collective-permute-start.13 = (bf16[4,24,3072]{2,1,0:T(8,128)(2,1)S(1)}, bf16[4,24,3072]{2,1,0:T(8,128)(2,1)S(1)}, u32[]{:S(2)}, u32[]{:S(2)}) collective-permute-start(bf16[4,24,3072]{2,1,0:T(8,128)(2,1)S(1)} %bitcast.325), channel_id=1, source_target_pairs={{0,16},{8,24},{16,0},{24,8},{1,17},{9,25},{17,1},{25,9},{2,18},{10... | collective-permute-start | bytes 1769480 | tf_op jit(solution)/shard_map/ppermute | solution.py:449
  63.4 12.8 %collective-permute-start.15 = (bf16[1,96,768]{2,1,0:T(8,128)(2,1)}, bf16[1,96,768]{2,1,0:T(8,128)(2,1)S(1)}, u32[]{:S(2)}, u32[]{:S(2)}) collective-permute-start(bf16[1,96,768]{2,1,0:T(8,128)(2,1)} %convert_bitcast_fusion), channel_id=1, source_target_pairs={{0,4},{1,5},{2,6},{3,7},{4,0},{5,1},{6,2},{7,3},{8,12},{9,13},{10,... | collective-permute-start | bytes 442376 | tf_op jit(solution)/shard_map/ppermute | solution.py:444
  79.3 9.2 %collective-permute-start.19 = (bf16[2,96,768]{2,1,0:T(8,128)(2,1)S(1)}, bf16[2,96,768]{2,1,0:T(8,128)(2,1)S(1)}, u32[]{:S(2)}, u32[]{:S(2)}) collective-permute-start(bf16[2,96,768]{2,1,0:T(8,128)(2,1)S(1)} %maximum_bitcast_fusion.3), channel_id=1, source_target_pairs={{0,2},{1,3},{2,0},{3,1},{4,6},{5,7},{6,4},{7,5},{8,10},{9,11},{10,... | collective-permute-start | bytes 884744 | tf_op jit(solution)/shard_map/ppermute | solution.py:444
  79.6 9.8 %collective-permute-start.17 = (bf16[2,24,3072]{2,1,0:T(8,128)(2,1)S(1)}, bf16[2,24,3072]{2,1,0:T(8,128)(2,1)S(1)}, u32[]{:S(2)}, u32[]{:S(2)}) collective-permute-start(bf16[2,24,3072]{2,1,0:T(8,128)(2,1)S(1)} %slice.312), channel_id=1, source_target_pairs={{0,8},{8,0},{16,24},{24,16},{1,9},{9,1},{17,25},{25,17},{2,10},{10... | collective-permute-start | bytes 884744 | tf_op jit(solution)/shard_map/ppermute | solution.py:449
  81.9 9.0 %collective-permute-start.16 = (bf16[4,128,768]{2,1,0:T(8,128)(2,1)S(1)}, bf16[4,128,768]{2,1,0:T(8,128)(2,1)S(1)}, u32[]{:S(2)}, u32[]{:S(2)}) collective-permute-start(bf16[4,128,768]{2,1,0:T(8,128)(2,1)S(1)} %dynamic-slice_bitcast_fusion.3), channel_id=1, source_target_pairs={{0,1},{1,0},{2,3},{3,2},{4,5},{5,4},{6,7},{7,6},{8,9},{9,8},{10,11... | collective-permute-start | bytes 2359304 | tf_op jit(solution)/shard_map/ppermute | solution.py:439
  91.0 23.9 %collective-permute-start.24 = (bf16[16,24,3072]{2,1,0:T(8,128)(2,1)}, bf16[16,24,3072]{2,1,0:T(8,128)(2,1)}, u32[]{:S(2)}, u32[]{:S(2)}) collective-permute-start(bf16[16,24,3072]{2,1,0:T(8,128)(2,1)} %constant_dynamic-update-slice_fusion.7.held_ref), channel_id=1, source_target_pairs={{0,1},{1,0},{2,3},{3,2},{4,5},{5,4},{6,7},{7,6},{8,9},{9,8},{10,11... | collective-permute-start | bytes 7077896 | tf_op jit(solution)/shard_map/ppermute | solution.py:439
  91.6 11.1 %collective-permute-start.20 = (bf16[2,128,768]{2,1,0:T(8,128)(2,1)S(1)}, bf16[2,128,768]{2,1,0:T(8,128)(2,1)S(1)}, u32[]{:S(2)}, u32[]{:S(2)}) collective-permute-start(bf16[2,128,768]{2,1,0:T(8,128)(2,1)S(1)} %fusion.17), channel_id=1, source_target_pairs={{0,2},{1,3},{2,0},{3,1},{4,6},{5,7},{6,4},{7,5},{8,10},{9,11},{10,... | collective-permute-start | bytes 1179656 | tf_op jit(solution)/shard_map/ppermute | solution.py:444
  93.3 17.4 %collective-permute-start.22 = (bf16[4,96,768]{2,1,0:T(8,128)(2,1)}, bf16[4,96,768]{2,1,0:T(8,128)(2,1)}, u32[]{:S(2)}, u32[]{:S(2)}) collective-permute-start(bf16[4,96,768]{2,1,0:T(8,128)(2,1)} %bitcast.33), channel_id=1, source_target_pairs={{0,8},{8,0},{16,24},{24,16},{1,9},{9,1},{17,25},{25,17},{2,10},{10... | collective-permute-start | bytes 1769480 | tf_op jit(solution)/shard_map/ppermute | solution.py:449
  94.7 15.0 %collective-permute-start.23 = (bf16[4,96,768]{2,1,0:T(8,128)(2,1)}, bf16[4,96,768]{2,1,0:T(8,128)(2,1)}, u32[]{:S(2)}, u32[]{:S(2)}) collective-permute-start(bf16[4,96,768]{2,1,0:T(8,128)(2,1)} %bitcast.33), channel_id=1, source_target_pairs={{0,16},{8,24},{16,0},{24,8},{1,17},{9,25},{17,1},{25,9},{2,18},{10... | collective-permute-start | bytes 1769480 | tf_op jit(solution)/shard_map/ppermute | solution.py:449
  102.9 11.3 %collective-permute-start.21 = (bf16[1,128,768]{2,1,0:T(8,128)(2,1)S(1)}, bf16[1,128,768]{2,1,0:T(8,128)(2,1)S(1)}, u32[]{:S(2)}, u32[]{:S(2)}) collective-permute-start(bf16[1,128,768]{2,1,0:T(8,128)(2,1)S(1)} %dynamic-slice_convert_fusion.10), channel_id=1, source_target_pairs={{0,4},{1,5},{2,6},{3,7},{4,0},{5,1},{6,2},{7,3},{8,12},{9,13},{10,... | collective-permute-start | bytes 589832 | tf_op jit(solution)/shard_map/ppermute | solution.py:444
  115.0 18.7 %collective-permute-start.25 = (bf16[2,96,768]{2,1,0:T(8,128)(2,1)S(1)}, bf16[2,96,768]{2,1,0:T(8,128)(2,1)S(1)}, u32[]{:S(2)}, u32[]{:S(2)}) collective-permute-start(bf16[2,96,768]{2,1,0:T(8,128)(2,1)S(1)} %slice.316), channel_id=1, source_target_pairs={{0,8},{8,0},{16,24},{24,16},{1,9},{9,1},{17,25},{25,17},{2,10},{10... | collective-permute-start | bytes 884744 | tf_op jit(solution)/shard_map/ppermute | solution.py:449
  117.4 16.3 %collective-permute-start.26 = (bf16[2,96,768]{2,1,0:T(8,128)(2,1)S(1)}, bf16[2,96,768]{2,1,0:T(8,128)(2,1)S(1)}, u32[]{:S(2)}, u32[]{:S(2)}) collective-permute-start(bf16[2,96,768]{2,1,0:T(8,128)(2,1)S(1)} %slice.317), channel_id=1, source_target_pairs={{0,16},{8,24},{16,0},{24,8},{1,17},{9,25},{17,1},{25,9},{2,18},{10... | collective-permute-start | bytes 884744 | tf_op jit(solution)/shard_map/ppermute | solution.py:449
  212.7 10.7 %collective-permute-start.49 = (bf16[64,768]{1,0:T(8,128)(2,1)S(1)}, bf16[64,768]{1,0:T(8,128)(2,1)S(1)}, u32[]{:S(2)}, u32[]{:S(2)}) collective-permute-start(bf16[64,768]{1,0:T(8,128)(2,1)S(1)} %get-tuple-element.335), channel_id=1, source_target_pairs={{0,4},{1,5},{2,6},{3,7},{4,0},{5,1},{6,2},{7,3},{8,12},{9,13},{10,... | collective-permute-start | bytes 294920 | tf_op jit(solution)/shard_map/ppermute | solution.py:444
  214.1 9.3 %collective-permute-start.50 = (bf16[64,768]{1,0:T(8,128)(2,1)S(1)}, bf16[64,768]{1,0:T(8,128)(2,1)S(1)}, u32[]{:S(2)}, u32[]{:S(2)}) collective-permute-start(bf16[64,768]{1,0:T(8,128)(2,1)S(1)} %get-tuple-element.334), channel_id=1, source_target_pairs={{0,6},{1,7},{2,4},{3,5},{4,2},{5,3},{6,0},{7,1},{8,14},{9,15},{10,... | collective-permute-start | bytes 294920 | tf_op jit(solution)/shard_map/ppermute | solution.py:444
  231.1 27.2 %collective-permute-start.51 = (bf16[16,96,768]{2,1,0:T(8,128)(2,1)}, bf16[16,96,768]{2,1,0:T(8,128)(2,1)S(1)}, u32[]{:S(2)}, u32[]{:S(2)}) collective-permute-start(bf16[16,96,768]{2,1,0:T(8,128)(2,1)} %bitcast.369), channel_id=1, source_target_pairs={{0,1},{1,0},{2,3},{3,2},{4,5},{5,4},{6,7},{7,6},{8,9},{9,8},{10,11... | collective-permute-start | bytes 7077896 | tf_op jit(solution)/shard_map/ppermute | solution.py:439
  234.3 12.8 %collective-permute-start.43 = (bf16[4,64,768]{2,1,0:T(8,128)(2,1)}, bf16[4,64,768]{2,1,0:T(8,128)(2,1)S(1)}, u32[]{:S(2)}, u32[]{:S(2)}) collective-permute-start(bf16[4,64,768]{2,1,0:T(8,128)(2,1)} %pad_maximum_fusion.12), channel_id=1, source_target_pairs={{0,16},{8,24},{16,0},{24,8},{1,17},{9,25},{17,1},{25,9},{2,18},{10... | collective-permute-start | bytes 1179656 | tf_op jit(solution)/shard_map/ppermute | solution.py:449
  236.5 9.9 %collective-permute-start.40 = (s32[8,192]{1,0:T(8,128)S(1)}, s32[8,192]{1,0:T(8,128)S(1)}, u32[]{:S(2)}, u32[]{:S(2)}) collective-permute-start(s32[8,192]{1,0:T(8,128)S(1)} %add_bitcast_fusion.5), channel_id=1, source_target_pairs={{0,16},{8,24},{16,0},{24,8},{1,17},{9,25},{17,1},{25,9},{2,18},{10... | collective-permute-start | bytes 18440 | tf_op jit(solution)/shard_map/ppermute | solution.py:449
  237.1 9.3 %collective-permute-start.41 = (s32[8,192]{1,0:T(8,128)S(1)}, s32[8,192]{1,0:T(8,128)S(1)}, u32[]{:S(2)}, u32[]{:S(2)}) collective-permute-start(s32[8,192]{1,0:T(8,128)S(1)} %add_bitcast_fusion.5), channel_id=1, source_target_pairs={{0,8},{8,0},{16,24},{24,16},{1,9},{9,1},{17,25},{25,17},{2,10},{10... | collective-permute-start | bytes 18440 | tf_op jit(solution)/shard_map/ppermute | solution.py:449
  240.3 23.2 %collective-permute-start.42 = (bf16[4,64,768]{2,1,0:T(8,128)(2,1)}, bf16[4,64,768]{2,1,0:T(8,128)(2,1)S(1)}, u32[]{:S(2)}, u32[]{:S(2)}) collective-permute-start(bf16[4,64,768]{2,1,0:T(8,128)(2,1)} %pad_maximum_fusion.12), channel_id=1, source_target_pairs={{0,8},{8,0},{16,24},{24,16},{1,9},{9,1},{17,25},{25,17},{2,10},{10... | collective-permute-start | bytes 1179656 | tf_op jit(solution)/shard_map/ppermute | solution.py:449
  247.8 23.2 %collective-permute-start.44 = (bf16[2,64,768]{2,1,0:T(8,128)(2,1)}, bf16[2,64,768]{2,1,0:T(8,128)(2,1)S(1)}, u32[]{:S(2)}, u32[]{:S(2)}) collective-permute-start(bf16[2,64,768]{2,1,0:T(8,128)(2,1)} %slice.321), channel_id=1, source_target_pairs={{0,8},{8,0},{16,24},{24,16},{1,9},{9,1},{17,25},{25,17},{2,10},{10... | collective-permute-start | bytes 589832 | tf_op jit(solution)/shard_map/ppermute | solution.py:449
  263.4 28.1 %collective-permute-start.54 = (bf16[16,24,3072]{2,1,0:T(8,128)(2,1)}, bf16[16,24,3072]{2,1,0:T(8,128)(2,1)}, u32[]{:S(2)}, u32[]{:S(2)}) collective-permute-start(bf16[16,24,3072]{2,1,0:T(8,128)(2,1)} %bitcast.88), channel_id=1, source_target_pairs={{0,1},{1,0},{2,3},{3,2},{4,5},{5,4},{6,7},{7,6},{8,9},{9,8},{10,11... | collective-permute-start | bytes 7077896 | tf_op jit(solution)/shard_map/ppermute | solution.py:439
  276.3 69.3 %collective-permute-start.46 = (bf16[16,64,768]{2,1,0:T(8,128)(2,1)}, bf16[16,64,768]{2,1,0:T(8,128)(2,1)}, u32[]{:S(2)}, u32[]{:S(2)}) collective-permute-start(bf16[16,64,768]{2,1,0:T(8,128)(2,1)} %constant_dynamic-update-slice_fusion.17.held_ref), channel_id=1, source_target_pairs={{0,1},{1,0},{2,3},{3,2},{4,5},{5,4},{6,7},{7,6},{8,9},{9,8},{10,11... | collective-permute-start | bytes 4718600 | tf_op jit(solution)/shard_map/ppermute | solution.py:439
  277.9 11.6 %collective-permute-start.52 = (bf16[2,96,768]{2,1,0:T(8,128)(2,1)S(1)}, bf16[2,96,768]{2,1,0:T(8,128)(2,1)S(1)}, u32[]{:S(2)}, u32[]{:S(2)}) collective-permute-start(bf16[2,96,768]{2,1,0:T(8,128)(2,1)S(1)} %get-tuple-element.343), channel_id=1, source_target_pairs={{0,16},{8,24},{16,0},{24,8},{1,17},{9,25},{17,1},{25,9},{2,18},{10... | collective-permute-start | bytes 884744 | tf_op jit(solution)/shard_map/ppermute | solution.py:449
  278.6 10.9 %collective-permute-start.53 = (bf16[2,96,768]{2,1,0:T(8,128)(2,1)S(1)}, bf16[2,96,768]{2,1,0:T(8,128)(2,1)S(1)}, u32[]{:S(2)}, u32[]{:S(2)}) collective-permute-start(bf16[2,96,768]{2,1,0:T(8,128)(2,1)S(1)} %get-tuple-element.342), channel_id=1, source_target_pairs={{0,8},{8,0},{16,24},{24,16},{1,9},{9,1},{17,25},{25,17},{2,10},{10... | collective-permute-start | bytes 884744 | tf_op jit(solution)/shard_map/ppermute | solution.py:449
  314.7 15.5 %collective-permute-start.55 = (bf16[4,96,768]{2,1,0:T(8,128)(2,1)}, bf16[4,96,768]{2,1,0:T(8,128)(2,1)S(1)}, u32[]{:S(2)}, u32[]{:S(2)}) collective-permute-start(bf16[4,96,768]{2,1,0:T(8,128)(2,1)} %pad_maximum_fusion.7), channel_id=1, source_target_pairs={{0,8},{8,0},{16,24},{24,16},{1,9},{9,1},{17,25},{25,17},{2,10},{10... | collective-permute-start | bytes 1769480 | tf_op jit(solution)/shard_map/ppermute | solution.py:449
  315.5 15.1 %collective-permute-start.56 = (bf16[4,96,768]{2,1,0:T(8,128)(2,1)}, bf16[4,96,768]{2,1,0:T(8,128)(2,1)S(1)}, u32[]{:S(2)}, u32[]{:S(2)}) collective-permute-start(bf16[4,96,768]{2,1,0:T(8,128)(2,1)} %pad_maximum_fusion.8), channel_id=1, source_target_pairs={{0,16},{8,24},{16,0},{24,8},{1,17},{9,25},{17,1},{25,9},{2,18},{10... | collective-permute-start | bytes 1769480 | tf_op jit(solution)/shard_map/ppermute | solution.py:449
  344.3 30.8 %collective-permute-start.63 = (bf16[16,24,3328]{2,1,0:T(8,128)(2,1)}, bf16[16,24,3328]{2,1,0:T(8,128)(2,1)}, u32[]{:S(2)}, u32[]{:S(2)}) collective-permute-start(bf16[16,24,3328]{2,1,0:T(8,128)(2,1)} %fusion.29), channel_id=1, source_target_pairs={{0,1},{1,0},{2,3},{3,2},{4,5},{5,4},{6,7},{7,6},{8,9},{9,8},{10,11... | collective-permute-start | bytes 7667720 | tf_op jit(solution)/shard_map/ppermute | solution.py:439
  351.8 18.3 %collective-permute-start.64 = (bf16[1,96,768]{2,1,0:T(8,128)(2,1)}, bf16[1,96,768]{2,1,0:T(8,128)(2,1)}, u32[]{:S(2)}, u32[]{:S(2)}) collective-permute-start(bf16[1,96,768]{2,1,0:T(8,128)(2,1)} %dynamic-slice_convert_fusion.13), channel_id=1, source_target_pairs={{0,4},{1,5},{2,6},{3,7},{4,0},{5,1},{6,2},{7,3},{8,12},{9,13},{10,... | collective-permute-start | bytes 442376 | tf_op jit(solution)/shard_map/ppermute | solution.py:444
  352.9 20.0 %collective-permute-start.61 = (bf16[4,24,3072]{2,1,0:T(8,128)(2,1)}, bf16[4,24,3072]{2,1,0:T(8,128)(2,1)S(1)}, u32[]{:S(2)}, u32[]{:S(2)}) collective-permute-start(bf16[4,24,3072]{2,1,0:T(8,128)(2,1)} %pad_maximum_fusion.9), channel_id=1, source_target_pairs={{0,8},{8,0},{16,24},{24,16},{1,9},{9,1},{17,25},{25,17},{2,10},{10... | collective-permute-start | bytes 1769480 | tf_op jit(solution)/shard_map/ppermute | solution.py:449
  354.2 18.7 %collective-permute-start.62 = (bf16[4,24,3072]{2,1,0:T(8,128)(2,1)}, bf16[4,24,3072]{2,1,0:T(8,128)(2,1)}, u32[]{:S(2)}, u32[]{:S(2)}) collective-permute-start(bf16[4,24,3072]{2,1,0:T(8,128)(2,1)} %pad_maximum_fusion.10), channel_id=1, source_target_pairs={{0,16},{8,24},{16,0},{24,8},{1,17},{9,25},{17,1},{25,9},{2,18},{10... | collective-permute-start | bytes 1769480 | tf_op jit(solution)/shard_map/ppermute | solution.py:449
  355.2 16.8 %collective-permute-start.60 = (bf16[1,128,768]{2,1,0:T(8,128)(2,1)}, bf16[1,128,768]{2,1,0:T(8,128)(2,1)}, u32[]{:S(2)}, u32[]{:S(2)}) collective-permute-start(bf16[1,128,768]{2,1,0:T(8,128)(2,1)} %bitcast.353), channel_id=1, source_target_pairs={{0,4},{1,5},{2,6},{3,7},{4,0},{5,1},{6,2},{7,3},{8,12},{9,13},{10,... | collective-permute-start | bytes 589832 | tf_op jit(solution)/shard_map/ppermute | solution.py:444
  377.6 18.7 %collective-permute-start.68 = (bf16[2,24,3072]{2,1,0:T(8,128)(2,1)S(1)}, bf16[2,24,3072]{2,1,0:T(8,128)(2,1)}, u32[]{:S(2)}, u32[]{:S(2)}) collective-permute-start(bf16[2,24,3072]{2,1,0:T(8,128)(2,1)S(1)} %fusion.23), channel_id=1, source_target_pairs={{0,2},{1,3},{2,0},{3,1},{4,6},{5,7},{6,4},{7,5},{8,10},{9,11},{10,... | collective-permute-start | bytes 884744 | tf_op jit(solution)/shard_map/ppermute | solution.py:444
  378.8 19.3 %collective-permute-start.66 = (bf16[2,24,3328]{2,1,0:T(8,128)(2,1)}, bf16[2,24,3328]{2,1,0:T(8,128)(2,1)}, u32[]{:S(2)}, u32[]{:S(2)}) collective-permute-start(bf16[2,24,3328]{2,1,0:T(8,128)(2,1)} %get-tuple-element.339), channel_id=1, source_target_pairs={{0,16},{8,24},{16,0},{24,8},{1,17},{9,25},{17,1},{25,9},{2,18},{10... | collective-permute-start | bytes 958472 | tf_op jit(solution)/shard_map/ppermute | solution.py:449
  380.2 17.9 %collective-permute-start.67 = (bf16[2,24,3328]{2,1,0:T(8,128)(2,1)}, bf16[2,24,3328]{2,1,0:T(8,128)(2,1)}, u32[]{:S(2)}, u32[]{:S(2)}) collective-permute-start(bf16[2,24,3328]{2,1,0:T(8,128)(2,1)} %get-tuple-element.338), channel_id=1, source_target_pairs={{0,8},{8,0},{16,24},{24,16},{1,9},{9,1},{17,25},{25,17},{2,10},{10... | collective-permute-start | bytes 958472 | tf_op jit(solution)/shard_map/ppermute | solution.py:449
  380.9 20.2 %collective-permute-start.65 = (bf16[2,128,768]{2,1,0:T(8,128)(2,1)S(1)}, bf16[2,128,768]{2,1,0:T(8,128)(2,1)}, u32[]{:S(2)}, u32[]{:S(2)}) collective-permute-start(bf16[2,128,768]{2,1,0:T(8,128)(2,1)S(1)} %maximum_bitcast_fusion), channel_id=1, source_target_pairs={{0,2},{1,3},{2,0},{3,1},{4,6},{5,7},{6,4},{7,5},{8,10},{9,11},{10,... | collective-permute-start | bytes 1179656 | tf_op jit(solution)/shard_map/ppermute | solution.py:444
  403.1 17.9 %collective-permute-start.69 = (bf16[4,24,3328]{2,1,0:T(8,128)(2,1)}, bf16[4,24,3328]{2,1,0:T(8,128)(2,1)}, u32[]{:S(2)}, u32[]{:S(2)}) collective-permute-start(bf16[4,24,3328]{2,1,0:T(8,128)(2,1)} %pad_maximum_fusion.3), channel_id=1, source_target_pairs={{0,8},{8,0},{16,24},{24,16},{1,9},{9,1},{17,25},{25,17},{2,10},{10... | collective-permute-start | bytes 1916936 | tf_op jit(solution)/shard_map/ppermute | solution.py:449
  404.4 16.7 %collective-permute-start.70 = (bf16[4,24,3328]{2,1,0:T(8,128)(2,1)}, bf16[4,24,3328]{2,1,0:T(8,128)(2,1)}, u32[]{:S(2)}, u32[]{:S(2)}) collective-permute-start(bf16[4,24,3328]{2,1,0:T(8,128)(2,1)} %pad_maximum_fusion.4), channel_id=1, source_target_pairs={{0,16},{8,24},{16,0},{24,8},{1,17},{9,25},{17,1},{25,9},{2,18},{10... | collective-permute-start | bytes 1916936 | tf_op jit(solution)/shard_map/ppermute | solution.py:449
  405.2 15.1 %collective-permute-start.71 = (bf16[1,24,3072]{2,1,0:T(8,128)(2,1)}, bf16[1,24,3072]{2,1,0:T(8,128)(2,1)S(1)}, u32[]{:S(2)}, u32[]{:S(2)}) collective-permute-start(bf16[1,24,3072]{2,1,0:T(8,128)(2,1)} %dynamic-slice_convert_fusion.12), channel_id=1, source_target_pairs={{0,4},{1,5},{2,6},{3,7},{4,0},{5,1},{6,2},{7,3},{8,12},{9,13},{10,... | collective-permute-start | bytes 442376 | tf_op jit(solution)/shard_map/ppermute | solution.py:444
  422.5 18.5 %collective-permute-start.72 = (bf16[4,128,768]{2,1,0:T(8,128)(2,1)}, bf16[4,128,768]{2,1,0:T(8,128)(2,1)}, u32[]{:S(2)}, u32[]{:S(2)}) collective-permute-start(bf16[4,128,768]{2,1,0:T(8,128)(2,1)} %bitcast.112), channel_id=1, source_target_pairs={{0,8},{8,0},{16,24},{24,16},{1,9},{9,1},{17,25},{25,17},{2,10},{10... | collective-permute-start | bytes 2359304 | tf_op jit(solution)/shard_map/ppermute | solution.py:449
  423.3 17.7 %collective-permute-start.73 = (bf16[4,128,768]{2,1,0:T(8,128)(2,1)}, bf16[4,128,768]{2,1,0:T(8,128)(2,1)}, u32[]{:S(2)}, u32[]{:S(2)}) collective-permute-start(bf16[4,128,768]{2,1,0:T(8,128)(2,1)} %bitcast.112), channel_id=1, source_target_pairs={{0,16},{8,24},{16,0},{24,8},{1,17},{9,25},{17,1},{25,9},{2,18},{10... | collective-permute-start | bytes 2359304 | tf_op jit(solution)/shard_map/ppermute | solution.py:449
  424.5 16.5 %collective-permute-start.74 = (bf16[2,24,3328]{2,1,0:T(8,128)(2,1)S(1)}, bf16[2,24,3328]{2,1,0:T(8,128)(2,1)S(1)}, u32[]{:S(2)}, u32[]{:S(2)}) collective-permute-start(bf16[2,24,3328]{2,1,0:T(8,128)(2,1)S(1)} %fusion.19), channel_id=1, source_target_pairs={{0,2},{1,3},{2,0},{3,1},{4,6},{5,7},{6,4},{7,5},{8,10},{9,11},{10,... | collective-permute-start | bytes 958472 | tf_op jit(solution)/shard_map/ppermute | solution.py:444
  453.1 19.7 %collective-permute-start.78 = (bf16[16,128,768]{2,1,0:T(8,128)(2,1)S(1)}, bf16[16,128,768]{2,1,0:T(8,128)(2,1)}, u32[]{:S(2)}, u32[]{:S(2)}) collective-permute-start(bf16[16,128,768]{2,1,0:T(8,128)(2,1)S(1)} %constant_dynamic-update-slice_fusion.25.held_ref), channel_id=1, source_target_pairs={{0,1},{1,0},{2,3},{3,2},{4,5},{5,4},{6,7},{7,6},{8,9},{9,8},{10,11... | collective-permute-start | bytes 9437192 | tf_op jit(solution)/shard_map/ppermute | solution.py:439
  (63 other events, 456.4 us)

commit v3 on v2

v3 whole, which is shorter than its diff:
```python
import functools
import math

import jax
import jax.numpy as jnp
from jax import lax
from jax.experimental import pallas as pl
from jax.experimental.pallas import tpu as pltpu
from jax.sharding import PartitionSpec as P

HD = 64
V_REAL = 50257
STEP = 5


LN_EPS = 1e-05
SMOOTHING = 0.1
BETA_ONE = 0.9
BETA_TWO = 0.999
ADAM_EPS = 1e-12
DECAY = 0.01
RATE = 0.3
CLIP_AT = 0.01
MASKED = -1e30
CHUNK = 1280
PIECE = 640
VMEM_BYTES = 58 * 2**20


def layer_norm(inputs, gain, shift):
    centre = jnp.mean(inputs, axis=-1, keepdims=True)
    centred = inputs - centre
    spread = jnp.mean(centred * centred, axis=-1, keepdims=True)
    return centred * lax.rsqrt(spread + LN_EPS) * gain + shift


def gelu_tanh(inputs):
    return (
        0.5
        * inputs
        * (1.0 + jnp.tanh(0.7978845608028654 * (inputs + 0.044715 * inputs * inputs * inputs)))
    )


def dot_plain(left_op, right_op):
    return jnp.dot(left_op, right_op, preferred_element_type=jnp.float32)


def dot_first(left_op, right_op):
    return lax.dot_general(
        left_op, right_op, (((0,), (0,)), ((), ())), preferred_element_type=jnp.float32
    )


def dot_second(left_op, right_op):
    return lax.dot_general(
        left_op, right_op, (((1,), (1,)), ((), ())), preferred_element_type=jnp.float32
    )


def params():
    return pltpu.CompilerParams(vmem_limit_bytes=VMEM_BYTES)


def cost(flops, bytes_accessed):
    return pl.CostEstimate(
        flops=int(flops), bytes_accessed=int(bytes_accessed), transcendentals=0
    )


def whole_block():
    return pl.BlockSpec(memory_space=pltpu.VMEM)


def shape_of(shape, dtype):
    return jax.ShapeDtypeStruct(tuple(shape), dtype)


def causal_scores(queries, keys, causal):
    return jnp.where(causal, dot_second(queries, keys) * HD ** (-0.5), MASKED)


def causal_mask(count):
    query = lax.broadcasted_iota(jnp.int32, (count, count), 0)
    key = lax.broadcasted_iota(jnp.int32, (count, count), 1)
    return key <= query


def head_span(head):
    return slice(head * HD, (head + 1) * HD)


def attention_forward(embedded, positions, vec_rows, w_qkv, w_proj, chooser):
    count, width = embedded.shape
    low = jnp.bfloat16

    half = width // 2

    def body(
        e_ref, p_ref, v_ref, qkv_ref, proj_ref, c_ref, x0_ref, packed_ref, x1_ref, h2_ref, own_ref, other_ref, o_ref
    ):
        x0 = e_ref[...] + p_ref[...].astype(jnp.float32)
        x0_ref[...] = x0
        h1 = layer_norm(x0, v_ref[0:1, :], v_ref[1:2, :]).astype(low)
        parts = []
        for place, bias in enumerate((6, None, 7)):
            span = slice(place * width, (place + 1) * width)
            part = dot_plain(h1, qkv_ref[:, span])
            if bias is not None:
                part = part + v_ref[bias : bias + 1, :]
            parts.append(part.astype(low))
            packed_ref[:, span] = parts[-1]
        queries, keys, values = parts
        causal = causal_mask(count)
        for head in range(0, width // HD, 2):
            mixed = []
            for one in (head, head + 1):
                span = head_span(one)
                scores = causal_scores(queries[:, span], keys[:, span], causal)
                grown = jnp.exp(scores - jnp.max(scores, axis=-1, keepdims=True))
                probs = (grown / jnp.sum(grown, axis=-1, keepdims=True)).astype(low)
                mixed.append(dot_plain(probs, values[:, span]))
            o_ref[:, head * HD : (head + 2) * HD] = jnp.concatenate(mixed, axis=1).astype(low)
        x1 = x0 + dot_plain(o_ref[...], proj_ref[...]) + v_ref[8:9, :]
        x1_ref[...] = x1
        h2 = layer_norm(x1, v_ref[2:3, :], v_ref[3:4, :]).astype(low)
        h2_ref[...] = h2
        for place, value in enumerate((h1, o_ref[...], h2)):
            span = slice(place * half, (place + 1) * half)
            own_ref[:, span] = dot_plain(value, c_ref[0]).astype(low)
            other_ref[:, span] = dot_plain(value, c_ref[1]).astype(low)

    shape = (count, width)
    return pl.pallas_call(
        body,
        out_shape=[
            shape_of(shape, jnp.float32),
            shape_of((count, 3 * width), low),
            shape_of(shape, jnp.float32),
            shape_of(shape, low),
            shape_of((count, 3 * half), low),
            shape_of((count, 3 * half), low),
        ],
        in_specs=[whole_block()] * 6,
        out_specs=[whole_block()] * 6,
        scratch_shapes=[pltpu.VMEM(shape, low)],
        compiler_params=params(),
        cost_estimate=cost(20 * count * width * width, 8 * width * width),
    )(embedded, positions, vec_rows, w_qkv, w_proj, chooser)


def hidden_forward(normed, vec_rows, w_up, chooser, dp_index):
    count, width = normed.shape
    blocks = len(w_up)
    hidden = blocks * width
    half = width // 2
    low = jnp.bfloat16

    def body(dp_ref, h_ref, v_ref, c_ref, *refs):
        w_refs = refs[:blocks]
        pre_ref, act_ref, own_ref, other_ref = refs[blocks:]
        for place in range(blocks):
            span = slice(place * width, (place + 1) * width)
            pre = dot_plain(h_ref[...], w_refs[place][...]) + v_ref[10 + place : 11 + place, :]
            pre_ref[:, span] = pre
            act_ref[:, span] = gelu_tanh(pre).astype(low)
        for place in range(blocks):
            source = pl.multiple_of((dp_ref[0] ^ place) * width, width)
            part = act_ref[:, pl.ds(source, width)]
            span = slice(place * half, (place + 1) * half)
            own_ref[:, span] = dot_plain(part, c_ref[0]).astype(low)
            other_ref[:, span] = dot_plain(part, c_ref[1]).astype(low)

    return pl.pallas_call(
        body,
        out_shape=[
            shape_of((count, hidden), jnp.float32),
            shape_of((count, hidden), low),
            shape_of((count, hidden // 2), low),
            shape_of((count, hidden // 2), low),
        ],
        in_specs=[pl.BlockSpec(memory_space=pltpu.SMEM)] + [whole_block()] * (3 + blocks),
        out_specs=[whole_block()] * 4,
        compiler_params=params(),
        cost_estimate=cost(3 * count * width * hidden, 2 * width * hidden),
    )(dp_index, normed, vec_rows, chooser, *w_up)


def output_forward(act, w_down, resid_mid, vec_rows, picks):
    count, width = resid_mid.shape
    number = picks.shape[0]

    def body(act_ref, w_ref, x1_ref, v_ref, pick_ref, x2_ref, out_ref):
        x2 = x1_ref[...] + dot_plain(act_ref[...], w_ref[...]) + v_ref[9:10, :]
        x2_ref[...] = x2
        final = layer_norm(x2, v_ref[4:5, :], v_ref[5:6, :]).astype(jnp.bfloat16)
        hot = pick_ref[...] == lax.broadcasted_iota(jnp.int32, (number, count), 1)
        hot = jnp.where(hot, 1.0, 0.0).astype(jnp.bfloat16)
        out_ref[...] = dot_plain(hot, final).astype(jnp.bfloat16)

    return pl.pallas_call(
        body,
        out_shape=[
            shape_of((count, width), jnp.float32),
            shape_of((number, width), jnp.bfloat16),
        ],
        in_specs=[whole_block()] * 5,
        out_specs=[whole_block()] * 2,
        compiler_params=params(),
        cost_estimate=cost(2 * act.size * width, 2 * w_down.size),
    )(act, w_down, resid_mid, vec_rows, picks)


def norm_backward(grad, inputs, gain):
    centred = inputs - jnp.mean(inputs, axis=-1, keepdims=True)
    scale = lax.rsqrt(jnp.mean(centred * centred, axis=-1, keepdims=True) + LN_EPS)
    normed = centred * scale
    scaled = grad * gain
    back = scale * (
        scaled
        - jnp.mean(scaled, axis=-1, keepdims=True)
        - normed * jnp.mean(scaled * normed, axis=-1, keepdims=True)
    )
    return (
        back,
        jnp.sum(grad * normed, axis=0, keepdims=True),
        jnp.sum(grad, axis=0, keepdims=True),
    )


def column_sum(value):
    return jnp.sum(value.astype(jnp.float32), axis=0, keepdims=True)


def choosers(width, rows, core, dp_index=None):
    column = jnp.arange(width, dtype=jnp.int32)
    target = jnp.arange(width // 2, dtype=jnp.int32)
    block = target // rows
    if dp_index is not None:
        per = width // (8 * rows)
        block = ((block // per) ^ dp_index) * per + block % per
    made = []
    for side in (core, 1 - core):
        source = (block * 2 + side) * rows + target % rows
        made.append((column[:, None] == source[None, :]).astype(jnp.bfloat16))
    return jnp.stack(made)


def gradient_blocks(lefts, spans, rights, smalls, name_rows):
    widths = [right[0].shape[1] for right in rights]
    total = sum(widths) + (smalls.shape[2] if smalls is not None else 0)
    arrays = [value for pair in zip(lefts, rights) for group in pair for value in group]
    if smalls is not None:
        arrays.append(smalls)
    number = len(lefts)
    rows = (spans[0][1] - spans[0][0]) // 4
    half = rows // 2
    low = jnp.bfloat16

    def body(*refs):
        in_refs, out_refs = refs[: len(arrays)], refs[len(arrays) :]

        def put(made, span):
            own, one, two, three = [made(place) for place in range(4)]
            out_refs[0][:, span] = own
            out_refs[1][:, span] = one.astype(low)
            out_refs[2][:, span] = two.astype(low)
            out_refs[3][:, span] = one[half:]
            out_refs[4][:, span] = two[:half]
            out_refs[5][:, span] = three[:half].astype(low)
            out_refs[6][:, span] = three[half:].astype(low)

        start = 0
        for index in range(number):
            left_a, left_b, right_a, right_b = in_refs[4 * index : 4 * index + 4]
            columns = slice(*spans[index])
            left = jnp.concatenate([left_a[:, columns], left_b[:, columns]], axis=0)
            for begin in range(0, widths[index], 768):
                stop = min(begin + 768, widths[index])
                right = jnp.concatenate([right_a[:, begin:stop], right_b[:, begin:stop]], axis=0)
                result = dot_first(left, right)
                put(
                    lambda place, result=result: result[place * rows : (place + 1) * rows],
                    slice(start + begin, start + stop),
                )
            start += widths[index]
        if smalls is not None:
            put(lambda place: in_refs[-1][place], slice(start, total))

    out = [shape_of((rows, total), jnp.float32)] + [shape_of((rows, total), low)] * 2
    out += [shape_of((half, total), jnp.float32)] * 2 + [shape_of((half, total), low)] * 2
    flops = sum(4 * left[0].shape[0] * 4 * rows * right[0].shape[1] for left, right in zip(lefts, rights))
    made = pl.pallas_call(
        body,
        out_shape=out,
        in_specs=[whole_block()] * len(arrays),
        out_specs=[whole_block()] * 7,
        compiler_params=params(),
        cost_estimate=cost(flops, 14 * rows * total),
    )(*arrays)
    return [value.reshape(-1, name_rows, total) for value in made]


def split_three(value):
    low = jnp.bfloat16
    first = value.astype(low)
    rest = value - first.astype(jnp.float32)
    second = rest.astype(low)
    return (first, second, (rest - second.astype(jnp.float32)).astype(low))


def pack_stats(top, total):
    lane = lax.broadcasted_iota(jnp.int32, (top.shape[0], 128), 1)
    tile = jnp.zeros((top.shape[0], 128), jnp.float32)
    for place, part in enumerate(split_three(top) + split_three(total)):
        tile = jnp.where(lane == place, part.astype(jnp.float32), tile)
    return tile.astype(jnp.bfloat16)


def unpack_stats(tile):
    wide = tile.astype(jnp.float32)
    return (
        wide[:, 0:1] + (wide[:, 1:2] + wide[:, 2:3]),
        wide[:, 3:4] + (wide[:, 4:5] + wide[:, 5:6]),
    )


def join(one, two):
    top = jnp.maximum(one[1], two[1])
    scale_one, scale_two = jnp.exp(one[1] - top), jnp.exp(two[1] - top)
    return (
        one[0] * scale_one + two[0] * scale_two,
        top,
        one[2] * scale_one + two[2] * scale_two,
    )


def unpack_rows(packed, width):
    top, total = unpack_stats(packed[:, width:])
    return (packed[:, :width].astype(jnp.float32), top, total)


def head_pass(head_in, table_low, here, rows, pick_count):
    count, width = head_in.shape
    chunks = table_low.shape[0] // CHUNK
    groups = count // (2 * pick_count)
    half = count // 2

    def body(here_ref, head_ref, table_ref, own_ref, stat_ref, sent_ref, acc_ref, tops_ref):
        head = head_ref[...]
        real = jnp.minimum(rows, V_REAL - here_ref[0])
        acc_ref[...] = jnp.zeros_like(acc_ref)

        def step(index, carry, masked):
            top, total = carry
            begin = pl.multiple_of(index * CHUNK, CHUNK)
            part = table_ref[pl.ds(begin, CHUNK), :]
            values = dot_second(head, part)
            if masked:
                local = lax.broadcasted_iota(jnp.int32, (1, CHUNK), 1) + begin
                values = jnp.where(local < real, values, MASKED)
            higher = jnp.maximum(top, jnp.max(values, axis=1, keepdims=True))
            grown = jnp.exp(values - higher)
            scale = jnp.exp(top - higher)
            acc_ref[...] = acc_ref[...] * scale + dot_plain(grown.astype(jnp.bfloat16), part)
            return (higher, total * scale + jnp.sum(grown, axis=1, keepdims=True))

        carry = (jnp.full((count, 1), MASKED, jnp.float32), jnp.zeros((count, 1), jnp.float32))
        unmasked = jnp.maximum(real, 0) // CHUNK
        carry = lax.fori_loop(0, unmasked, functools.partial(step, masked=False), carry)
        top, total = lax.fori_loop(unmasked, chunks, functools.partial(step, masked=True), carry)
        lane = lax.broadcasted_iota(jnp.int32, (count, 128), 1)
        tops_ref[...] = jnp.where(lane == 0, top, jnp.where(lane == 1, total, 0.0))
        for group in range(groups):
            own = pl.multiple_of((2 * group + here_ref[1]) * pick_count, pick_count)
            other = pl.multiple_of((2 * group + 1 - here_ref[1]) * pick_count, pick_count)
            span = slice(group * pick_count, (group + 1) * pick_count)
            own_ref[span, :] = acc_ref[pl.ds(own, pick_count), :]
            stat_ref[span, :] = tops_ref[pl.ds(own, pick_count), :]
            sent_ref[span, :width] = acc_ref[pl.ds(other, pick_count), :].astype(jnp.bfloat16)
            stats = tops_ref[pl.ds(other, pick_count), :]
            sent_ref[span, width:] = pack_stats(stats[:, 0:1], stats[:, 1:2])

    return pl.pallas_call(
        body,
        out_shape=[
            shape_of((half, width), jnp.float32),
            shape_of((half, 128), jnp.float32),
            shape_of((half, width + 128), jnp.bfloat16),
        ],
        in_specs=[pl.BlockSpec(memory_space=pltpu.SMEM)] + [whole_block()] * 2,
        out_specs=[whole_block()] * 3,
        scratch_shapes=[pltpu.VMEM((count, width), jnp.float32), pltpu.VMEM((count, 128), jnp.float32)],
        compiler_params=params(),
        cost_estimate=cost(4 * table_low.size * count, 2 * table_low.size),
    )(here, head_in, table_low)


def join_cores(own, stats, received, outer, pick_count):
    half, width = own.shape
    groups = half // pick_count

    def body(outer_ref, own_ref, stat_ref, received_ref, rows_ref, out_stat_ref, *sent_refs):
        for step in range(groups):
            start = pl.multiple_of((outer_ref[0] ^ step) * pick_count, pick_count)
            span = pl.ds(start, pick_count)
            stat = stat_ref[span, :]
            one = (own_ref[span, :], stat[:, 0:1], stat[:, 1:2])
            value, top, total = join(one, unpack_rows(received_ref[span, :], width))
            if step:
                sent_refs[step - 1][:, :width] = value.astype(jnp.bfloat16)
                sent_refs[step - 1][:, width:] = pack_stats(top, total)
            else:
                lane = lax.broadcasted_iota(jnp.int32, (pick_count, 128), 1)
                rows_ref[...] = value
                out_stat_ref[...] = jnp.where(lane == 0, top, jnp.where(lane == 1, total, 0.0))

    return pl.pallas_call(
        body,
        out_shape=[
            shape_of((pick_count, width), jnp.float32),
            shape_of((pick_count, 128), jnp.float32),
        ]
        + [shape_of((pick_count, width + 128), jnp.bfloat16)] * (groups - 1),
        in_specs=[pl.BlockSpec(memory_space=pltpu.SMEM)] + [whole_block()] * 3,
        out_specs=[whole_block()] * (groups + 1),
        compiler_params=params(),
        cost_estimate=cost(4 * own.size, 8 * own.size),
    )(outer, own, stats, received)


def output_backward(rows, stats, received, picked, target_rows, row_sum, picks, resid_out, vec_rows, token_count):
    count, width = resid_out.shape
    number = picks.shape[0]
    low = jnp.bfloat16
    others = len(received)

    def body(rows_ref, stat_ref, *refs):
        received_refs = refs[:others]
        f_ref, t_ref, sum_ref, pick_ref, x_ref, v_ref, dx_ref, dy_ref, vec_ref, norm_ref = refs[others:]
        stat = stat_ref[...]
        value = (rows_ref[...], stat[:, 0:1], stat[:, 1:2])
        for ref in received_refs:
            value = join(value, unpack_rows(ref[...], width))
        mean, top, total = value
        target = t_ref[...]
        final = f_ref[...].astype(jnp.float32)
        norm = top + jnp.log(total)
        hit = jnp.sum(final * target, axis=1, keepdims=True)
        plain = jnp.sum(final * sum_ref[...], axis=1, keepdims=True)
        loss = (1.0 - SMOOTHING) * (norm - hit) + SMOOTHING * (norm - plain / V_REAL)
        lane = lax.broadcasted_iota(jnp.int32, (number, 128), 1)
        norm_ref[...] = jnp.where(lane == 0, norm, jnp.where(lane == 1, loss, 0.0))
        soft = jnp.exp(hit - norm)
        whole = ((soft - (1.0 - SMOOTHING) - SMOOTHING / V_REAL) / token_count).astype(low)
        factor = whole.astype(jnp.float32) - (soft - SMOOTHING / V_REAL) / token_count
        picked_grad = (
            mean * (1.0 / token_count) / total
            - sum_ref[...] * (SMOOTHING / V_REAL / token_count)
            + target * factor
        )
        hot = pick_ref[...] == lax.broadcasted_iota(jnp.int32, (number, count), 1)
        final_grad = lax.dot_general(
            jnp.where(hot, 1.0, 0.0),
            picked_grad,
            (((0,), (0,)), ((), ())),
            precision=lax.Precision.HIGHEST,
            preferred_element_type=jnp.float32,
        )
        back, gain, shift = norm_backward(final_grad, x_ref[...], v_ref[4:5, :])
        dx_ref[...] = back
        dy = back.astype(low)
        dy_ref[...] = dy
        vec_ref[0:1, :] = gain
        vec_ref[1:2, :] = shift
        vec_ref[2:3, :] = column_sum(dy)
        vec_ref[3:8, :] = jnp.zeros((5, width), jnp.float32)

    return pl.pallas_call(
        body,
        out_shape=[
            shape_of((count, width), jnp.float32),
            shape_of((count, width), low),
            shape_of((8, width), jnp.float32),
            shape_of((number, 128), jnp.float32),
        ],
        in_specs=[whole_block()] * (8 + others),
        out_specs=[whole_block()] * 4,
        compiler_params=params(),
        cost_estimate=cost(20 * count * width, 20 * count * width),
    )(rows, stats, *received, picked, target_rows, row_sum, picks, resid_out, vec_rows)


def hidden_backward(dy, w_down, pre):
    count, width = dy.shape
    hidden = pre.shape[1]
    low = jnp.bfloat16

    def body(dy_ref, w_ref, pre_ref, dpre_ref, vec_ref):
        vec_ref[...] = jnp.zeros_like(vec_ref)
        for place in range(hidden // width):
            span = slice(place * width, (place + 1) * width)
            grad = dot_second(dy_ref[...], w_ref[span, :])
            u = pre_ref[:, span]
            bent = jnp.tanh(0.7978845608028654 * (u + 0.044715 * u * u * u))
            slope = 0.5 * (1.0 + bent) + 0.5 * u * (1.0 - bent * bent) * (
                0.7978845608028654 * (1.0 + 3.0 * 0.044715 * u * u)
            )
            dpre = (grad * slope).astype(low)
            dpre_ref[:, span] = dpre
            vec_ref[place : place + 1, :] = column_sum(dpre)

    return pl.pallas_call(
        body,
        out_shape=[shape_of((count, hidden), low), shape_of((8, width), jnp.float32)],
        in_specs=[whole_block()] * 3,
        out_specs=[whole_block()] * 2,
        compiler_params=params(),
        cost_estimate=cost(2 * count * width * hidden, 2 * width * hidden),
    )(dy, w_down, pre)


def middle_backward(dpre, w_up, dx2, x1, w_proj, vec_rows):
    count, width = x1.shape
    low = jnp.bfloat16

    blocks = len(w_up)

    def body(dpre_ref, dx2_ref, x1_ref, proj_ref, v_ref, *refs):
        up_refs = refs[:blocks]
        dx1_ref, da_ref, mixed_ref, vec_ref = refs[blocks:]
        dh2 = jnp.zeros((count, width), jnp.float32)
        for place in range(blocks):
            span = slice(place * width, (place + 1) * width)
            dh2 = dh2 + dot_second(dpre_ref[:, span], up_refs[place][...])
        back, gain, shift = norm_backward(dh2, x1_ref[...], v_ref[2:3, :])
        dx1 = back + dx2_ref[...]
        dx1_ref[...] = dx1
        da = dx1.astype(low)
        da_ref[...] = da
        vec_ref[0:1, :] = gain
        vec_ref[1:2, :] = shift
        vec_ref[2:3, :] = column_sum(da)
        vec_ref[3:8, :] = jnp.zeros((5, width), jnp.float32)
        mixed_ref[...] = dot_second(da, proj_ref[...]).astype(low)

    return pl.pallas_call(
        body,
        out_shape=[
            shape_of((count, width), jnp.float32),
            shape_of((count, width), low),
            shape_of((count, width), low),
            shape_of((8, width), jnp.float32),
        ],
        in_specs=[whole_block()] * (5 + blocks),
        out_specs=[whole_block()] * 4,
        compiler_params=params(),
        cost_estimate=cost(10 * count * width * width, 10 * width * width),
    )(dpre, dx2, x1, w_proj, vec_rows, *w_up)


def attention_backward(mixed, dx1, packed, x0, w_qkv, vec_rows):
    count, width = x0.shape
    low = jnp.bfloat16

    def body(mixed_ref, dx1_ref, packed_ref, x0_ref, qkv_ref, v_ref, dx0_ref, rows_ref, grad_ref, vec_ref):
        causal = causal_mask(count)
        for head in range(0, width // HD, 2):
            sides = ([], [], [])
            for one in (head, head + 1):
                queries = packed_ref[:, one * HD : (one + 1) * HD]
                keys = packed_ref[:, width + one * HD : width + (one + 1) * HD]
                values = packed_ref[:, 2 * width + one * HD : 2 * width + (one + 1) * HD]
                scores = causal_scores(queries, keys, causal)
                grown = jnp.exp(scores - jnp.max(scores, axis=-1, keepdims=True))
                probs = grown / jnp.sum(grown, axis=-1, keepdims=True)
                out_grad = mixed_ref[:, one * HD : (one + 1) * HD]
                grad_p = dot_second(out_grad, values)
                centre = jnp.sum(probs * grad_p, axis=-1, keepdims=True)
                grad_s = (probs * (grad_p - centre)).astype(low)
                sides[0].append(dot_plain(grad_s, keys) * HD ** (-0.5))
                sides[1].append(dot_first(grad_s, queries) * HD ** (-0.5))
                sides[2].append(dot_first(probs.astype(low), out_grad))
            for place, side in enumerate(sides):
                start = place * width + head * HD
                grad_ref[:, start : start + 2 * HD] = jnp.concatenate(side, axis=1).astype(low)
        dh1 = dot_second(grad_ref[...], qkv_ref[...])
        back, gain, shift = norm_backward(dh1, x0_ref[...], v_ref[0:1, :])
        vec_ref[0:1, :] = gain
        vec_ref[1:2, :] = shift
        vec_ref[2:3, :] = column_sum(grad_ref[:, :width])
        vec_ref[3:4, :] = column_sum(grad_ref[:, 2 * width :])
        vec_ref[4:8, :] = jnp.zeros((4, width), jnp.float32)
        dx0 = back + dx1_ref[...]
        dx0_ref[...] = dx0
        rows_ref[...] = dx0.astype(low)

    return pl.pallas_call(
        body,
        out_shape=[
            shape_of((count, width), jnp.float32),
            shape_of((count, width), low),
            shape_of((count, 3 * width), low),
            shape_of((8, width), jnp.float32),
        ],
        in_specs=[whole_block()] * 6,
        out_specs=[whole_block()] * 4,
        compiler_params=params(),
        cost_estimate=cost(16 * count * width * width, 10 * width * width),
    )(mixed, dx1, packed, x0, w_qkv, vec_rows)


def bit_of(index, level):
    return (index >> level) & 1


def xor_order(parts, index):
    level = 0
    while (1 << level) < len(parts):
        odd = bit_of(index, level) == 1
        step = 1 << level
        placed = list(parts)
        for place in range(len(parts)):
            if not place & step:
                low, high = parts[place], parts[place | step]
                placed[place] = jnp.where(odd, high, low)
                placed[place | step] = jnp.where(odd, low, high)
        parts = placed
        level += 1
    return parts


def tree_sum(parts):
    while len(parts) > 1:
        parts = [parts[place] + parts[place + 1] for place in range(0, len(parts), 2)]
    return parts[0]


def swap_core(value):
    count = lax.axis_size("vocab")
    return lax.ppermute(value, "vocab", [(i, i ^ 1) for i in range(count)])


def swap_outer(value, step):
    count = lax.axis_size("vocab")
    return lax.ppermute(value, "vocab", [(i, i ^ (2 * step)) for i in range(count)])


def swap_dp(value, step):
    count = lax.axis_size("dp")
    return lax.ppermute(value, "dp", [(i, i ^ step) for i in range(count)])


def places():
    vocab_index = lax.axis_index("vocab")
    return (lax.axis_index("dp"), vocab_index // 2, vocab_index % 2)


def gather_vocab(value):
    _, outer, core = places()
    pair = jnp.stack(xor_order([value, swap_core(value)], core))
    count = lax.axis_size("vocab") // 2
    parts = [pair] + [swap_outer(pair, step) for step in range(1, count)]
    return jnp.concatenate(xor_order(parts, outer), axis=0)


def gather_dp(value):
    dp_index, _, _ = places()
    parts = [value] + [swap_dp(value, step) for step in range(1, lax.axis_size("dp"))]
    return jnp.stack(xor_order(parts, dp_index))


def sum_all(value):
    value = value + swap_core(value)
    value = tree_sum([value] + [swap_dp(value, step) for step in range(1, lax.axis_size("dp"))])
    return tree_sum(outer_parts(value))


def outer_parts(value):
    count = lax.axis_size("vocab") // 2
    return [value] + [swap_outer(value, step) for step in range(1, count)]


def behind(value, *others):
    return lax.optimization_barrier((value, others))[0]


class Slots:
    def __init__(self):
        self.last = None

    def open(self, value):
        return value if self.last is None else behind(value, self.last)

    def close(self, *results):
        self.last = results


class OuterGather:
    def __init__(self, value):
        self.held = value[None]

    def advance(self, slots):
        count = lax.axis_size("vocab") // 2
        step = count // (2 * self.held.shape[0])
        if step:
            shape = (-1,) + self.held.shape[1:]
            held = slots.open(self.held)
            self.held = jnp.stack([held, swap_outer(held, step)], axis=1).reshape(shape)

    def finish(self, slots):
        while self.held.shape[0] < lax.axis_size("vocab") // 2:
            self.advance(slots)
        return self.held


def ring_first(held, slots):
    held = slots.open(held)
    return (held, swap_dp(held, 1), swap_dp(held, 2))


def ring_second(parts, slots):
    held, from_one, from_two = parts
    half = held.shape[0] // 2
    low, high = slots.open((from_two[:half], from_one[half:]))
    return jnp.concatenate([held, from_one, from_two, swap_dp(low, 1), swap_dp(high, 2)], axis=0)


def place_blocks(held, other, cuts):
    dp_index, outer, core = places()
    count = held.shape[0]
    outer_count = lax.axis_size("vocab") // 2
    here = jnp.stack([dp_index, outer, core]).astype(jnp.int32)
    if held.ndim == 3:
        spans, shapes = [], []
        for width in cuts:
            spans.append((sum(w for _, w in spans), width))
            shapes.append((held.shape[1], width))

        def take(ref, block, index):
            return ref.at[block, :, pl.ds(*spans[index])]

    else:
        shapes = [
            held.shape[2:] if isinstance(one, int) else (one[1] - one[0],) + held.shape[2:]
            for one in cuts
        ]

        def take(ref, block, index):
            one = cuts[index]
            if isinstance(one, int):
                return ref.at[block, one]
            return ref.at[block, pl.ds(one[0], one[1] - one[0])]


    def body(here_ref, held_ref, other_ref, *refs):
        out_refs, sems = refs[: len(cuts)], refs[len(cuts)]

        def copies(block):
            dp_place = (block // outer_count) ^ here_ref[0]
            outer_place = (block % outer_count) ^ here_ref[1]
            target = (dp_place * outer_count + outer_place) * 2
            made = []
            for side, ref in enumerate((held_ref, other_ref)):
                place = target + (here_ref[2] ^ side)
                for index in range(len(cuts)):
                    made.append(
                        pltpu.make_async_copy(
                            take(ref, block, index),
                            out_refs[index].at[place],
                            sems.at[index, side, block],
                        )
                    )
            return made

        def start(block, carry):
            for copy in copies(block):
                copy.start()
            return carry

        def wait(block, carry):
            for copy in copies(block):
                copy.wait()
            return carry

        lax.fori_loop(0, count, start, 0)
        lax.fori_loop(0, count, wait, 0)

    any_space = pl.BlockSpec(memory_space=pl.ANY)
    return pl.pallas_call(
        body,
        out_shape=[
            jax.ShapeDtypeStruct((2 * count,) + tuple(shape), held.dtype) for shape in shapes
        ],
        in_specs=[pl.BlockSpec(memory_space=pltpu.SMEM), any_space, any_space],
        out_specs=[pl.BlockSpec(memory_space=pltpu.VMEM) for _ in cuts],
        scratch_shapes=[pltpu.SemaphoreType.DMA((len(cuts), 2, count))],
        compiler_params=pltpu.CompilerParams(vmem_limit_bytes=VMEM_BYTES),
        cost_estimate=pl.CostEstimate(
            flops=0, bytes_accessed=4 * held.size * held.dtype.itemsize, transcendentals=0
        ),
    )(here, held, other)


def tile_of(values):
    row = lax.broadcasted_iota(jnp.int32, (8, 128), 0)
    lane = lax.broadcasted_iota(jnp.int32, (8, 128), 1)
    tile = jnp.zeros((8, 128), jnp.float32)
    for place, value in enumerate(values):
        if value is not None:
            tile = jnp.where((row == 0) & (lane == place), value, tile)
    return tile


def total_of(value):
    return jnp.sum(jnp.sum(value, axis=1, keepdims=True), axis=0, keepdims=True)


def fold_rows(value):
    return jnp.sum(value.reshape(-1, 8, value.shape[1]), axis=0)


def prepare_table(table, smalls, dp_count, first):
    rows, width = table.shape
    chunks = -(-rows // CHUNK)
    per = max(n for n in range(1, 9) if chunks % n == 0 and n * CHUNK <= rows)
    tile = per * CHUNK
    steps = chunks // per

    def body(first_ref, table_ref, *refs):
        small_refs, (low_ref, sum_ref, row_ref, acc_ref) = refs[: len(smalls)], refs[len(smalls) :]
        step = pl.program_id(0)
        row = lax.broadcasted_iota(jnp.int32, (tile, 1), 0) + step * tile
        value = jnp.where(row < rows, table_ref[...], 0.0)
        rounded = value.astype(jnp.bfloat16)
        low_ref[...] = rounded
        part = fold_rows(value * value)
        whole = jnp.where(row + first_ref[0] < V_REAL, rounded.astype(jnp.float32), 0.0)
        whole = jnp.sum(fold_rows(whole), axis=0, keepdims=True)

        @pl.when(step == 0)
        def _():
            acc_ref[...] = part
            row_ref[...] = whole

        @pl.when(step > 0)
        def _():
            acc_ref[...] += part
            row_ref[...] += whole

        @pl.when(step == steps - 1)
        def _():
            terms = [None] + [total_of(ref[...] * ref[...]) for ref in small_refs]
            terms.append(total_of(acc_ref[...]) / dp_count)
            sum_ref[...] = tile_of(terms)

    return pl.pallas_call(
        body,
        grid=(steps,),
        out_shape=[
            jax.ShapeDtypeStruct((chunks * CHUNK, width), jnp.bfloat16),
            jax.ShapeDtypeStruct((8, 128), jnp.float32),
            jax.ShapeDtypeStruct((1, width), jnp.float32),
        ],
        in_specs=[pl.BlockSpec(memory_space=pltpu.SMEM), pl.BlockSpec((tile, width), lambda i: (i, 0))]
        + [whole_block() for _ in smalls],
        out_specs=[pl.BlockSpec((tile, width), lambda i: (i, 0)), whole_block(), whole_block()],
        scratch_shapes=[pltpu.VMEM((8, width), jnp.float32)],
        compiler_params=pltpu.CompilerParams(vmem_limit_bytes=VMEM_BYTES),
        cost_estimate=pl.CostEstimate(
            flops=4 * table.size, bytes_accessed=6 * table.size, transcendentals=0
        ),
    )(first, table, *smalls)


def logit_grad(values, columns, norms, targets, scale):
    drop = jnp.where(
        columns == targets,
        scale * (1.0 - SMOOTHING + SMOOTHING / V_REAL),
        scale * (SMOOTHING / V_REAL),
    )
    return jnp.exp(values - norms) - drop


def table_part(earlier, head_all, table_low, targets, norms, first, rows, scale, start, stop):
    count, width = head_all.shape
    block = min(512, count)

    def body(first_ref, head_ref, table_ref, target_ref, norm_ref, *refs):
        out_ref, done_ref = refs[-2:]
        done_ref[...] = jnp.zeros_like(done_ref)
        begin = (pl.program_id(0) + start) * PIECE
        real = jnp.minimum(rows, V_REAL - first_ref[0])
        part = table_ref[...]
        local = lax.broadcasted_iota(jnp.int32, (PIECE, 1), 0) + begin
        columns = local + first_ref[0]

        def total_of_blocks(masked):
            total = jnp.zeros((PIECE, width), jnp.float32)
            for place in range(0, count, block):
                span = slice(place, place + block)
                head = head_ref[span, :]
                grad = logit_grad(
                    dot_second(part, head), columns, norm_ref[:, span], target_ref[:, span], scale
                )
                if masked:
                    grad = jnp.where(local < real, grad, 0.0)
                total = total + dot_plain(grad.astype(jnp.bfloat16), head)
            return total

        @pl.when(begin + PIECE <= real)
        def _():
            out_ref[...] = total_of_blocks(False)

        @pl.when(begin + PIECE > real)
        def _():
            out_ref[...] = total_of_blocks(True)

    args = [first, head_all, table_low, targets, norms]
    specs = [
        pl.BlockSpec(memory_space=pltpu.SMEM),
        whole_block(),
        pl.BlockSpec((PIECE, width), lambda i: (i + start, 0)),
        whole_block(),
        whole_block(),
    ]
    aliases = {}
    if earlier is not None:
        aliases = {len(args): 0}
        args.append(earlier)
        specs.append(pl.BlockSpec(memory_space=pl.ANY))
    size = (stop - start) * PIECE
    return pl.pallas_call(
        body,
        grid=(stop - start,),
        out_shape=[
            jax.ShapeDtypeStruct(table_low.shape, jnp.float32),
            jax.ShapeDtypeStruct((8, 128), jnp.float32),
        ],
        in_specs=specs,
        out_specs=[pl.BlockSpec((PIECE, width), lambda i: (i + start, 0)), whole_block()],
        input_output_aliases=aliases,
        compiler_params=pltpu.CompilerParams(vmem_limit_bytes=VMEM_BYTES),
        cost_estimate=pl.CostEstimate(
            flops=4 * size * width * count,
            bytes_accessed=6 * size * width,
            transcendentals=size * count,
        ),
    )(*args)


def token_lists(ids, first, rows, cap, bands):
    local = ids - first
    mine = (local >= 0) & (local < rows)
    tokens = jnp.arange(ids.shape[1], dtype=jnp.int32)
    band = local // CHUNK
    key = jnp.where(mine, band * ids.shape[1] + tokens[None, :], bands * ids.shape[1])
    slot = jnp.sum((key[:, None, :] < key[:, :, None]).astype(jnp.int32), axis=2)
    slots = jnp.arange(cap, dtype=jnp.int32)
    hot = (slot[:, None, :] == slots[None, :, None]) & mine[:, None, :]
    row = jnp.sum(jnp.where(hot, local[:, None, :], 0), axis=2)
    token = jnp.sum(jnp.where(hot, tokens[None, None, :], 0), axis=2)
    upto = jnp.arange(bands, dtype=jnp.int32)
    ends = (band[:, None, :] <= upto[None, :, None]) & mine[:, None, :]
    return (jnp.sum(ends.astype(jnp.int32), axis=2), row, token)


def add_rows(table_grad, held, other, ends, row_list, token_list, gradients, weight_sums, dp_count):
    padded, width = table_grad.shape
    dp_index, outer, core = places()
    here = jnp.stack([dp_index, outer, core]).astype(jnp.int32)
    outer_count = lax.axis_size("vocab") // 2
    sequences, bands = ends.shape
    tokens = held.shape[1]
    cap = row_list.shape[1]
    fine = 256
    per = CHUNK // fine
    kept = sequences if sequences * tokens * width * 4 <= 2**24 else 1

    def body(here_ref, end_ref, row_ref, token_ref, grad_in_ref, held_ref, other_ref, sums_ref, *refs):
        small_refs = refs[: len(gradients)]
        grad_out_ref, total_ref, grad_ref, rows_ref, in_sems, out_sems = refs[len(gradients) :]

        def in_copy(index):
            span = pl.ds(pl.multiple_of(index * CHUNK, CHUNK), CHUNK)
            return pltpu.make_async_copy(grad_in_ref.at[span], grad_ref.at[span], in_sems.at[index])

        def out_copy(index):
            span = pl.ds(pl.multiple_of(index * CHUNK, CHUNK), CHUNK)
            return pltpu.make_async_copy(grad_ref.at[span], grad_out_ref.at[span], out_sems.at[index])

        for index in range(bands):
            in_copy(index).start()
        clip = jnp.zeros((1, 1), jnp.float32)
        for ref in small_refs:
            clip = clip + total_of(ref[...] * ref[...])

        def widen(index, carry):
            dp_place = (index // 2) // outer_count
            outer_place = (index // 2) % outer_count
            block = (dp_place ^ here_ref[0]) * outer_count + (outer_place ^ here_ref[1])
            span = pl.ds(pl.multiple_of(index % kept * tokens, tokens), tokens)

            @pl.when(index % 2 == here_ref[2])
            def _():
                rows_ref[span, :] = held_ref[block].astype(jnp.float32)

            @pl.when(index % 2 != here_ref[2])
            def _():
                rows_ref[span, :] = other_ref[block].astype(jnp.float32)

            return carry

        if kept > 1:
            lax.fori_loop(0, sequences, widen, 0)
        acc = jnp.zeros((8, width), jnp.float32)
        for band in range(bands):
            in_copy(band).wait()

            def sequence(index, carry, band=band):
                if kept == 1:
                    widen(index, 0)

                def one(slot, carry):
                    row = row_ref[index * cap + slot]
                    token = index % kept * tokens + token_ref[index * cap + slot]
                    grad_ref[pl.ds(row, 1), :] += rows_ref[pl.ds(token, 1), :]
                    return carry

                begin = end_ref[index * bands + band - 1] if band else 0
                lax.fori_loop(begin, end_ref[index * bands + band], one, 0)
                return carry

            lax.fori_loop(0, sequences, sequence, 0)
            out_copy(band).start()

            def square(index, acc, band=band):
                span = pl.ds(pl.multiple_of(band * CHUNK + index * fine, fine), fine)
                value = grad_ref[span, :]
                return acc + fold_rows(value * value)

            acc = lax.fori_loop(0, per, square, acc)
        total_ref[...] = sums_ref[...] + tile_of([clip + total_of(acc) / dp_count])
        for band in range(bands):
            out_copy(band).wait()

    smem = pl.BlockSpec(memory_space=pltpu.SMEM)
    any_space = pl.BlockSpec(memory_space=pl.ANY)
    return pl.pallas_call(
        body,
        out_shape=[
            jax.ShapeDtypeStruct(table_grad.shape, jnp.float32),
            jax.ShapeDtypeStruct((8, 128), jnp.float32),
        ],
        in_specs=[smem, smem, smem, smem, any_space, whole_block(), whole_block(), whole_block()]
        + [whole_block() for _ in gradients],
        out_specs=[any_space, whole_block()],
        scratch_shapes=[
            pltpu.VMEM((padded, width), jnp.float32),
            pltpu.VMEM((kept * tokens, width), jnp.float32),
            pltpu.SemaphoreType.DMA((bands,)),
            pltpu.SemaphoreType.DMA((bands,)),
        ],
        input_output_aliases={4: 0},
        compiler_params=pltpu.CompilerParams(vmem_limit_bytes=VMEM_BYTES),
        cost_estimate=pl.CostEstimate(
            flops=2 * table_grad.size, bytes_accessed=8 * table_grad.size, transcendentals=0
        ),
    )(
        here,
        ends.reshape(-1),
        row_list.reshape(-1),
        token_list.reshape(-1),
        table_grad,
        held,
        other,
        weight_sums,
        *gradients,
    )


def moments_of(gradient, first, second, factor):
    clipped = gradient * factor
    first = BETA_ONE * first + (1.0 - BETA_ONE) * clipped
    second = BETA_TWO * second + (1.0 - BETA_TWO) * clipped * clipped
    return (first, second)


def update_of(weight, first, second):
    scaled = second * (1.0 / (1.0 - BETA_TWO**STEP))
    root = scaled * lax.rsqrt(scaled) + ADAM_EPS
    return first * (1.0 / (1.0 - BETA_ONE**STEP)) / root + DECAY * weight


def clip_factor(sums):
    return jnp.minimum(1.0, CLIP_AT / jnp.sqrt(sums[0:1, 0:1]))


def table_tile(rows, dp_count):
    return -(-rows // (3 * dp_count * 8)) * 8


def update_norms(sums, smalls, table_set, dp_count):
    weight, gradient, first, second = table_set
    rows, width = weight.shape
    tile = -(-rows // (6 * dp_count * 8)) * 8
    last = -(-rows // tile) - 1
    here = lax.axis_index("dp").astype(jnp.int32).reshape(1)
    number = len(smalls)

    def body(here_ref, sums_ref, w_ref, g_ref, m_ref, s_ref, *refs):
        small_refs = refs[: 4 * number]
        out_refs = refs[4 * number : 7 * number]
        norm_ref, acc_ref, term_ref = refs[7 * number :]
        step = pl.program_id(0)
        factor = clip_factor(sums_ref[...])

        @pl.when(step == 0)
        def _():
            acc_ref[...] = jnp.zeros_like(acc_ref)
            terms = [None]
            for place in range(number):
                w, g, m, s = (ref[...] for ref in small_refs[4 * place : 4 * place + 4])
                m, s = moments_of(g, m, s, factor)
                u = update_of(w, m, s)
                out_refs[3 * place][...] = m
                out_refs[3 * place + 1][...] = s
                out_refs[3 * place + 2][...] = u
                terms.append(total_of(u * u))
            term_ref[...] = tile_of(terms)

        row = (here_ref[0] * 6 + step) * tile + lax.broadcasted_iota(jnp.int32, (tile, 1), 0)
        m, s = moments_of(g_ref[...], m_ref[...], s_ref[...], factor)
        u = jnp.where(row < rows, update_of(w_ref[...], m, s), 0.0)
        acc_ref[...] += fold_rows(u * u)

        @pl.when(step == 5)
        def _():
            norm_ref[...] = term_ref[...] + tile_of([None] * (number + 1) + [total_of(acc_ref[...])])

    block = pl.BlockSpec(
        (tile, width), lambda i, here_ref: (jnp.minimum(here_ref[0] * 6 + i, last), 0)
    )
    flat = [value for group in smalls for value in group]
    outs = [jax.ShapeDtypeStruct(group[0].shape, jnp.float32) for group in smalls for _ in range(3)]
    made = pl.pallas_call(
        body,
        grid_spec=pltpu.PrefetchScalarGridSpec(
            num_scalar_prefetch=1,
            grid=(6,),
            in_specs=[whole_block()] + [block] * 4 + [whole_block() for _ in flat],
            out_specs=[whole_block() for _ in outs] + [whole_block()],
            scratch_shapes=[pltpu.VMEM((8, width), jnp.float32), pltpu.VMEM((8, 128), jnp.float32)],
        ),
        out_shape=outs + [jax.ShapeDtypeStruct((8, 128), jnp.float32)],
        compiler_params=pltpu.CompilerParams(vmem_limit_bytes=VMEM_BYTES),
        cost_estimate=pl.CostEstimate(
            flops=20 * tile * 6 * width, bytes_accessed=16 * tile * 6 * width, transcendentals=2 * tile * 6 * width
        ),
    )(here, sums, weight, gradient, first, second, *flat)
    return ([made[3 * place : 3 * place + 3] for place in range(number)], made[-1])


def write_updates(sums, norms, smalls, table_set):
    weight, gradient, first, second = table_set
    rows, width = weight.shape
    tile = table_tile(rows, lax.axis_size("dp"))
    steps = -(-rows // tile)
    number = len(smalls)

    def body(sums_ref, norms_ref, w_ref, g_ref, m_ref, s_ref, *refs):
        small_refs = refs[: 2 * number]
        out_w, out_m, out_s = refs[2 * number : 2 * number + 3]
        small_outs = refs[2 * number + 3 :]
        sums = sums_ref[...]
        pace = RATE * jnp.sqrt(sums) / jnp.sqrt(norms_ref[...])

        @pl.when(pl.program_id(0) == 0)
        def _():
            for place in range(number):
                w, u = (ref[...] for ref in small_refs[2 * place : 2 * place + 2])
                small_outs[place][...] = w - pace[0:1, place + 1 : place + 2] * u

        m, s = moments_of(g_ref[...], m_ref[...], s_ref[...], clip_factor(sums))
        w = w_ref[...]
        out_m[...] = m
        out_s[...] = s
        out_w[...] = w - pace[0:1, number + 1 : number + 2] * update_of(w, m, s)

    block = pl.BlockSpec((tile, width), lambda i: (i, 0))
    flat = [value for group in smalls for value in group]
    outs = [jax.ShapeDtypeStruct(weight.shape, jnp.float32)] * 3
    outs += [jax.ShapeDtypeStruct(group[0].shape, jnp.float32) for group in smalls]
    return pl.pallas_call(
        body,
        grid=(steps,),
        out_shape=outs,
        in_specs=[whole_block(), whole_block()] + [block] * 4 + [whole_block() for _ in flat],
        out_specs=[block] * 3 + [whole_block() for _ in smalls],
        compiler_params=pltpu.CompilerParams(vmem_limit_bytes=VMEM_BYTES),
        cost_estimate=pl.CostEstimate(
            flops=20 * weight.size, bytes_accessed=28 * weight.size, transcendentals=2 * weight.size
        ),
    )(sums, norms, weight, gradient, first, second, *flat)


def pick_half(value, index, axis):
    return lax.dynamic_index_in_dim(value, index, axis, keepdims=False)


class OuterSum:
    def __init__(self, held):
        self.held = held
        self.step = 1

    def advance(self, slots):
        held = self.held
        if held.shape[0] > 1:
            _, outer, _ = places()
            pairs = held.reshape((-1, 2) + held.shape[1:])
            own = (outer // self.step) % 2
            out = slots.open(pick_half(pairs, 1 - own, 1).astype(jnp.bfloat16))
            self.held = pick_half(pairs, own, 1) + swap_outer(out, self.step).astype(jnp.float32)
            self.step *= 2

    def finish(self, slots):
        while self.held.shape[0] > 1:
            self.advance(slots)
        return self.held.reshape(self.held.shape[1:])


def scatter_first(parts, slots):
    own, one, two, one_upper, two_lower, first, second = parts
    half = first.shape[0]
    low = jnp.bfloat16
    first, second = slots.open((first, second))
    into_two = swap_dp(first, 1).astype(jnp.float32)
    into_one = swap_dp(second, 2).astype(jnp.float32)
    return (
        own,
        one.at[half:].set((one_upper + into_one).astype(low)),
        two.at[:half].set((two_lower + into_two).astype(low)),
    )


def scatter_second(parts, slots):
    own, one, two = parts
    one, two = slots.open((one, two))
    return own + (swap_dp(one, 1).astype(jnp.float32) + swap_dp(two, 2).astype(jnp.float32))


def shards(
    token_ids,
    pick_rows,
    target_ids,
    attn_in,
    attn_out,
    mlp_in,
    mlp_out,
    positions,
    vectors,
    table,
    *moments,
):
    low = jnp.bfloat16
    dp_index, outer, core = places()
    dp_count = lax.axis_size("dp")
    shard_count = lax.axis_size("vocab")
    device_count = dp_count * shard_count
    outer_count = shard_count // 2
    vocab_rows, width = table.shape
    seq_len = token_ids.shape[1]
    pick_count = pick_rows.shape[1]
    vocab_start = lax.axis_index("vocab") * vocab_rows

    slots = Slots()
    unit_rows = attn_in.shape[0]
    small_count = positions.size + vectors.size
    small_width = -(-small_count // (unit_rows * 128)) * 128
    small = jnp.concatenate([positions.astype(low).reshape(-1), vectors.astype(low).reshape(-1)])
    small = jnp.pad(small, (0, unit_rows * small_width - small_count))
    first = OuterGather(
        jnp.concatenate(
            [attn_in.astype(low), attn_out.astype(low), small.reshape(unit_rows, small_width)], axis=1
        )
    )
    up_parts = mlp_in.shape[1] // width
    both = OuterGather(
        jnp.concatenate(
            [
                jnp.swapaxes(mlp_in.astype(low).reshape(unit_rows, up_parts, width), 0, 1),
                mlp_out.astype(low).reshape(-1, unit_rows, width),
            ],
            axis=0,
        )
    )
    small_masters = (attn_in, attn_out, mlp_in, mlp_out, positions, vectors)

    first.advance(slots)
    packed_ids = jnp.concatenate([token_ids, target_ids], axis=1)
    ids_pair = jnp.stack(xor_order([packed_ids, swap_core(packed_ids)], core))
    slots.close(first.held, ids_pair)

    first.finish(slots)
    ids_parts = outer_parts(slots.open(ids_pair))
    group_packed = jnp.concatenate(xor_order(ids_parts, outer), axis=0).reshape(shard_count, -1)
    group_targets = group_packed[:, seq_len:]
    slots.close(first.held, group_packed)

    first_ring = ring_first(first.held, slots)
    both.advance(slots)
    group_local = slots.open(group_packed) - vocab_start
    mine = (group_local >= 0) & (group_local < vocab_rows)
    served = jnp.take(table, jnp.where(mine, group_local, 0).reshape(-1), axis=0)
    served = jnp.where(mine.reshape(-1)[:, None], served, 0.0).astype(low)
    served = served.reshape(outer_count, 2, -1, width)
    slots.close(first_ring, both.held, served)

    first_held = ring_second(first_ring, slots)
    served = slots.open(served)
    served = pick_half(served, core, 1) + swap_core(pick_half(served, 1 - core, 1))
    slots.close(first_held, served)

    both.finish(slots)
    first_other = swap_core(slots.open(first_held))
    embedded = OuterSum(slots.open(served)[:, :seq_len].astype(jnp.float32))
    embedded.advance(slots)
    first_column = vocab_start.astype(jnp.int32).reshape(1)
    table_low, weight_sums, row_part = prepare_table(
        slots.open(table), small_masters, dp_count, first_column
    )
    slots.close(first_other, both.held, embedded.held, table_low)

    both_ring = ring_first(both.held, slots)
    embedded = embedded.finish(slots)
    w_qkv, w_proj, small_all = place_blocks(
        slots.open(first_held), first_other, (3 * width, width, small_width)
    )
    slots.close(embedded, w_qkv)

    w_qkv = w_qkv.reshape(width, 3 * width)
    w_proj = w_proj.reshape(width, width)
    small_all = slots.open(small_all).reshape(device_count, -1)
    pos_low = small_all[:, : positions.size].reshape(seq_len, width)
    vec_low = small_all[:, positions.size : small_count].reshape((device_count,) + vectors.shape)
    vec_rows = jnp.moveaxis(vec_low, 0, 1).reshape(vectors.shape[0], width).astype(jnp.float32)
    unit_chooser = choosers(width, unit_rows, core, dp_index)
    slots.close(both_ring, embedded, vec_rows, pos_low, unit_chooser)

    both_held = ring_second(both_ring, slots)
    resid_in, packed, resid_mid, normed_two, lefts_own, lefts_sent = attention_forward(
        slots.open(embedded), pos_low, vec_rows, w_qkv, w_proj, unit_chooser
    )
    target_rows = served[:, seq_len:].astype(jnp.float32)
    target_rows = OuterSum(target_rows)
    target_rows.advance(slots)
    slots.close(both_held, normed_two, target_rows.held)

    both_other = swap_core(slots.open(both_held))
    lefts_got = swap_core(slots.open(lefts_sent))
    target_rows = target_rows.finish(slots)
    packed_all = gather_dp(slots.open(group_packed)).reshape(device_count, -1)
    made = place_blocks(
        both_held, both_other, tuple(range(up_parts)) + ((up_parts, both_held.shape[1]),)
    )
    w_up = [value.reshape(width, width) for value in made[:up_parts]]
    w_down = made[up_parts].reshape(-1, width)
    hidden_pre, hidden_act, act_own, act_sent = hidden_forward(
        normed_two,
        vec_rows,
        w_up,
        choosers(width, mlp_out.shape[0], core),
        dp_index.astype(jnp.int32).reshape(1),
    )
    picks = pick_rows.reshape(-1, 1)
    resid_out, picked = output_forward(hidden_act, w_down, resid_mid, vec_rows, picks)
    slots.close(picked, packed_all, lefts_got, target_rows)

    tail_rows = jnp.concatenate(split_three(row_part), axis=0)
    sent = jnp.concatenate([picked, jnp.pad(tail_rows, ((0, 13), (0, 0)))], axis=0)
    same_core = jnp.stack(outer_parts(slots.open(sent)))
    act_got = swap_core(slots.open(act_sent))
    slots.close(same_core, act_got)

    ordered = jnp.stack(xor_order([same_core[step] for step in range(outer_count)], outer))
    head_in = jnp.stack(xor_order([ordered, swap_core(slots.open(ordered))], core), axis=1)
    row_sum = head_in[:, :, pick_count : pick_count + 3].astype(jnp.float32).reshape(-1, width)
    row_sum = jnp.sum(row_sum, axis=0, keepdims=True)
    head_in = head_in[:, :, :pick_count]
    head_in = head_in.reshape(-1, width)
    slots.close(head_in)
    ring = ring_first(same_core[:, :pick_count], slots)
    here = jnp.stack([vocab_start, core]).astype(jnp.int32)
    head_own, head_stat, head_sent = head_pass(slots.open(head_in), table_low, here, vocab_rows, pick_count)
    slots.close(head_sent, ring)

    head_got = swap_core(slots.open(head_sent))
    joined = join_cores(
        head_own, head_stat, head_got, outer.astype(jnp.int32).reshape(1), pick_count
    )
    slots.close(joined[0])

    received = [
        swap_outer(value, step + 1) for step, value in enumerate(slots.open(tuple(joined[2:])))
    ]
    token_count = device_count * pick_count
    grad_top, grad_branch, vec_down, row_stats = output_backward(
        joined[0],
        joined[1],
        received,
        picked,
        target_rows,
        row_sum,
        picks,
        resid_out,
        vec_rows,
        float(token_count),
    )
    slots.close(grad_branch)

    dy_got = swap_core(slots.open(grad_branch))
    stats_pair = slots.open(row_stats[:, :2].T)
    stats_pair = jnp.stack(xor_order([stats_pair, swap_core(stats_pair)], core))
    ring = ring_second(ring, slots)
    grad_pre, vec_up = hidden_backward(slots.open(grad_branch), w_down, hidden_pre)
    slots.close(dy_got, stats_pair, grad_pre, ring)

    pre_got = swap_core(slots.open(grad_pre))
    stats_parts = outer_parts(slots.open(stats_pair))
    stats_group = jnp.concatenate(xor_order(stats_parts, outer), axis=0)
    down = gradient_blocks(
        [(act_own, act_got)],
        [(0, act_own.shape[1])],
        [(slots.open(grad_branch), dy_got)],
        None,
        mlp_out.shape[0],
    )
    slots.close(pre_got, stats_group, down[5])

    lefts = (lefts_own, lefts_got)
    left_spans = [(place * width // 2, (place + 1) * width // 2) for place in range(3)]
    down = scatter_first(down, slots)
    stats_all = gather_dp(slots.open(stats_group))
    up = gradient_blocks(
        [lefts], left_spans[2:], [(slots.open(grad_pre), pre_got)], None, unit_rows
    )
    grad_mid, grad_attn, grad_mixed, vec_middle = middle_backward(
        behind(grad_pre, up[5]), w_up, grad_top, resid_mid, w_proj, vec_rows
    )
    slots.close(down, up, grad_mid, stats_all)

    down = OuterSum(scatter_second(down, slots))
    attn_got = swap_core(slots.open(grad_attn))
    ring_other = swap_core(slots.open(ring))
    grad_in, grad_rows, grad_packed, vec_first = attention_backward(
        grad_mixed, slots.open(grad_mid), packed, resid_in, w_qkv, vec_rows
    )
    slots.close(down.held, grad_rows, attn_got, ring_other)
    grad_in, vec_first = slots.open((grad_in, vec_first))

    norm_all = (stats_all[:, :, 0].reshape(1, -1) + math.log(token_count)).astype(jnp.float32)
    loss = jnp.sum(stats_all[:, :, 1]) / token_count
    targets_all = packed_all[:, seq_len:].reshape(1, -1)
    counts, row_list, token_list = token_lists(
        packed_all[:, :seq_len],
        vocab_start,
        vocab_rows,
        4 * seq_len // shard_count,
        table_low.shape[0] // CHUNK,
    )

    vec_grad = jnp.concatenate(
        [
            vec_first[0:2],
            vec_middle[0:2],
            vec_down[0:2],
            vec_first[2:4],
            vec_middle[2:3],
            vec_down[2:3],
            vec_up[0:4],
        ],
        axis=0,
    )
    vec_width = vectors.shape[1]
    vec_blocks = jnp.moveaxis(vec_grad.reshape(-1, device_count, vec_width), 1, 0)
    small_grad = jnp.concatenate(
        [grad_in.reshape(device_count, -1), vec_blocks.reshape(device_count, -1)], axis=1
    )
    small_grad = jnp.pad(small_grad, ((0, 0), (0, unit_rows * small_width - small_count)))
    small_grad = small_grad.reshape(-1, 2, unit_rows, small_width)
    small_sent = pick_half(small_grad, 1 - core, 1).astype(low)

    pieces = table_low.shape[0] // PIECE
    bounds = [0] + [round(pieces * share) for share in (0.3, 0.7, 0.9)] + [pieces]

    def head_part(earlier, part, mark):
        if bounds[part] == bounds[part + 1]:
            return (earlier, mark)
        return table_part(
            earlier,
            head_all,
            table_low,
            targets_all,
            behind(norm_all, mark),
            first_column,
            vocab_rows,
            1.0 / token_count,
            bounds[part],
            bounds[part + 1],
        )

    up = scatter_first(up, slots)
    packed_got = swap_core(slots.open(grad_packed))
    small_got = swap_core(slots.open(small_sent))
    small_sum = pick_half(small_grad, core, 1) + small_got.astype(jnp.float32)
    small_sum = small_sum.reshape(4, outer_count * unit_rows, small_width)
    small_sum = jnp.stack([pick_half(small_sum, dp_index ^ step, 0) for step in range(4)])
    head_all = place_blocks(slots.open(ring), ring_other, (width,))[0].reshape(-1, width)
    rows = OuterGather(slots.open(grad_rows))
    rows.advance(slots)
    slots.close(up[1:], packed_got, small_sum, rows.held, head_all)

    up = OuterSum(scatter_second(up, slots))
    rows_outer = rows.finish(slots)
    down.advance(slots)
    first = gradient_blocks(
        [lefts, lefts],
        left_spans[:2],
        [(grad_packed, slots.open(packed_got)), (grad_attn, attn_got)],
        small_sum,
        unit_rows,
    )
    table_grad, mark = head_part(None, 0, first[5])
    slots.close(up.held, first[5], rows_outer, down.held, mark)

    first = scatter_first(first, slots)
    rows_ring = ring_first(rows_outer, slots)
    up.advance(slots)
    table_grad, mark = head_part(table_grad, 1, slots.last)
    slots.close(first[1:], rows_ring, up.held, mark)

    first = scatter_second(first, slots)
    rows_held = ring_second(rows_ring, slots)
    up_own = up.finish(slots)
    table_grad, mark = head_part(table_grad, 2, slots.last)
    slots.close(first, up_own, rows_held, mark)

    first_terms = [pick_half(first, outer, 0)]
    for step in range(1, outer_count):
        sent = slots.open(pick_half(first, outer ^ step, 0).astype(low))
        first_terms.append(swap_outer(sent, step).astype(jnp.float32))
    first_own = tree_sum(first_terms)
    rows_other = swap_core(slots.open(rows_held))
    down_own = down.finish(slots)
    table_grad, mark = head_part(table_grad, 3, slots.last)
    small_own = first_own[:, 4 * width :].reshape(-1)
    gradients = (
        first_own[:, : 3 * width],
        first_own[:, 3 * width : 4 * width],
        up_own,
        down_own,
        small_own[: positions.size].reshape(positions.shape),
        small_own[positions.size : small_count].reshape(vectors.shape),
    )
    table_grad, sums = add_rows(
        table_grad, rows_held, rows_other, counts, row_list, token_list, gradients, weight_sums, dp_count
    )
    sums = sum_all(sums)
    grad_norm = jnp.sqrt(sums[0, 0])
    firsts, seconds = moments[:7], moments[7:]
    smalls = list(zip(small_masters, gradients, firsts, seconds))
    table_set = (table, table_grad, firsts[6], seconds[6])
    made, norms = update_norms(sums, smalls, table_set, dp_count)
    norms = sum_all(norms)
    ratios = jnp.sqrt(sums[0, 1:8]) / jnp.sqrt(norms[0, 1:8])
    written = write_updates(
        sums, norms, [(weight, group[2]) for weight, group in zip(small_masters, made)], table_set
    )
    new_weights = list(written[3:]) + [written[0]]
    new_firsts = [group[0] for group in made] + [written[1]]
    new_seconds = [group[1] for group in made] + [written[2]]
    return (loss, grad_norm, ratios, *new_weights, *new_firsts, *new_seconds)


def solution(mesh):
    rows = P(("dp", "vocab"), None)
    weights = (rows, rows, rows, rows, rows, P(None, ("dp", "vocab")), P("vocab", None))
    return jax.shard_map(
        shards,
        mesh=mesh,
        in_specs=(rows, rows, rows) + weights * 3,
        out_specs=(P(), P(), P()) + weights * 3,
        check_vma=False,
    )
```

time: 617 us -> 579 us (0.938)
  Pallas kernels: 284 us -> 266 us
  waiting for transfers between devices: 94.1 us -> 83.7 us
  other arithmetic: 48.9 us -> 40.6 us
    ppermute x44 -> x40, waiting for transfers between devices: 40.5 us -> 21.1 us  [swap_dp(): return lax.ppermute(value, 'dp', [(i, i ^ step) for i in range(count)])]
    ppermute x34 -> x35, waiting for transfers between devices: 47.6 us -> 57.6 us  [swap_outer(): lax.ppermute(value, 'vocab', [(i, i ^ 2 * step) for i in range(count)])]
    add x8 -> x5, other arithmetic: 10.9 us -> 1.45 us  [the longest x1 0.66 us: shards(): stats_all[:, :, 0].reshape(1, -1) + math.log(token_count)]
    pallas_call x1, Pallas kernels: 23.7 us -> 15.8 us  [add_rows(): pl.pallas_call(body, out_shape=[jax.ShapeDtypeStruct(table_grad.shape, jn...]
    scatter x0 -> x6, other arithmetic: none -> 6.4 us  [the longest x3 3.59 us: scatter_first(): two.at[:half].set((two_lower + into_two).astype(low))]
    ppermute x34 -> x35, starting transfers between devices: 50.4 us -> 55.8 us  [swap_outer(): lax.ppermute(value, 'vocab', [(i, i ^ 2 * step) for i in range(count)])]
    unnamed x63 -> x109, local copies, waits for them, and re-layouts: 24.7 us -> 19.8 us
    pallas_call x7 -> x9, Pallas kernels: 62.6 us -> 67.5 us  [the longest x1 22.5 us: head_pass(): pl.pallas_call(body, out_shape=[shape_of((half, width), jnp.float32), sha...]
  transfers between devices with their start and end apart: 93 -> 93, of which waited for: 41 -> 31; matrix products, arithmetic and copies ran while one was open for 16% -> 16% of each run, Pallas kernels for 24% -> 30%
where the time goes in v3:
time: 579 us; the launch traced here: 567 us
  Pallas kernels  266 us (46%)
  starting transfers between devices  101 us (17%)
  waiting for transfers between devices  83.7 us (14%)
  local copies, waits for them, and re-layouts  69.9 us (12%)
  other arithmetic  40.6 us (7%)
  between operations  6.12 us (1%)
    pallas_call x4, Pallas kernels, table_part(): pl.pallas_call(body, grid=(stop - start,), out_shape=[jax.ShapeDtypeStruc...  63.2 us
    ppermute x35, waiting for transfers between devices, swap_outer(): lax.ppermute(value, 'vocab', [(i, i ^ 2 * step) for i in range(count)])  57.6 us
    ppermute x35, starting transfers between devices, swap_outer(): lax.ppermute(value, 'vocab', [(i, i ^ 2 * step) for i in range(count)])  55.8 us
    pallas_call x1, Pallas kernels, write_updates(): pl.pallas_call(body, grid=(steps,), out_shape=outs, in_specs=[whole_block...  55 us
    ppermute x40, starting transfers between devices, swap_dp(): return lax.ppermute(value, 'dp', [(i, i ^ step) for i in range(count)])  42.9 us
    pallas_call x1, Pallas kernels, head_pass(): pl.pallas_call(body, out_shape=[shape_of((half, width), jnp.float32), sha...  22.5 us
    ppermute x40, waiting for transfers between devices, swap_dp(): return lax.ppermute(value, 'dp', [(i, i ^ step) for i in range(count)])  21.1 us
    pallas_call x3, Pallas kernels, place_blocks(): pl.pallas_call(body, out_shape=[jax.ShapeDtypeStruct((2 * count,) + tuple...  20.8 us
  transfers between devices with their start and end apart: 93, of which 31 were waited for; matrix products, arithmetic and copies ran while one was open for 16% of the time, Pallas kernels for 30%

profile of v3, /device:TPU:0, one launch (start us, length us, event | category | flops | bytes accessed | tf_op | source)
XLA Modules:
  0.0 567.5 jit_solution(2005821961234957591)
XLA Ops:
  5.9 3.7 collective-permute-start.1
  10.7 7.1 %collective-permute-done.1 = bf16[1,24,3328]{2,1,0:T(8,128)(2,1)S(1)} collective-permute-done((bf16[1,24,3328]{2,1,0:T(8,128)(2,1)S(1)}, bf16[1,24,3328]{2,1,0:T(8,128)(2,1)S(1)}, u32[]{:S(2)}, u32[]{:S(2)}) %collective-permute-start.1) | collective-permute-done | bytes 159776 | tf_op jit(solution)/shard_map/ppermute | solution.py:646
  17.8 3.6 collective-permute-start.2
  23.4 2.6 collective-permute-done.3
  26.0 5.0 collective-permute-done.5
  35.3 2.3 collective-permute-start.8
  37.6 12.6 %gather_fusion = bf16[1536,768]{1,0:T(8,128)(2,1)S(1)} fusion(f32[6288,768]{1,0:T(8,128)} %w_ref.3, s32[2048]{0:T(1024)S(1)} %pad_clamp_fusion), kind=kCustom, calls=%fused_computation | custom fusion | bytes 4724736 | tf_op jit(solution)/shard_map/jit(_take)/gather | solution.py:1314
  60.0 5.0 collective-permute-done.10
  71.2 13.9 %shard_map.415 = (bf16[6400,768]{1,0:T(8,128)(2,1)}, f32[8,128]{1,0:T(8,128)}, f32[1,768]{1,0:T(1,128)}) custom-call(s32[1]{0:T(128)} %bitcast.1.first_ref, f32[6288,768]{1,0:T(8,128)} %w_ref.3, f32[24,2304]{1,0:T(8,128)} %refs_0_.5, f32[24,768]{1,0:T(8,128)} %refs_2_.5, f32[24,3072]{1,0:T(8,128)} %refs_4_.5, f32[96,768]{1,0:T(8,128)} %refs_6_.3, ...), custom_call_target="tpu_custom_call" | custom-call | flops 19316736 | bytes 28975104 | tf_op jit(solution)/shard_map/pallas_call | solution.py:857
  86.2 6.0 %collective-permute-done.14 = bf16[2,8,24,768]{3,2,1,0:T(8,128)(2,1)S(1)} collective-permute-done((bf16[2,8,24,768]{3,2,1,0:T(8,128)(2,1)S(1)}, bf16[2,8,24,768]{3,2,1,0:T(8,128)(2,1)S(1)}, u32[]{:S(2)}, u32[]{:S(2)}) %collective-permute-start.14) | collective-permute-done | bytes 589856 | tf_op jit(solution)/shard_map/ppermute | solution.py:646
  96.8 6.5 %shard_map.416 = (bf16[32,24,2304]{2,1,0:T(8,128)(2,1)}, bf16[32,24,768]{2,1,0:T(8,128)(2,1)}, bf16[32,24,256]{2,1,0:T(8,128)(2,1)}) custom-call(s32[3]{0:T(128)} %pad_add_fusion.2.here_ref, bf16[16,24,3328]{2,1,0:T(8,128)(2,1)} %constant_dynamic-update-slice_fusion.2.held_ref, bf16[16,24,3328]{2,1,0:T(8,128)(2,1)} %collective-permute-done.13.other_ref), custom_call_target="tpu_custom_call" | custom-call | bytes 10223616 | tf_op jit(solution)/shard_map/pallas_call | solution.py:790
  112.4 7.5 %collective-permute-done.16 = bf16[4,8,24,768]{3,2,1,0:T(8,128)(2,1)} collective-permute-done((bf16[4,8,24,768]{3,2,1,0:T(8,128)(2,1)S(1)}, bf16[4,8,24,768]{3,2,1,0:T(8,128)(2,1)}, u32[]{:S(2)}, u32[]{:S(2)}) %collective-permute-start.16) | collective-permute-done | bytes 1179680 | tf_op jit(solution)/shard_map/ppermute | solution.py:651
  125.0 2.4 constant_dynamic-update-slice_fusion.10
  127.4 8.7 %shard_map.417 = (f32[128,768]{1,0:T(8,128)}, bf16[128,2304]{1,0:T(8,128)(2,1)}, f32[128,768]{1,0:T(8,128)}, bf16[128,768]{1,0:T(8,128)(2,1)}, bf16[128,1152]{1,0:T(8,128)(2,1)}, /*index=5*/bf16[128,1152]{1,0:T(8,128)(2,1)}) custom-call(f32[128,768]{1,0:T(8,128)} %add_bitcast_fusion.e_ref, bf16[128,768]{1,0:T(8,128)(2,1)} %reshape.783.p_ref, ...), custom_call_target="tpu_custom_call" | custom-call | flops 1509949440 | bytes 4718592 | tf_op jit(solution)/shard_map/pallas_call | solution.py:134
  147.6 4.6 collective-permute-done.26
  152.9 9.7 %shard_map.418 = (bf16[32,24,768]{2,1,0:T(8,128)(2,1)}, bf16[32,24,768]{2,1,0:T(8,128)(2,1)}, bf16[32,24,768]{2,1,0:T(8,128)(2,1)}, bf16[32,24,768]{2,1,0:T(8,128)(2,1)}, bf16[32,4,24,768]{3,2,1,0:T(8,128)(2,1)}) custom-call(s32[3]{0:T(128)} %pad_add_fusion.2.here_ref, bf16[16,8,24,768]{3,2,1,0:T(8,128)(2,1)} %constant_dynamic-update-slice_fusion.7.held_ref, ...), custom_call_target="tpu_custom_call" | custom-call | bytes 18874368 | tf_op jit(solution)/shard_map/pallas_call | solution.py:790
  162.6 5.4 shard_map.419
  168.0 4.6 shard_map.420
  174.8 3.2 collective-permute-start.27
  180.1 5.8 %collective-permute-done.28 = bf16[80,768]{1,0:T(8,128)(2,1)S(1)} collective-permute-done((bf16[80,768]{1,0:T(8,128)(2,1)S(1)}, bf16[80,768]{1,0:T(8,128)(2,1)S(1)}, u32[]{:S(2)}, u32[]{:S(2)}) %collective-permute-start.28) | collective-permute-done | bytes 122912 | tf_op jit(solution)/shard_map/ppermute | solution.py:646
  191.8 22.5 %shard_map.421 = (f32[256,768]{1,0:T(8,128)}, f32[256,128]{1,0:T(8,128)}, bf16[256,896]{1,0:T(8,128)(2,1)}) custom-call(s32[2]{0:T(128)} %pad_add_fusion.1.here_ref, bf16[512,768]{1,0:T(8,128)(2,1)} %bitcast.242, bf16[6400,768]{1,0:T(8,128)(2,1)} %get-tuple-element.295.table_ref), custom_call_target="tpu_custom_call" | custom-call | flops 10066329600 | bytes 9830400 | tf_op jit(solution)/shard_map/pallas_call | solution.py:384
  217.2 2.7 shard_map.422
  222.1 2.4 collective-permute-start.37
  225.9 7.9 %collective-permute-done.36.refs_1_ = bf16[64,896]{1,0:T(8,128)(2,1)S(1)} collective-permute-done((bf16[64,896]{1,0:T(8,128)(2,1)}, bf16[64,896]{1,0:T(8,128)(2,1)S(1)}, u32[]{:S(2)}, u32[]{:S(2)}) %collective-permute-start.36) | collective-permute-done | bytes 114720 | tf_op jit(solution)/shard_map/ppermute | solution.py:646
  234.4 3.3 shard_map.423
  240.5 5.6 shard_map.424
  251.0 3.7 shard_map.425
  258.4 4.3 shard_map.426
  265.1 6.7 %shard_map.427 = (f32[128,768]{1,0:T(8,128)}, bf16[128,768]{1,0:T(8,128)(2,1)}, bf16[128,768]{1,0:T(8,128)(2,1)}, f32[8,768]{1,0:T(8,128)}) custom-call(bf16[128,3072]{1,0:T(8,128)(2,1)} %get-tuple-element.372.refs_2_.dpre_ref, f32[128,768]{1,0:T(8,128)} %get-tuple-element.373.dx2_ref, f32[128,768]{1,0:T(8,128)} %get-tuple-element.315.x1_ref, ...), custom_call_target="tpu_custom_call" | custom-call | flops 754974720 | bytes 5898240 | tf_op jit(solution)/shard_map/pallas_call | solution.py:547
  280.6 10.5 %shard_map.428 = (f32[128,768]{1,0:T(8,128)}, bf16[128,768]{1,0:T(8,128)(2,1)}, bf16[128,2304]{1,0:T(8,128)(2,1)}, f32[8,768]{1,0:T(8,128)}) custom-call(bf16[128,768]{1,0:T(8,128)(2,1)} %get-tuple-element.377.mixed_ref, f32[128,768]{1,0:T(8,128)} %get-tuple-element.378.dx1_ref, bf16[128,2304]{1,0:T(8,128)(2,1)} %get-tuple-element.379.packed_ref, ...), custom_call_target="tpu_custom_call" | custom-call | flops 1207959552 | bytes 5898240 | tf_op jit(solution)/shard_map/pallas_call | solution.py:598
  302.6 4.6 shard_map.429
  307.3 3.7 collective-permute-done.59
  315.8 4.7 shard_map.430
  325.1 18.2 %shard_map.431 = (f32[6400,768]{1,0:T(8,128)}, f32[8,128]{1,0:T(8,128)}) custom-call(s32[1]{0:T(128)} %bitcast.1.first_ref, bf16[2048,768]{1,0:T(8,128)(2,1)} %bitcast.192, bf16[6400,768]{1,0:T(8,128)(2,1)} %get-tuple-element.295.table_ref, s32[1,2048]{1,0:T(1,128)} %reshape.815.target_ref, f32[1,2048]{1,0:T(1,128)} %add.458.norm_ref), custom_call_target="tpu_custom_call" | custom-call | flops 12079595520 | bytes 8847360 | tf_op jit(solution)/shard_map/pallas_call | solution.py:933
  349.9 23.3 %shard_map.432 = (f32[6400,768]{1,0:T(8,128)}, f32[8,128]{1,0:T(8,128)}) custom-call(s32[1]{0:T(128)} %bitcast.1.first_ref, bf16[2048,768]{1,0:T(8,128)(2,1)} %bitcast.193, bf16[6400,768]{1,0:T(8,128)(2,1)} %get-tuple-element.295.table_ref, s32[1,2048]{1,0:T(1,128)} %reshape.815.target_ref, ...), custom_call_target="tpu_custom_call", output_to_operand_aliasing={{0}: (5, {})} | custom-call | flops 16106127360 | bytes 11796480 | tf_op jit(solution)/shard_map/pallas_call | solution.py:933
  382.0 2.2 collective-permute-start.71
  386.8 13.4 %shard_map.433 = (f32[6400,768]{1,0:T(8,128)}, f32[8,128]{1,0:T(8,128)}) custom-call(s32[1]{0:T(128)} %bitcast.1.first_ref, bf16[2048,768]{1,0:T(8,128)(2,1)} %bitcast.194, bf16[6400,768]{1,0:T(8,128)(2,1)} %get-tuple-element.295.table_ref, s32[1,2048]{1,0:T(1,128)} %reshape.815.target_ref, ...), custom_call_target="tpu_custom_call", output_to_operand_aliasing={{0}: (5, {})} | custom-call | flops 8053063680 | bytes 5898240 | tf_op jit(solution)/shard_map/pallas_call | solution.py:933
  405.6 2.9 add_add_fusion
  421.0 8.3 %shard_map.434 = (f32[6400,768]{1,0:T(8,128)}, f32[8,128]{1,0:T(8,128)}) custom-call(s32[1]{0:T(128)} %bitcast.1.first_ref, bf16[2048,768]{1,0:T(8,128)(2,1)} %bitcast.195, bf16[6400,768]{1,0:T(8,128)(2,1)} %get-tuple-element.295.table_ref, s32[1,2048]{1,0:T(1,128)} %reshape.815.target_ref, ...), custom_call_target="tpu_custom_call", output_to_operand_aliasing={{0}: (5, {})} | custom-call | flops 4026531840 | bytes 2949120 | tf_op jit(solution)/shard_map/pallas_call | solution.py:933
  430.0 4.7 collective-permute-done.76
  438.5 15.8 %shard_map.435 = (f32[6400,768]{1,0:T(8,128)}, f32[8,128]{1,0:T(8,128)}) custom-call(s32[3]{0:T(128)} %pad_add_fusion.2.here_ref, s32[160]{0:T(256)} %reshape.798.end_ref, s32[2048]{0:T(1024)} %reshape.799.row_ref, s32[2048]{0:T(1024)} %reshape.800.token_ref, f32[6400,768]{1,0:T(8,128)} %get-tuple-element.431.grad_in_ref, ...), custom_call_target="tpu_custom_call", output_to_operand_aliasing={{0}: (4, {})} | custom-call | flops 9830400 | bytes 39321600 | tf_op jit(solution)/shard_map/pallas_call | solution.py:1049
  462.9 5.9 %collective-permute-start.83 = (f32[8,128]{1,0:T(8,128)S(1)}, f32[8,128]{1,0:T(8,128)S(1)}, u32[]{:S(2)}, u32[]{:S(2)}) collective-permute-start(f32[8,128]{1,0:T(8,128)S(1)} %add_add_fusion.6), channel_id=1, source_target_pairs={{0,2},{1,3},{2,0},{3,1},{4,6},{5,7},{6,4},{7,5},{8,10},{9,11},{10,... | collective-permute-start | bytes 12296 | tf_op jit(solution)/shard_map/ppermute | solution.py:646
  468.8 3.1 collective-permute-start.84
  473.4 3.8 collective-permute-done.85
  477.8 14.2 %shard_map.436 = (f32[24,2304]{1,0:T(8,128)}, f32[24,2304]{1,0:T(8,128)}, f32[24,2304]{1,0:T(8,128)}, f32[24,768]{1,0:T(8,128)}, f32[24,768]{1,0:T(8,128)}, /*in...) custom-call(s32[1]{0:T(128)} %bitcast.3.dp_ref.here_ref, ...), custom_call_target="tpu_custom_call" | custom-call | flops 24330240 | bytes 19464192 | tf_op jit(solution)/shard_map/pallas_call | solution.py:1146
  498.7 2.3 collective-permute-done.89
  503.0 2.4 collective-permute-start.92
  509.7 55.0 %shard_map.437 = (f32[6288,768]{1,0:T(8,128)}, f32[6288,768]{1,0:T(8,128)}, f32[6288,768]{1,0:T(8,128)}, f32[24,2304]{1,0:T(8,128)}, f32[24,768]{1,0:T(8,128)}, ...) custom-call(f32[8,128]{1,0:T(8,128)} %add_add_fusion.5.sums_ref, ...), custom_call_target="tpu_custom_call" | custom-call | flops 96583680 | bytes 135217152 | tf_op jit(solution)/shard_map/pallas_call | solution.py:1194
  (435 shorter events, 183.1 us)
Async XLA Ops:
  5.9 11.9 %collective-permute-start.1 = (bf16[1,24,3328]{2,1,0:T(8,128)(2,1)S(1)}, bf16[1,24,3328]{2,1,0:T(8,128)(2,1)S(1)}, u32[]{:S(2)}, u32[]{:S(2)}) collective-permute-start(bf16[1,24,3328]{2,1,0:T(8,128)(2,1)S(1)} %get-tuple-element.489), channel_id=1, source_target_pairs={{0,4},{1,5},{2,6},{3,7},{4,0},{5,1},{6,2},{7,3},{8,12},{9,13},{10,... | collective-permute-start | bytes 479240 | tf_op jit(solution)/shard_map/ppermute | solution.py:646
  31.3 21.6 %collective-permute-start.6 = (bf16[4,24,3328]{2,1,0:T(8,128)(2,1)S(1)}, bf16[4,24,3328]{2,1,0:T(8,128)(2,1)}, u32[]{:S(2)}, u32[]{:S(2)}) collective-permute-start(bf16[4,24,3328]{2,1,0:T(8,128)(2,1)S(1)} %bitcast.223), channel_id=1, source_target_pairs={{0,8},{8,0},{16,24},{24,16},{1,9},{9,1},{17,25},{25,17},{2,10},{10... | collective-permute-start | bytes 1916936 | tf_op jit(solution)/shard_map/ppermute | solution.py:651
  32.9 20.0 %collective-permute-start.7 = (bf16[4,24,3328]{2,1,0:T(8,128)(2,1)S(1)}, bf16[4,24,3328]{2,1,0:T(8,128)(2,1)}, u32[]{:S(2)}, u32[]{:S(2)}) collective-permute-start(bf16[4,24,3328]{2,1,0:T(8,128)(2,1)S(1)} %bitcast.224), channel_id=1, source_target_pairs={{0,16},{8,24},{16,0},{24,8},{1,17},{9,25},{17,1},{25,9},{2,18},{10... | collective-permute-start | bytes 1916936 | tf_op jit(solution)/shard_map/ppermute | solution.py:651
  35.3 15.7 %collective-permute-start.8 = (bf16[1,8,24,768]{3,2,1,0:T(8,128)(2,1)S(1)}, bf16[1,8,24,768]{3,2,1,0:T(8,128)(2,1)}, u32[]{:S(2)}, u32[]{:S(2)}) collective-permute-start(bf16[1,8,24,768]{3,2,1,0:T(8,128)(2,1)S(1)} %maximum_bitcast_fusion.3), channel_id=1, source_target_pairs={{0,4},{1,5},{2,6},{3,7},{4,0},{5,1},{6,2},{7,3},{8,12},{9,13},{10,... | collective-permute-start | bytes 884744 | tf_op jit(solution)/shard_map/ppermute | solution.py:646
  53.0 13.6 %collective-permute-start.9 = (bf16[4,192,768]{2,1,0:T(8,128)(2,1)S(1)}, bf16[4,192,768]{2,1,0:T(8,128)(2,1)S(1)}, u32[]{:S(2)}, u32[]{:S(2)}) collective-permute-start(bf16[4,192,768]{2,1,0:T(8,128)(2,1)S(1)} %dynamic-slice_bitcast_fusion), channel_id=1, source_target_pairs={{0,1},{1,0},{2,3},{3,2},{4,5},{5,4},{6,7},{7,6},{8,9},{9,8},{10,11... | collective-permute-start | bytes 3538952 | tf_op jit(solution)/shard_map/ppermute | solution.py:641
  66.7 25.6 %collective-permute-start.13 = (bf16[16,24,3328]{2,1,0:T(8,128)(2,1)}, bf16[16,24,3328]{2,1,0:T(8,128)(2,1)}, u32[]{:S(2)}, u32[]{:S(2)}) collective-permute-start(bf16[16,24,3328]{2,1,0:T(8,128)(2,1)} %constant_dynamic-update-slice_fusion.2.held_ref), channel_id=1, source_target_pairs={{0,1},{1,0},{2,3},{3,2},{4,5},{5,4},{6,7},{7,6},{8,9},{9,8},{10,11... | collective-permute-start | bytes 7667720 | tf_op jit(solution)/shard_map/ppermute | solution.py:641
  67.8 17.3 %collective-permute-start.12 = (bf16[2,128,768]{2,1,0:T(8,128)(2,1)}, bf16[2,128,768]{2,1,0:T(8,128)(2,1)}, u32[]{:S(2)}, u32[]{:S(2)}) collective-permute-start(bf16[2,128,768]{2,1,0:T(8,128)(2,1)} %fusion.2), channel_id=1, source_target_pairs={{0,2},{1,3},{2,0},{3,1},{4,6},{5,7},{6,4},{7,5},{8,10},{9,11},{10,... | collective-permute-start | bytes 1179656 | tf_op jit(solution)/shard_map/ppermute | solution.py:646
  70.1 22.0 %collective-permute-start.14 = (bf16[2,8,24,768]{3,2,1,0:T(8,128)(2,1)S(1)}, bf16[2,8,24,768]{3,2,1,0:T(8,128)(2,1)S(1)}, u32[]{:S(2)}, u32[]{:S(2)}) collective-permute-start(bf16[2,8,24,768]{3,2,1,0:T(8,128)(2,1)S(1)} %copy-done.3), channel_id=1, source_target_pairs={{0,2},{1,3},{2,0},{3,1},{4,6},{5,7},{6,4},{7,5},{8,10},{9,11},{10,... | collective-permute-start | bytes 1769480 | tf_op jit(solution)/shard_map/ppermute | solution.py:646
  92.2 27.7 %collective-permute-start.16 = (bf16[4,8,24,768]{3,2,1,0:T(8,128)(2,1)S(1)}, bf16[4,8,24,768]{3,2,1,0:T(8,128)(2,1)}, u32[]{:S(2)}, u32[]{:S(2)}) collective-permute-start(bf16[4,8,24,768]{3,2,1,0:T(8,128)(2,1)S(1)} %bitcast.211), channel_id=1, source_target_pairs={{0,8},{8,0},{16,24},{24,16},{1,9},{9,1},{17,25},{25,17},{2,10},{10... | collective-permute-start | bytes 3538952 | tf_op jit(solution)/shard_map/ppermute | solution.py:651
  93.3 27.3 %collective-permute-start.17 = (bf16[4,8,24,768]{3,2,1,0:T(8,128)(2,1)S(1)}, bf16[4,8,24,768]{3,2,1,0:T(8,128)(2,1)S(1)}, u32[]{:S(2)}, u32[]{:S(2)}) collective-permute-start(bf16[4,8,24,768]{3,2,1,0:T(8,128)(2,1)S(1)} %bitcast.212), channel_id=1, source_target_pairs={{0,16},{8,24},{16,0},{24,8},{1,17},{9,25},{17,1},{25,9},{2,18},{10... | collective-permute-start | bytes 3538952 | tf_op jit(solution)/shard_map/ppermute | solution.py:651
  120.6 16.6 %collective-permute-start.20 = (bf16[2,64,768]{2,1,0:T(8,128)(2,1)}, bf16[2,64,768]{2,1,0:T(8,128)(2,1)S(1)}, u32[]{:S(2)}, u32[]{:S(2)}) collective-permute-start(bf16[2,64,768]{2,1,0:T(8,128)(2,1)} %fusion.13), channel_id=1, source_target_pairs={{0,2},{1,3},{2,0},{3,1},{4,6},{5,7},{6,4},{7,5},{8,10},{9,11},{10,... | collective-permute-start | bytes 589832 | tf_op jit(solution)/shard_map/ppermute | solution.py:646
  123.4 13.8 %collective-permute-start.18 = (bf16[2,8,24,768]{3,2,1,0:T(8,128)(2,1)S(1)}, bf16[2,8,24,768]{3,2,1,0:T(8,128)(2,1)S(1)}, u32[]{:S(2)}, u32[]{:S(2)}) collective-permute-start(bf16[2,8,24,768]{3,2,1,0:T(8,128)(2,1)S(1)} %slice.284), channel_id=1, source_target_pairs={{0,8},{8,0},{16,24},{24,16},{1,9},{9,1},{17,25},{25,17},{2,10},{10... | collective-permute-start | bytes 1769480 | tf_op jit(solution)/shard_map/ppermute | solution.py:651
  124.5 13.6 %collective-permute-start.19 = (bf16[2,8,24,768]{3,2,1,0:T(8,128)(2,1)S(1)}, bf16[2,8,24,768]{3,2,1,0:T(8,128)(2,1)S(1)}, u32[]{:S(2)}, u32[]{:S(2)}) collective-permute-start(bf16[2,8,24,768]{3,2,1,0:T(8,128)(2,1)S(1)} %slice.285), channel_id=1, source_target_pairs={{0,16},{8,24},{16,0},{24,8},{1,17},{9,25},{17,1},{25,9},{2,18},{10... | collective-permute-start | bytes 1769480 | tf_op jit(solution)/shard_map/ppermute | solution.py:651
  139.0 13.9 %collective-permute-start.21 = (bf16[16,8,24,768]{3,2,1,0:T(8,128)(2,1)}, bf16[16,8,24,768]{3,2,1,0:T(8,128)(2,1)}, u32[]{:S(2)}, u32[]{:S(2)}) collective-permute-start(bf16[16,8,24,768]{3,2,1,0:T(8,128)(2,1)} %constant_dynamic-update-slice_fusion.7.held_ref), channel_id=1, source_target_pairs={{0,1},{1,0},{2,3},{3,2},{4,5},{5,4},{6,7},{7,6},{8,9},{9,8},{10,11... | collective-permute-start | bytes 14155784 | tf_op jit(solution)/shard_map/ppermute | solution.py:641
  146.0 27.4 %collective-permute-start.25 = (bf16[128,1152]{1,0:T(8,128)(2,1)S(1)}, bf16[128,1152]{1,0:T(8,128)(2,1)S(1)}, u32[]{:S(2)}, u32[]{:S(2)}) collective-permute-start(bf16[128,1152]{1,0:T(8,128)(2,1)S(1)} %copy-done.41), channel_id=1, source_target_pairs={{0,1},{1,0},{2,3},{3,2},{4,5},{5,4},{6,7},{7,6},{8,9},{9,8},{10,11... | collective-permute-start | bytes 884744 | tf_op jit(solution)/shard_map/ppermute | solution.py:641
  173.5 12.4 %collective-permute-start.28 = (bf16[80,768]{1,0:T(8,128)(2,1)S(1)}, bf16[80,768]{1,0:T(8,128)(2,1)S(1)}, u32[]{:S(2)}, u32[]{:S(2)}) collective-permute-start(bf16[80,768]{1,0:T(8,128)(2,1)S(1)} %pad_maximum_fusion.7), channel_id=1, source_target_pairs={{0,4},{1,5},{2,6},{3,7},{4,0},{5,1},{6,2},{7,3},{8,12},{9,13},{10,... | collective-permute-start | bytes 368648 | tf_op jit(solution)/shard_map/ppermute | solution.py:646
  189.3 25.0 %collective-permute-start.32 = (bf16[4,64,768]{2,1,0:T(8,128)(2,1)S(1)}, bf16[4,64,768]{2,1,0:T(8,128)(2,1)S(1)}, u32[]{:S(2)}, u32[]{:S(2)}) collective-permute-start(bf16[4,64,768]{2,1,0:T(8,128)(2,1)S(1)} %slice.289), channel_id=1, source_target_pairs={{0,8},{8,0},{16,24},{24,16},{1,9},{9,1},{17,25},{25,17},{2,10},{10... | collective-permute-start | bytes 1179656 | tf_op jit(solution)/shard_map/ppermute | solution.py:651
  190.3 24.1 %collective-permute-start.33 = (bf16[4,64,768]{2,1,0:T(8,128)(2,1)S(1)}, bf16[4,64,768]{2,1,0:T(8,128)(2,1)S(1)}, u32[]{:S(2)}, u32[]{:S(2)}) collective-permute-start(bf16[4,64,768]{2,1,0:T(8,128)(2,1)S(1)} %slice.289), channel_id=1, source_target_pairs={{0,16},{8,24},{16,0},{24,8},{1,17},{9,25},{17,1},{25,9},{2,18},{10... | collective-permute-start | bytes 1179656 | tf_op jit(solution)/shard_map/ppermute | solution.py:651
  254.8 17.1 %collective-permute-start.46 = (f32[8,2,64]{2,1,0:T(2,128)S(1)}, f32[8,2,64]{2,1,0:T(2,128)S(1)}, u32[]{:S(2)}, u32[]{:S(2)}) collective-permute-start(f32[8,2,64]{2,1,0:T(2,128)S(1)} %pad_maximum_fusion.10), channel_id=1, source_target_pairs={{0,24},{8,16},{16,8},{24,0},{1,25},{9,17},{17,9},{25,1},{2,26},{10... | collective-permute-start | bytes 12296 | tf_op jit(solution)/shard_map/ppermute | solution.py:651
  256.8 15.1 %collective-permute-start.47 = (f32[8,2,64]{2,1,0:T(2,128)S(1)}, f32[8,2,64]{2,1,0:T(2,128)S(1)}, u32[]{:S(2)}, u32[]{:S(2)}) collective-permute-start(f32[8,2,64]{2,1,0:T(2,128)S(1)} %pad_maximum_fusion.10), channel_id=1, source_target_pairs={{0,16},{8,24},{16,0},{24,8},{1,17},{9,25},{17,1},{25,9},{2,18},{10... | collective-permute-start | bytes 12296 | tf_op jit(solution)/shard_map/ppermute | solution.py:651
  257.3 14.6 %collective-permute-start.48 = (f32[8,2,64]{2,1,0:T(2,128)S(1)}, f32[8,2,64]{2,1,0:T(2,128)S(1)}, u32[]{:S(2)}, u32[]{:S(2)}) collective-permute-start(f32[8,2,64]{2,1,0:T(2,128)S(1)} %pad_maximum_fusion.10), channel_id=1, source_target_pairs={{0,8},{8,0},{16,24},{24,16},{1,9},{9,1},{17,25},{25,17},{2,10},{10... | collective-permute-start | bytes 12296 | tf_op jit(solution)/shard_map/ppermute | solution.py:651
  273.5 19.3 %collective-permute-start.54 = (bf16[16,64,768]{2,1,0:T(8,128)(2,1)S(1)}, bf16[16,64,768]{2,1,0:T(8,128)(2,1)}, u32[]{:S(2)}, u32[]{:S(2)}) collective-permute-start(bf16[16,64,768]{2,1,0:T(8,128)(2,1)S(1)} %constant_dynamic-update-slice_fusion.12.held_ref), channel_id=1, source_target_pairs={{0,1},{1,0},{2,3},{3,2},{4,5},{5,4},{6,7},{7,6},{8,9},{9,8},{10,11... | collective-permute-start | bytes 4718600 | tf_op jit(solution)/shard_map/ppermute | solution.py:641
  273.5 17.5 %collective-permute-start.51 = (bf16[4,96,768]{2,1,0:T(8,128)(2,1)S(1)}, bf16[4,96,768]{2,1,0:T(8,128)(2,1)S(1)}, u32[]{:S(2)}, u32[]{:S(2)}) collective-permute-start(bf16[4,96,768]{2,1,0:T(8,128)(2,1)S(1)} %fusion.6), channel_id=1, source_target_pairs={{0,8},{8,0},{16,24},{24,16},{1,9},{9,1},{17,25},{25,17},{2,10},{10... | collective-permute-start | bytes 1769480 | tf_op jit(solution)/shard_map/ppermute | solution.py:651
  274.6 16.5 %collective-permute-start.52 = (bf16[4,96,768]{2,1,0:T(8,128)(2,1)}, bf16[4,96,768]{2,1,0:T(8,128)(2,1)}, u32[]{:S(2)}, u32[]{:S(2)}) collective-permute-start(bf16[4,96,768]{2,1,0:T(8,128)(2,1)} %fusion.7), channel_id=1, source_target_pairs={{0,16},{8,24},{16,0},{24,8},{1,17},{9,25},{17,1},{25,9},{2,18},{10... | collective-permute-start | bytes 1769480 | tf_op jit(solution)/shard_map/ppermute | solution.py:651
  280.6 12.2 %collective-permute-start.53 = (bf16[128,768]{1,0:T(8,128)(2,1)S(1)}, bf16[128,768]{1,0:T(8,128)(2,1)S(1)}, u32[]{:S(2)}, u32[]{:S(2)}) collective-permute-start(bf16[128,768]{1,0:T(8,128)(2,1)S(1)} %copy-done.19), channel_id=1, source_target_pairs={{0,1},{1,0},{2,3},{3,2},{4,5},{5,4},{6,7},{7,6},{8,9},{9,8},{10,11... | collective-permute-start | bytes 589832 | tf_op jit(solution)/shard_map/ppermute | solution.py:641
  298.8 12.3 %collective-permute-start.59 = (bf16[1,128,768]{2,1,0:T(8,128)(2,1)S(1)}, bf16[1,128,768]{2,1,0:T(8,128)(2,1)S(1)}, u32[]{:S(2)}, u32[]{:S(2)}) collective-permute-start(bf16[1,128,768]{2,1,0:T(8,128)(2,1)S(1)} %bitcast.259), channel_id=1, source_target_pairs={{0,4},{1,5},{2,6},{3,7},{4,0},{5,1},{6,2},{7,3},{8,12},{9,13},{10,... | collective-permute-start | bytes 589832 | tf_op jit(solution)/shard_map/ppermute | solution.py:646
  300.1 11.8 %collective-permute-start.57 = (bf16[2,24,3072]{2,1,0:T(8,128)(2,1)}, bf16[2,24,3072]{2,1,0:T(8,128)(2,1)}, u32[]{:S(2)}, u32[]{:S(2)}) collective-permute-start(bf16[2,24,3072]{2,1,0:T(8,128)(2,1)} %bitcast.269), channel_id=1, source_target_pairs={{0,8},{8,0},{16,24},{24,16},{1,9},{9,1},{17,25},{25,17},{2,10},{10... | collective-permute-start | bytes 884744 | tf_op jit(solution)/shard_map/ppermute | solution.py:651
  301.1 11.9 %collective-permute-start.56 = (bf16[2,24,3072]{2,1,0:T(8,128)(2,1)}, bf16[2,24,3072]{2,1,0:T(8,128)(2,1)}, u32[]{:S(2)}, u32[]{:S(2)}) collective-permute-start(bf16[2,24,3072]{2,1,0:T(8,128)(2,1)} %bitcast.268), channel_id=1, source_target_pairs={{0,16},{8,24},{16,0},{24,8},{1,17},{9,25},{17,1},{25,9},{2,18},{10... | collective-permute-start | bytes 884744 | tf_op jit(solution)/shard_map/ppermute | solution.py:651
  302.6 12.3 %collective-permute-start.55 = (bf16[128,2304]{1,0:T(8,128)(2,1)S(1)}, bf16[128,2304]{1,0:T(8,128)(2,1)S(1)}, u32[]{:S(2)}, u32[]{:S(2)}) collective-permute-start(bf16[128,2304]{1,0:T(8,128)(2,1)S(1)} %copy-done.15), channel_id=1, source_target_pairs={{0,1},{1,0},{2,3},{3,2},{4,5},{5,4},{6,7},{7,6},{8,9},{9,8},{10,11... | collective-permute-start | bytes 1769480 | tf_op jit(solution)/shard_map/ppermute | solution.py:641
  320.5 22.8 %collective-permute-start.63 = (bf16[2,96,768]{2,1,0:T(8,128)(2,1)S(1)}, bf16[2,96,768]{2,1,0:T(8,128)(2,1)S(1)}, u32[]{:S(2)}, u32[]{:S(2)}) collective-permute-start(bf16[2,96,768]{2,1,0:T(8,128)(2,1)S(1)} %fusion.10), channel_id=1, source_target_pairs={{0,2},{1,3},{2,0},{3,1},{4,6},{5,7},{6,4},{7,5},{8,10},{9,11},{10,... | collective-permute-start | bytes 884744 | tf_op jit(solution)/shard_map/ppermute | solution.py:646
  320.5 23.6 %collective-permute-start.62 = (bf16[2,128,768]{2,1,0:T(8,128)(2,1)S(1)}, bf16[2,128,768]{2,1,0:T(8,128)(2,1)S(1)}, u32[]{:S(2)}, u32[]{:S(2)}) collective-permute-start(bf16[2,128,768]{2,1,0:T(8,128)(2,1)S(1)} %maximum_bitcast_fusion.1), channel_id=1, source_target_pairs={{0,2},{1,3},{2,0},{3,1},{4,6},{5,7},{6,4},{7,5},{8,10},{9,11},{10,... | collective-permute-start | bytes 1179656 | tf_op jit(solution)/shard_map/ppermute | solution.py:646
  322.5 21.7 %collective-permute-start.60 = (bf16[4,24,3072]{2,1,0:T(8,128)(2,1)}, bf16[4,24,3072]{2,1,0:T(8,128)(2,1)S(1)}, u32[]{:S(2)}, u32[]{:S(2)}) collective-permute-start(bf16[4,24,3072]{2,1,0:T(8,128)(2,1)} %fusion.8), channel_id=1, source_target_pairs={{0,8},{8,0},{16,24},{24,16},{1,9},{9,1},{17,25},{25,17},{2,10},{10... | collective-permute-start | bytes 1769480 | tf_op jit(solution)/shard_map/ppermute | solution.py:651
  323.5 20.8 %collective-permute-start.61 = (bf16[4,24,3072]{2,1,0:T(8,128)(2,1)S(1)}, bf16[4,24,3072]{2,1,0:T(8,128)(2,1)S(1)}, u32[]{:S(2)}, u32[]{:S(2)}) collective-permute-start(bf16[4,24,3072]{2,1,0:T(8,128)(2,1)S(1)} %copy-done.37), channel_id=1, source_target_pairs={{0,16},{8,24},{16,0},{24,8},{1,17},{9,25},{17,1},{25,9},{2,18},{10... | collective-permute-start | bytes 1769480 | tf_op jit(solution)/shard_map/ppermute | solution.py:651
  345.6 32.0 %collective-permute-start.66 = (bf16[4,128,768]{2,1,0:T(8,128)(2,1)S(1)}, bf16[4,128,768]{2,1,0:T(8,128)(2,1)}, u32[]{:S(2)}, u32[]{:S(2)}) collective-permute-start(bf16[4,128,768]{2,1,0:T(8,128)(2,1)S(1)} %bitcast.218), channel_id=1, source_target_pairs={{0,8},{8,0},{16,24},{24,16},{1,9},{9,1},{17,25},{25,17},{2,10},{10... | collective-permute-start | bytes 2359304 | tf_op jit(solution)/shard_map/ppermute | solution.py:651
  346.7 30.9 %collective-permute-start.67 = (bf16[4,128,768]{2,1,0:T(8,128)(2,1)S(1)}, bf16[4,128,768]{2,1,0:T(8,128)(2,1)}, u32[]{:S(2)}, u32[]{:S(2)}) collective-permute-start(bf16[4,128,768]{2,1,0:T(8,128)(2,1)S(1)} %bitcast.219), channel_id=1, source_target_pairs={{0,16},{8,24},{16,0},{24,8},{1,17},{9,25},{17,1},{25,9},{2,18},{10... | collective-permute-start | bytes 2359304 | tf_op jit(solution)/shard_map/ppermute | solution.py:651
  347.3 26.0 %collective-permute-start.68 = (bf16[2,24,3072]{2,1,0:T(8,128)(2,1)S(1)}, bf16[2,24,3072]{2,1,0:T(8,128)(2,1)}, u32[]{:S(2)}, u32[]{:S(2)}) collective-permute-start(bf16[2,24,3072]{2,1,0:T(8,128)(2,1)S(1)} %fusion.11), channel_id=1, source_target_pairs={{0,2},{1,3},{2,0},{3,1},{4,6},{5,7},{6,4},{7,5},{8,10},{9,11},{10,... | collective-permute-start | bytes 884744 | tf_op jit(solution)/shard_map/ppermute | solution.py:646
  347.4 27.7 %collective-permute-start.65 = (bf16[2,24,3328]{2,1,0:T(8,128)(2,1)}, bf16[2,24,3328]{2,1,0:T(8,128)(2,1)}, u32[]{:S(2)}, u32[]{:S(2)}) collective-permute-start(bf16[2,24,3328]{2,1,0:T(8,128)(2,1)} %bitcast.95), channel_id=1, source_target_pairs={{0,8},{8,0},{16,24},{24,16},{1,9},{9,1},{17,25},{25,17},{2,10},{10... | collective-permute-start | bytes 958472 | tf_op jit(solution)/shard_map/ppermute | solution.py:651
  348.4 28.4 %collective-permute-start.64 = (bf16[2,24,3328]{2,1,0:T(8,128)(2,1)}, bf16[2,24,3328]{2,1,0:T(8,128)(2,1)S(1)}, u32[]{:S(2)}, u32[]{:S(2)}) collective-permute-start(bf16[2,24,3328]{2,1,0:T(8,128)(2,1)} %bitcast.96), channel_id=1, source_target_pairs={{0,16},{8,24},{16,0},{24,8},{1,17},{9,25},{17,1},{25,9},{2,18},{10... | collective-permute-start | bytes 958472 | tf_op jit(solution)/shard_map/ppermute | solution.py:651
  380.4 23.1 %collective-permute-start.72 = (bf16[2,128,768]{2,1,0:T(8,128)(2,1)}, bf16[2,128,768]{2,1,0:T(8,128)(2,1)}, u32[]{:S(2)}, u32[]{:S(2)}) collective-permute-start(bf16[2,128,768]{2,1,0:T(8,128)(2,1)} %slice.296), channel_id=1, source_target_pairs={{0,8},{8,0},{16,24},{24,16},{1,9},{9,1},{17,25},{25,17},{2,10},{10... | collective-permute-start | bytes 1179656 | tf_op jit(solution)/shard_map/ppermute | solution.py:651
  381.5 23.0 %collective-permute-start.73 = (bf16[2,128,768]{2,1,0:T(8,128)(2,1)S(1)}, bf16[2,128,768]{2,1,0:T(8,128)(2,1)}, u32[]{:S(2)}, u32[]{:S(2)}) collective-permute-start(bf16[2,128,768]{2,1,0:T(8,128)(2,1)S(1)} %slice.297), channel_id=1, source_target_pairs={{0,16},{8,24},{16,0},{24,8},{1,17},{9,25},{17,1},{25,9},{2,18},{10... | collective-permute-start | bytes 1179656 | tf_op jit(solution)/shard_map/ppermute | solution.py:651
  382.0 20.7 %collective-permute-start.71 = (bf16[1,24,3072]{2,1,0:T(8,128)(2,1)}, bf16[1,24,3072]{2,1,0:T(8,128)(2,1)S(1)}, u32[]{:S(2)}, u32[]{:S(2)}) collective-permute-start(bf16[1,24,3072]{2,1,0:T(8,128)(2,1)} %dynamic-slice_convert_fusion.6), channel_id=1, source_target_pairs={{0,4},{1,5},{2,6},{3,7},{4,0},{5,1},{6,2},{7,3},{8,12},{9,13},{10,... | collective-permute-start | bytes 442376 | tf_op jit(solution)/shard_map/ppermute | solution.py:646
  384.3 21.3 %collective-permute-start.69 = (bf16[4,24,3328]{2,1,0:T(8,128)(2,1)}, bf16[4,24,3328]{2,1,0:T(8,128)(2,1)S(1)}, u32[]{:S(2)}, u32[]{:S(2)}) collective-permute-start(bf16[4,24,3328]{2,1,0:T(8,128)(2,1)} %fusion.3), channel_id=1, source_target_pairs={{0,8},{8,0},{16,24},{24,16},{1,9},{9,1},{17,25},{25,17},{2,10},{10... | collective-permute-start | bytes 1916936 | tf_op jit(solution)/shard_map/ppermute | solution.py:651
  385.2 20.3 %collective-permute-start.70 = (bf16[4,24,3328]{2,1,0:T(8,128)(2,1)}, bf16[4,24,3328]{2,1,0:T(8,128)(2,1)}, u32[]{:S(2)}, u32[]{:S(2)}) collective-permute-start(bf16[4,24,3328]{2,1,0:T(8,128)(2,1)} %fusion.4), channel_id=1, source_target_pairs={{0,16},{8,24},{16,0},{24,8},{1,17},{9,25},{17,1},{25,9},{2,18},{10... | collective-permute-start | bytes 1916936 | tf_op jit(solution)/shard_map/ppermute | solution.py:651
  408.5 30.0 %collective-permute-start.74 = (bf16[16,128,768]{2,1,0:T(8,128)(2,1)S(1)}, bf16[16,128,768]{2,1,0:T(8,128)(2,1)}, u32[]{:S(2)}, u32[]{:S(2)}) collective-permute-start(bf16[16,128,768]{2,1,0:T(8,128)(2,1)S(1)} %constant_dynamic-update-slice_fusion.17.held_ref), channel_id=1, source_target_pairs={{0,1},{1,0},{2,3},{3,2},{4,5},{5,4},{6,7},{7,6},{8,9},{9,8},{10,11... | collective-permute-start | bytes 9437192 | tf_op jit(solution)/shard_map/ppermute | solution.py:641
  414.5 14.7 %collective-permute-start.78 = (bf16[1,96,768]{2,1,0:T(8,128)(2,1)S(1)}, bf16[1,96,768]{2,1,0:T(8,128)(2,1)S(1)}, u32[]{:S(2)}, u32[]{:S(2)}) collective-permute-start(bf16[1,96,768]{2,1,0:T(8,128)(2,1)S(1)} %dynamic-slice_convert_fusion.5), channel_id=1, source_target_pairs={{0,4},{1,5},{2,6},{3,7},{4,0},{5,1},{6,2},{7,3},{8,12},{9,13},{10,... | collective-permute-start | bytes 442376 | tf_op jit(solution)/shard_map/ppermute | solution.py:646
  416.5 13.5 %collective-permute-start.75 = (bf16[24,3328]{1,0:T(8,128)(2,1)S(1)}, bf16[24,3328]{1,0:T(8,128)(2,1)S(1)}, u32[]{:S(2)}, u32[]{:S(2)}) collective-permute-start(bf16[24,3328]{1,0:T(8,128)(2,1)S(1)} %get-tuple-element.434), channel_id=1, source_target_pairs={{0,2},{1,3},{2,0},{3,1},{4,6},{5,7},{6,4},{7,5},{8,10},{9,11},{10,... | collective-permute-start | bytes 479240 | tf_op jit(solution)/shard_map/ppermute | solution.py:646
  418.5 16.3 %collective-permute-start.76 = (bf16[24,3328]{1,0:T(8,128)(2,1)S(1)}, bf16[24,3328]{1,0:T(8,128)(2,1)S(1)}, u32[]{:S(2)}, u32[]{:S(2)}) collective-permute-start(bf16[24,3328]{1,0:T(8,128)(2,1)S(1)} %get-tuple-element.435), channel_id=1, source_target_pairs={{0,4},{1,5},{2,6},{3,7},{4,0},{5,1},{6,2},{7,3},{8,12},{9,13},{10,... | collective-permute-start | bytes 479240 | tf_op jit(solution)/shard_map/ppermute | solution.py:646
  418.9 15.9 %collective-permute-start.77 = (bf16[24,3328]{1,0:T(8,128)(2,1)S(1)}, bf16[24,3328]{1,0:T(8,128)(2,1)S(1)}, u32[]{:S(2)}, u32[]{:S(2)}) collective-permute-start(bf16[24,3328]{1,0:T(8,128)(2,1)S(1)} %get-tuple-element.436), channel_id=1, source_target_pairs={{0,6},{1,7},{2,4},{3,5},{4,2},{5,3},{6,0},{7,1},{8,14},{9,15},{10,... | collective-permute-start | bytes 479240 | tf_op jit(solution)/shard_map/ppermute | solution.py:646
  (90 other events, 650.3 us)

commit v4 on v3

--- a/solution.py
+++ b/solution.py
@@ -263,10 +263,10 @@
         def put(made, span):
             own, one, two, three = [made(place) for place in range(4)]
             out_refs[0][:, span] = own
-            out_refs[1][:, span] = one.astype(low)
-            out_refs[2][:, span] = two.astype(low)
-            out_refs[3][:, span] = one[half:]
-            out_refs[4][:, span] = two[:half]
+            out_refs[1][:, span] = one[:half].astype(low)
+            out_refs[2][:, span] = one[half:]
+            out_refs[3][:, span] = two[:half]
+            out_refs[4][:, span] = two[half:].astype(low)
             out_refs[5][:, span] = three[:half].astype(low)
             out_refs[6][:, span] = three[half:].astype(low)
 
@@ -287,8 +287,8 @@
         if smalls is not None:
             put(lambda place: in_refs[-1][place], slice(start, total))
 
-    out = [shape_of((rows, total), jnp.float32)] + [shape_of((rows, total), low)] * 2
-    out += [shape_of((half, total), jnp.float32)] * 2 + [shape_of((half, total), low)] * 2
+    out = [shape_of((rows, total), jnp.float32)]
+    out += [shape_of((half, total), kind) for kind in (low, jnp.float32, jnp.float32, low, low, low)]
     flops = sum(4 * left[0].shape[0] * 4 * rows * right[0].shape[1] for left, right in zip(lefts, rights))
     made = pl.pallas_call(
         body,
@@ -1164,7 +1164,7 @@
 def write_updates(sums, norms, smalls, table_set):
     weight, gradient, first, second = table_set
     rows, width = weight.shape
-    tile = table_tile(rows, lax.axis_size("dp"))
+    tile = 2 * table_tile(rows, lax.axis_size("dp"))
     steps = -(-rows // tile)
     number = len(smalls)
 
@@ -1230,16 +1230,15 @@
 
 
 def scatter_first(parts, slots):
-    own, one, two, one_upper, two_lower, first, second = parts
-    half = first.shape[0]
+    own, one_lower, one_upper, two_lower, two_upper, first, second = parts
     low = jnp.bfloat16
     first, second = slots.open((first, second))
     into_two = swap_dp(first, 1).astype(jnp.float32)
     into_one = swap_dp(second, 2).astype(jnp.float32)
     return (
         own,
-        one.at[half:].set((one_upper + into_one).astype(low)),
-        two.at[:half].set((two_lower + into_two).astype(low)),
+        jnp.concatenate([one_lower, (one_upper + into_one).astype(low)], axis=0),
+        jnp.concatenate([(two_lower + into_two).astype(low), two_upper], axis=0),
     )
 
 
@@ -1380,7 +1379,14 @@
     sent = jnp.concatenate([picked, jnp.pad(tail_rows, ((0, 13), (0, 0)))], axis=0)
     same_core = jnp.stack(outer_parts(slots.open(sent)))
     act_got = swap_core(slots.open(act_sent))
-    slots.close(same_core, act_got)
+    counts, row_list, token_list = token_lists(
+        slots.open(packed_all)[:, :seq_len],
+        vocab_start,
+        vocab_rows,
+        4 * seq_len // shard_count,
+        table_low.shape[0] // CHUNK,
+    )
+    slots.close(same_core, act_got, counts, row_list, token_list)
 
     ordered = jnp.stack(xor_order([same_core[step] for step in range(outer_count)], outer))
     head_in = jnp.stack(xor_order([ordered, swap_core(slots.open(ordered))], core), axis=1)
@@ -1461,14 +1467,6 @@
     norm_all = (stats_all[:, :, 0].reshape(1, -1) + math.log(token_count)).astype(jnp.float32)
     loss = jnp.sum(stats_all[:, :, 1]) / token_count
     targets_all = packed_all[:, seq_len:].reshape(1, -1)
-    counts, row_list, token_list = token_lists(
-        packed_all[:, :seq_len],
-        vocab_start,
-        vocab_rows,
-        4 * seq_len // shard_count,
-        table_low.shape[0] // CHUNK,
-    )
-
     vec_grad = jnp.concatenate(
         [
             vec_first[0:2],

time: 579 us -> 571 us (0.986)
    scatter x6 -> x0, other arithmetic: 6.4 us -> none  [the longest x3 3.59 us: scatter_first(): two.at[:half].set((two_lower + into_two).astype(low))]
    unnamed x109 -> x113, local copies, waits for them, and re-layouts: 19.8 us -> 20.1 us
  transfers between devices with their start and end apart: 93 -> 93, of which waited for: 31 -> 30; matrix products, arithmetic and copies ran while one was open for 16% -> 16% of each run, Pallas kernels for 30% -> 30%
where the time goes in v4:
time: 571 us; the launch traced here: 561 us
  Pallas kernels  266 us (47%)
  starting transfers between devices  99.4 us (17%)
  waiting for transfers between devices  79.9 us (14%)
  local copies, waits for them, and re-layouts  70.9 us (12%)
  other arithmetic  39.3 us (7%)
  between operations  5.98 us (1%)
    pallas_call x4, Pallas kernels, table_part(): pl.pallas_call(body, grid=(stop - start,), out_shape=[jax.ShapeDtypeStruc...  63.6 us
    ppermute x35, starting transfers between devices, swap_outer(): lax.ppermute(value, 'vocab', [(i, i ^ 2 * step) for i in range(count)])  54.3 us
    ppermute x35, waiting for transfers between devices, swap_outer(): lax.ppermute(value, 'vocab', [(i, i ^ 2 * step) for i in range(count)])  53.5 us
    pallas_call x1, Pallas kernels, write_updates(): pl.pallas_call(body, grid=(steps,), out_shape=outs, in_specs=[whole_block...  52.5 us
    ppermute x40, starting transfers between devices, swap_dp(): return lax.ppermute(value, 'dp', [(i, i ^ step) for i in range(count)])  42.9 us
    pallas_call x1, Pallas kernels, head_pass(): pl.pallas_call(body, out_shape=[shape_of((half, width), jnp.float32), sha...  22.7 us
    ppermute x40, waiting for transfers between devices, swap_dp(): return lax.ppermute(value, 'dp', [(i, i ^ step) for i in range(count)])  21.1 us
    pallas_call x3, Pallas kernels, place_blocks(): pl.pallas_call(body, out_shape=[jax.ShapeDtypeStruct((2 * count,) + tuple...  20.8 us
  transfers between devices with their start and end apart: 93, of which 30 were waited for; matrix products, arithmetic and copies ran while one was open for 16% of the time, Pallas kernels for 30%

profile of v4, /device:TPU:0, one launch (start us, length us, event | category | flops | bytes accessed | tf_op | source)
XLA Modules:
  0.0 561.1 jit_solution(1252687810762236999)
XLA Ops:
  5.9 3.7 collective-permute-start.1
  10.7 7.1 %collective-permute-done.1 = bf16[1,24,3328]{2,1,0:T(8,128)(2,1)S(1)} collective-permute-done((bf16[1,24,3328]{2,1,0:T(8,128)(2,1)S(1)}, bf16[1,24,3328]{2,1,0:T(8,128)(2,1)S(1)}, u32[]{:S(2)}, u32[]{:S(2)}) %collective-permute-start.1) | collective-permute-done | bytes 159776 | tf_op jit(solution)/shard_map/ppermute | solution.py:646
  17.8 3.6 collective-permute-start.2
  23.4 2.6 collective-permute-done.3
  26.0 5.0 collective-permute-done.5
  35.3 2.3 collective-permute-start.8
  37.6 12.6 %gather_fusion = bf16[1536,768]{1,0:T(8,128)(2,1)S(1)} fusion(f32[6288,768]{1,0:T(8,128)} %w_ref.3, s32[2048]{0:T(1024)S(1)} %pad_clamp_fusion), kind=kCustom, calls=%fused_computation | custom fusion | bytes 4724736 | tf_op jit(solution)/shard_map/jit(_take)/gather | solution.py:1313
  60.0 5.0 collective-permute-done.10
  71.2 13.9 %shard_map.415 = (bf16[6400,768]{1,0:T(8,128)(2,1)}, f32[8,128]{1,0:T(8,128)}, f32[1,768]{1,0:T(1,128)}) custom-call(s32[1]{0:T(128)} %bitcast.1.first_ref, f32[6288,768]{1,0:T(8,128)} %w_ref.3, f32[24,2304]{1,0:T(8,128)} %refs_0_.5, f32[24,768]{1,0:T(8,128)} %refs_2_.5, f32[24,3072]{1,0:T(8,128)} %refs_4_.5, f32[96,768]{1,0:T(8,128)} %refs_6_.3, ...), custom_call_target="tpu_custom_call" | custom-call | flops 19316736 | bytes 28975104 | tf_op jit(solution)/shard_map/pallas_call | solution.py:857
  86.2 5.9 %collective-permute-done.14 = bf16[2,8,24,768]{3,2,1,0:T(8,128)(2,1)S(1)} collective-permute-done((bf16[2,8,24,768]{3,2,1,0:T(8,128)(2,1)S(1)}, bf16[2,8,24,768]{3,2,1,0:T(8,128)(2,1)S(1)}, u32[]{:S(2)}, u32[]{:S(2)}) %collective-permute-start.14) | collective-permute-done | bytes 589856 | tf_op jit(solution)/shard_map/ppermute | solution.py:646
  96.8 6.5 %shard_map.416 = (bf16[32,24,2304]{2,1,0:T(8,128)(2,1)}, bf16[32,24,768]{2,1,0:T(8,128)(2,1)}, bf16[32,24,256]{2,1,0:T(8,128)(2,1)}) custom-call(s32[3]{0:T(128)} %pad_add_fusion.2.here_ref, bf16[16,24,3328]{2,1,0:T(8,128)(2,1)} %constant_dynamic-update-slice_fusion.2.held_ref, bf16[16,24,3328]{2,1,0:T(8,128)(2,1)} %collective-permute-done.13.other_ref), custom_call_target="tpu_custom_call" | custom-call | bytes 10223616 | tf_op jit(solution)/shard_map/pallas_call | solution.py:790
  112.4 7.5 %collective-permute-done.16 = bf16[4,8,24,768]{3,2,1,0:T(8,128)(2,1)} collective-permute-done((bf16[4,8,24,768]{3,2,1,0:T(8,128)(2,1)S(1)}, bf16[4,8,24,768]{3,2,1,0:T(8,128)(2,1)}, u32[]{:S(2)}, u32[]{:S(2)}) %collective-permute-start.16) | collective-permute-done | bytes 1179680 | tf_op jit(solution)/shard_map/ppermute | solution.py:651
  125.0 2.4 constant_dynamic-update-slice_fusion.10
  127.4 8.7 %shard_map.417 = (f32[128,768]{1,0:T(8,128)}, bf16[128,2304]{1,0:T(8,128)(2,1)}, f32[128,768]{1,0:T(8,128)}, bf16[128,768]{1,0:T(8,128)(2,1)}, bf16[128,1152]{1,0:T(8,128)(2,1)}, /*index=5*/bf16[128,1152]{1,0:T(8,128)(2,1)}) custom-call(f32[128,768]{1,0:T(8,128)} %add_bitcast_fusion.e_ref, bf16[128,768]{1,0:T(8,128)(2,1)} %reshape.611.p_ref, ...), custom_call_target="tpu_custom_call" | custom-call | flops 1509949440 | bytes 4718592 | tf_op jit(solution)/shard_map/pallas_call | solution.py:134
  147.6 4.6 collective-permute-done.26
  152.9 9.7 %shard_map.418 = (bf16[32,24,768]{2,1,0:T(8,128)(2,1)}, bf16[32,24,768]{2,1,0:T(8,128)(2,1)}, bf16[32,24,768]{2,1,0:T(8,128)(2,1)}, bf16[32,24,768]{2,1,0:T(8,128)(2,1)}, bf16[32,4,24,768]{3,2,1,0:T(8,128)(2,1)}) custom-call(s32[3]{0:T(128)} %pad_add_fusion.2.here_ref, bf16[16,8,24,768]{3,2,1,0:T(8,128)(2,1)} %constant_dynamic-update-slice_fusion.7.held_ref, ...), custom_call_target="tpu_custom_call" | custom-call | bytes 18874368 | tf_op jit(solution)/shard_map/pallas_call | solution.py:790
  162.6 5.4 shard_map.419
  168.0 4.6 shard_map.420
  174.8 3.2 collective-permute-start.27
  181.9 4.1 collective-permute-done.28
  191.8 22.7 %shard_map.421 = (f32[256,768]{1,0:T(8,128)}, f32[256,128]{1,0:T(8,128)}, bf16[256,896]{1,0:T(8,128)(2,1)}) custom-call(s32[2]{0:T(128)} %pad_add_fusion.1.here_ref, bf16[512,768]{1,0:T(8,128)(2,1)} %bitcast.242, bf16[6400,768]{1,0:T(8,128)(2,1)} %get-tuple-element.224.table_ref), custom_call_target="tpu_custom_call" | custom-call | flops 10066329600 | bytes 9830400 | tf_op jit(solution)/shard_map/pallas_call | solution.py:384
  217.4 2.7 shard_map.422
  220.2 2.1 collective-permute-start.35
  222.3 2.4 collective-permute-start.37
  226.1 7.9 %collective-permute-done.36.refs_1_ = bf16[64,896]{1,0:T(8,128)(2,1)S(1)} collective-permute-done((bf16[64,896]{1,0:T(8,128)(2,1)}, bf16[64,896]{1,0:T(8,128)(2,1)S(1)}, u32[]{:S(2)}, u32[]{:S(2)}) %collective-permute-start.36) | collective-permute-done | bytes 114720 | tf_op jit(solution)/shard_map/ppermute | solution.py:646
  234.7 3.3 shard_map.423
  240.8 5.6 %shard_map.424 = (bf16[128,3072]{1,0:T(8,128)(2,1)}, f32[8,768]{1,0:T(8,128)}) custom-call(bf16[128,768]{1,0:T(8,128)(2,1)} %get-tuple-element.282.dy_ref.refs_2_, bf16[3072,768]{1,0:T(8,128)(2,1)} %bitcast.197, f32[128,3072]{1,0:T(8,128)} %get-tuple-element.275.pre_ref), custom_call_target="tpu_custom_call" | custom-call | flops 603979776 | bytes 4718592 | tf_op jit(solution)/shard_map/pallas_call | solution.py:513
  251.2 3.5 shard_map.425
  258.4 4.1 shard_map.426
  265.0 6.7 %shard_map.427 = (f32[128,768]{1,0:T(8,128)}, bf16[128,768]{1,0:T(8,128)(2,1)}, bf16[128,768]{1,0:T(8,128)(2,1)}, f32[8,768]{1,0:T(8,128)}) custom-call(bf16[128,3072]{1,0:T(8,128)(2,1)} %get-tuple-element.302.refs_2_.dpre_ref, f32[128,768]{1,0:T(8,128)} %get-tuple-element.303.dx2_ref, f32[128,768]{1,0:T(8,128)} %get-tuple-element.244.x1_ref, ...), custom_call_target="tpu_custom_call" | custom-call | flops 754974720 | bytes 5898240 | tf_op jit(solution)/shard_map/pallas_call | solution.py:547
  281.3 10.7 %shard_map.428 = (f32[128,768]{1,0:T(8,128)}, bf16[128,768]{1,0:T(8,128)(2,1)}, bf16[128,2304]{1,0:T(8,128)(2,1)}, f32[8,768]{1,0:T(8,128)}) custom-call(bf16[128,768]{1,0:T(8,128)(2,1)} %get-tuple-element.307.mixed_ref, f32[128,768]{1,0:T(8,128)} %get-tuple-element.308.dx1_ref, bf16[128,2304]{1,0:T(8,128)(2,1)} %get-tuple-element.309.packed_ref, ...), custom_call_target="tpu_custom_call" | custom-call | flops 1207959552 | bytes 5898240 | tf_op jit(solution)/shard_map/pallas_call | solution.py:598
  303.2 4.6 shard_map.429
  307.8 3.7 collective-permute-done.59
  314.0 4.6 shard_map.430
  323.1 18.2 %shard_map.431 = (f32[6400,768]{1,0:T(8,128)}, f32[8,128]{1,0:T(8,128)}) custom-call(s32[1]{0:T(128)} %bitcast.1.first_ref, bf16[2048,768]{1,0:T(8,128)(2,1)} %bitcast.192, bf16[6400,768]{1,0:T(8,128)(2,1)} %get-tuple-element.224.table_ref, s32[1,2048]{1,0:T(1,128)} %reshape.643.target_ref, f32[1,2048]{1,0:T(1,128)} %add.446.norm_ref), custom_call_target="tpu_custom_call" | custom-call | flops 12079595520 | bytes 8847360 | tf_op jit(solution)/shard_map/pallas_call | solution.py:933
  348.0 23.3 %shard_map.432 = (f32[6400,768]{1,0:T(8,128)}, f32[8,128]{1,0:T(8,128)}) custom-call(s32[1]{0:T(128)} %bitcast.1.first_ref, bf16[2048,768]{1,0:T(8,128)(2,1)} %bitcast.193, bf16[6400,768]{1,0:T(8,128)(2,1)} %get-tuple-element.224.table_ref, s32[1,2048]{1,0:T(1,128)} %reshape.643.target_ref, ...), custom_call_target="tpu_custom_call", output_to_operand_aliasing={{0}: (5, {})} | custom-call | flops 16106127360 | bytes 11796480 | tf_op jit(solution)/shard_map/pallas_call | solution.py:933
  380.6 2.2 collective-permute-start.71
  385.3 13.8 %shard_map.433 = (f32[6400,768]{1,0:T(8,128)}, f32[8,128]{1,0:T(8,128)}) custom-call(s32[1]{0:T(128)} %bitcast.1.first_ref, bf16[2048,768]{1,0:T(8,128)(2,1)} %bitcast.194, bf16[6400,768]{1,0:T(8,128)(2,1)} %get-tuple-element.224.table_ref, s32[1,2048]{1,0:T(1,128)} %reshape.643.target_ref, ...), custom_call_target="tpu_custom_call", output_to_operand_aliasing={{0}: (5, {})} | custom-call | flops 8053063680 | bytes 5898240 | tf_op jit(solution)/shard_map/pallas_call | solution.py:933
  404.5 3.0 add_add_fusion
  417.1 8.3 %shard_map.434 = (f32[6400,768]{1,0:T(8,128)}, f32[8,128]{1,0:T(8,128)}) custom-call(s32[1]{0:T(128)} %bitcast.1.first_ref, bf16[2048,768]{1,0:T(8,128)(2,1)} %bitcast.195, bf16[6400,768]{1,0:T(8,128)(2,1)} %get-tuple-element.224.table_ref, s32[1,2048]{1,0:T(1,128)} %reshape.643.target_ref, ...), custom_call_target="tpu_custom_call", output_to_operand_aliasing={{0}: (5, {})} | custom-call | flops 4026531840 | bytes 2949120 | tf_op jit(solution)/shard_map/pallas_call | solution.py:933
  426.2 4.7 collective-permute-done.76
  434.6 18.0 %shard_map.435 = (f32[6400,768]{1,0:T(8,128)}, f32[8,128]{1,0:T(8,128)}) custom-call(s32[3]{0:T(128)} %pad_add_fusion.2.here_ref, s32[160]{0:T(256)} %reshape.626.end_ref, s32[2048]{0:T(1024)} %reshape.627.row_ref, s32[2048]{0:T(1024)} %reshape.628.token_ref, f32[6400,768]{1,0:T(8,128)} %get-tuple-element.361.grad_in_ref, ...), custom_call_target="tpu_custom_call", output_to_operand_aliasing={{0}: (4, {})} | custom-call | flops 9830400 | bytes 39321600 | tf_op jit(solution)/shard_map/pallas_call | solution.py:1049
  460.8 6.4 %collective-permute-start.83 = (f32[8,128]{1,0:T(8,128)S(1)}, f32[8,128]{1,0:T(8,128)S(1)}, u32[]{:S(2)}, u32[]{:S(2)}) collective-permute-start(f32[8,128]{1,0:T(8,128)S(1)} %add_add_fusion.6), channel_id=1, source_target_pairs={{0,2},{1,3},{2,0},{3,1},{4,6},{5,7},{6,4},{7,5},{8,10},{9,11},{10,... | collective-permute-start | bytes 12296 | tf_op jit(solution)/shard_map/ppermute | solution.py:646
  467.2 2.4 collective-permute-start.85
  473.2 14.2 %shard_map.436 = (f32[24,2304]{1,0:T(8,128)}, f32[24,2304]{1,0:T(8,128)}, f32[24,2304]{1,0:T(8,128)}, f32[24,768]{1,0:T(8,128)}, f32[24,768]{1,0:T(8,128)}, /*in...) custom-call(s32[1]{0:T(128)} %bitcast.3.dp_ref.here_ref, ...), custom_call_target="tpu_custom_call" | custom-call | flops 24330240 | bytes 19464192 | tf_op jit(solution)/shard_map/pallas_call | solution.py:1146
  494.1 2.3 collective-permute-done.89
  496.4 3.0 collective-permute-start.91
  506.1 52.5 %shard_map.437 = (f32[6288,768]{1,0:T(8,128)}, f32[6288,768]{1,0:T(8,128)}, f32[6288,768]{1,0:T(8,128)}, f32[24,2304]{1,0:T(8,128)}, f32[24,768]{1,0:T(8,128)}, ...) custom-call(f32[8,128]{1,0:T(8,128)} %add_add_fusion.5.sums_ref, ...), custom_call_target="tpu_custom_call" | custom-call | flops 96583680 | bytes 135217152 | tf_op jit(solution)/shard_map/pallas_call | solution.py:1194
  (446 shorter events, 179.9 us)
Async XLA Ops:
  5.9 11.9 %collective-permute-start.1 = (bf16[1,24,3328]{2,1,0:T(8,128)(2,1)S(1)}, bf16[1,24,3328]{2,1,0:T(8,128)(2,1)S(1)}, u32[]{:S(2)}, u32[]{:S(2)}) collective-permute-start(bf16[1,24,3328]{2,1,0:T(8,128)(2,1)S(1)} %get-tuple-element.419), channel_id=1, source_target_pairs={{0,4},{1,5},{2,6},{3,7},{4,0},{5,1},{6,2},{7,3},{8,12},{9,13},{10,... | collective-permute-start | bytes 479240 | tf_op jit(solution)/shard_map/ppermute | solution.py:646
  31.3 21.6 %collective-permute-start.6 = (bf16[4,24,3328]{2,1,0:T(8,128)(2,1)S(1)}, bf16[4,24,3328]{2,1,0:T(8,128)(2,1)}, u32[]{:S(2)}, u32[]{:S(2)}) collective-permute-start(bf16[4,24,3328]{2,1,0:T(8,128)(2,1)S(1)} %bitcast.223), channel_id=1, source_target_pairs={{0,8},{8,0},{16,24},{24,16},{1,9},{9,1},{17,25},{25,17},{2,10},{10... | collective-permute-start | bytes 1916936 | tf_op jit(solution)/shard_map/ppermute | solution.py:651
  32.9 20.0 %collective-permute-start.7 = (bf16[4,24,3328]{2,1,0:T(8,128)(2,1)S(1)}, bf16[4,24,3328]{2,1,0:T(8,128)(2,1)}, u32[]{:S(2)}, u32[]{:S(2)}) collective-permute-start(bf16[4,24,3328]{2,1,0:T(8,128)(2,1)S(1)} %bitcast.224), channel_id=1, source_target_pairs={{0,16},{8,24},{16,0},{24,8},{1,17},{9,25},{17,1},{25,9},{2,18},{10... | collective-permute-start | bytes 1916936 | tf_op jit(solution)/shard_map/ppermute | solution.py:651
  35.3 15.7 %collective-permute-start.8 = (bf16[1,8,24,768]{3,2,1,0:T(8,128)(2,1)S(1)}, bf16[1,8,24,768]{3,2,1,0:T(8,128)(2,1)}, u32[]{:S(2)}, u32[]{:S(2)}) collective-permute-start(bf16[1,8,24,768]{3,2,1,0:T(8,128)(2,1)S(1)} %maximum_bitcast_fusion.3), channel_id=1, source_target_pairs={{0,4},{1,5},{2,6},{3,7},{4,0},{5,1},{6,2},{7,3},{8,12},{9,13},{10,... | collective-permute-start | bytes 884744 | tf_op jit(solution)/shard_map/ppermute | solution.py:646
  53.0 13.6 %collective-permute-start.9 = (bf16[4,192,768]{2,1,0:T(8,128)(2,1)S(1)}, bf16[4,192,768]{2,1,0:T(8,128)(2,1)S(1)}, u32[]{:S(2)}, u32[]{:S(2)}) collective-permute-start(bf16[4,192,768]{2,1,0:T(8,128)(2,1)S(1)} %dynamic-slice_bitcast_fusion), channel_id=1, source_target_pairs={{0,1},{1,0},{2,3},{3,2},{4,5},{5,4},{6,7},{7,6},{8,9},{9,8},{10,11... | collective-permute-start | bytes 3538952 | tf_op jit(solution)/shard_map/ppermute | solution.py:641
  66.7 25.6 %collective-permute-start.13 = (bf16[16,24,3328]{2,1,0:T(8,128)(2,1)}, bf16[16,24,3328]{2,1,0:T(8,128)(2,1)}, u32[]{:S(2)}, u32[]{:S(2)}) collective-permute-start(bf16[16,24,3328]{2,1,0:T(8,128)(2,1)} %constant_dynamic-update-slice_fusion.2.held_ref), channel_id=1, source_target_pairs={{0,1},{1,0},{2,3},{3,2},{4,5},{5,4},{6,7},{7,6},{8,9},{9,8},{10,11... | collective-permute-start | bytes 7667720 | tf_op jit(solution)/shard_map/ppermute | solution.py:641
  67.8 17.3 %collective-permute-start.12 = (bf16[2,128,768]{2,1,0:T(8,128)(2,1)}, bf16[2,128,768]{2,1,0:T(8,128)(2,1)}, u32[]{:S(2)}, u32[]{:S(2)}) collective-permute-start(bf16[2,128,768]{2,1,0:T(8,128)(2,1)} %fusion.2), channel_id=1, source_target_pairs={{0,2},{1,3},{2,0},{3,1},{4,6},{5,7},{6,4},{7,5},{8,10},{9,11},{10,... | collective-permute-start | bytes 1179656 | tf_op jit(solution)/shard_map/ppermute | solution.py:646
  70.1 22.0 %collective-permute-start.14 = (bf16[2,8,24,768]{3,2,1,0:T(8,128)(2,1)S(1)}, bf16[2,8,24,768]{3,2,1,0:T(8,128)(2,1)S(1)}, u32[]{:S(2)}, u32[]{:S(2)}) collective-permute-start(bf16[2,8,24,768]{3,2,1,0:T(8,128)(2,1)S(1)} %copy-done.3), channel_id=1, source_target_pairs={{0,2},{1,3},{2,0},{3,1},{4,6},{5,7},{6,4},{7,5},{8,10},{9,11},{10,... | collective-permute-start | bytes 1769480 | tf_op jit(solution)/shard_map/ppermute | solution.py:646
  92.2 27.7 %collective-permute-start.16 = (bf16[4,8,24,768]{3,2,1,0:T(8,128)(2,1)S(1)}, bf16[4,8,24,768]{3,2,1,0:T(8,128)(2,1)}, u32[]{:S(2)}, u32[]{:S(2)}) collective-permute-start(bf16[4,8,24,768]{3,2,1,0:T(8,128)(2,1)S(1)} %bitcast.211), channel_id=1, source_target_pairs={{0,8},{8,0},{16,24},{24,16},{1,9},{9,1},{17,25},{25,17},{2,10},{10... | collective-permute-start | bytes 3538952 | tf_op jit(solution)/shard_map/ppermute | solution.py:651
  93.3 27.3 %collective-permute-start.17 = (bf16[4,8,24,768]{3,2,1,0:T(8,128)(2,1)S(1)}, bf16[4,8,24,768]{3,2,1,0:T(8,128)(2,1)S(1)}, u32[]{:S(2)}, u32[]{:S(2)}) collective-permute-start(bf16[4,8,24,768]{3,2,1,0:T(8,128)(2,1)S(1)} %bitcast.212), channel_id=1, source_target_pairs={{0,16},{8,24},{16,0},{24,8},{1,17},{9,25},{17,1},{25,9},{2,18},{10... | collective-permute-start | bytes 3538952 | tf_op jit(solution)/shard_map/ppermute | solution.py:651
  120.6 16.6 %collective-permute-start.20 = (bf16[2,64,768]{2,1,0:T(8,128)(2,1)}, bf16[2,64,768]{2,1,0:T(8,128)(2,1)S(1)}, u32[]{:S(2)}, u32[]{:S(2)}) collective-permute-start(bf16[2,64,768]{2,1,0:T(8,128)(2,1)} %fusion.7), channel_id=1, source_target_pairs={{0,2},{1,3},{2,0},{3,1},{4,6},{5,7},{6,4},{7,5},{8,10},{9,11},{10,... | collective-permute-start | bytes 589832 | tf_op jit(solution)/shard_map/ppermute | solution.py:646
  123.4 13.8 %collective-permute-start.18 = (bf16[2,8,24,768]{3,2,1,0:T(8,128)(2,1)S(1)}, bf16[2,8,24,768]{3,2,1,0:T(8,128)(2,1)S(1)}, u32[]{:S(2)}, u32[]{:S(2)}) collective-permute-start(bf16[2,8,24,768]{3,2,1,0:T(8,128)(2,1)S(1)} %slice.152), channel_id=1, source_target_pairs={{0,8},{8,0},{16,24},{24,16},{1,9},{9,1},{17,25},{25,17},{2,10},{10... | collective-permute-start | bytes 1769480 | tf_op jit(solution)/shard_map/ppermute | solution.py:651
  124.5 13.6 %collective-permute-start.19 = (bf16[2,8,24,768]{3,2,1,0:T(8,128)(2,1)S(1)}, bf16[2,8,24,768]{3,2,1,0:T(8,128)(2,1)S(1)}, u32[]{:S(2)}, u32[]{:S(2)}) collective-permute-start(bf16[2,8,24,768]{3,2,1,0:T(8,128)(2,1)S(1)} %slice.153), channel_id=1, source_target_pairs={{0,16},{8,24},{16,0},{24,8},{1,17},{9,25},{17,1},{25,9},{2,18},{10... | collective-permute-start | bytes 1769480 | tf_op jit(solution)/shard_map/ppermute | solution.py:651
  139.0 13.9 %collective-permute-start.21 = (bf16[16,8,24,768]{3,2,1,0:T(8,128)(2,1)}, bf16[16,8,24,768]{3,2,1,0:T(8,128)(2,1)}, u32[]{:S(2)}, u32[]{:S(2)}) collective-permute-start(bf16[16,8,24,768]{3,2,1,0:T(8,128)(2,1)} %constant_dynamic-update-slice_fusion.7.held_ref), channel_id=1, source_target_pairs={{0,1},{1,0},{2,3},{3,2},{4,5},{5,4},{6,7},{7,6},{8,9},{9,8},{10,11... | collective-permute-start | bytes 14155784 | tf_op jit(solution)/shard_map/ppermute | solution.py:641
  146.0 27.4 %collective-permute-start.25 = (bf16[128,1152]{1,0:T(8,128)(2,1)S(1)}, bf16[128,1152]{1,0:T(8,128)(2,1)S(1)}, u32[]{:S(2)}, u32[]{:S(2)}) collective-permute-start(bf16[128,1152]{1,0:T(8,128)(2,1)S(1)} %copy-done.43), channel_id=1, source_target_pairs={{0,1},{1,0},{2,3},{3,2},{4,5},{5,4},{6,7},{7,6},{8,9},{9,8},{10,11... | collective-permute-start | bytes 884744 | tf_op jit(solution)/shard_map/ppermute | solution.py:641
  173.5 12.4 %collective-permute-start.28 = (bf16[80,768]{1,0:T(8,128)(2,1)S(1)}, bf16[80,768]{1,0:T(8,128)(2,1)S(1)}, u32[]{:S(2)}, u32[]{:S(2)}) collective-permute-start(bf16[80,768]{1,0:T(8,128)(2,1)S(1)} %pad_maximum_fusion.13), channel_id=1, source_target_pairs={{0,4},{1,5},{2,6},{3,7},{4,0},{5,1},{6,2},{7,3},{8,12},{9,13},{10,... | collective-permute-start | bytes 368648 | tf_op jit(solution)/shard_map/ppermute | solution.py:646
  189.3 25.3 %collective-permute-start.32 = (bf16[4,64,768]{2,1,0:T(8,128)(2,1)S(1)}, bf16[4,64,768]{2,1,0:T(8,128)(2,1)S(1)}, u32[]{:S(2)}, u32[]{:S(2)}) collective-permute-start(bf16[4,64,768]{2,1,0:T(8,128)(2,1)S(1)} %slice.157), channel_id=1, source_target_pairs={{0,8},{8,0},{16,24},{24,16},{1,9},{9,1},{17,25},{25,17},{2,10},{10... | collective-permute-start | bytes 1179656 | tf_op jit(solution)/shard_map/ppermute | solution.py:651
  190.3 24.3 %collective-permute-start.33 = (bf16[4,64,768]{2,1,0:T(8,128)(2,1)S(1)}, bf16[4,64,768]{2,1,0:T(8,128)(2,1)S(1)}, u32[]{:S(2)}, u32[]{:S(2)}) collective-permute-start(bf16[4,64,768]{2,1,0:T(8,128)(2,1)S(1)} %slice.157), channel_id=1, source_target_pairs={{0,16},{8,24},{16,0},{24,8},{1,17},{9,25},{17,1},{25,9},{2,18},{10... | collective-permute-start | bytes 1179656 | tf_op jit(solution)/shard_map/ppermute | solution.py:651
  222.3 11.7 %collective-permute-start.36 = (bf16[64,896]{1,0:T(8,128)(2,1)}, bf16[64,896]{1,0:T(8,128)(2,1)S(1)}, u32[]{:S(2)}, u32[]{:S(2)}) collective-permute-start(bf16[64,896]{1,0:T(8,128)(2,1)} %get-tuple-element.268), channel_id=1, source_target_pairs={{0,4},{1,5},{2,6},{3,7},{4,0},{5,1},{6,2},{7,3},{8,12},{9,13},{10,... | collective-permute-start | bytes 344072 | tf_op jit(solution)/shard_map/ppermute | solution.py:646
  222.3 11.7 %collective-permute-start.37 = (bf16[64,896]{1,0:T(8,128)(2,1)}, bf16[64,896]{1,0:T(8,128)(2,1)S(1)}, u32[]{:S(2)}, u32[]{:S(2)}) collective-permute-start(bf16[64,896]{1,0:T(8,128)(2,1)} %get-tuple-element.269), channel_id=1, source_target_pairs={{0,6},{1,7},{2,4},{3,5},{4,2},{5,3},{6,0},{7,1},{8,14},{9,15},{10,... | collective-permute-start | bytes 344072 | tf_op jit(solution)/shard_map/ppermute | solution.py:646
  254.9 16.9 %collective-permute-start.46 = (f32[8,2,64]{2,1,0:T(2,128)S(1)}, f32[8,2,64]{2,1,0:T(2,128)S(1)}, u32[]{:S(2)}, u32[]{:S(2)}) collective-permute-start(f32[8,2,64]{2,1,0:T(2,128)S(1)} %pad_maximum_fusion.16), channel_id=1, source_target_pairs={{0,24},{8,16},{16,8},{24,0},{1,25},{9,17},{17,9},{25,1},{2,26},{10... | collective-permute-start | bytes 12296 | tf_op jit(solution)/shard_map/ppermute | solution.py:651
  256.9 14.8 %collective-permute-start.47 = (f32[8,2,64]{2,1,0:T(2,128)S(1)}, f32[8,2,64]{2,1,0:T(2,128)S(1)}, u32[]{:S(2)}, u32[]{:S(2)}) collective-permute-start(f32[8,2,64]{2,1,0:T(2,128)S(1)} %pad_maximum_fusion.16), channel_id=1, source_target_pairs={{0,16},{8,24},{16,0},{24,8},{1,17},{9,25},{17,1},{25,9},{2,18},{10... | collective-permute-start | bytes 12296 | tf_op jit(solution)/shard_map/ppermute | solution.py:651
  257.4 14.3 %collective-permute-start.48 = (f32[8,2,64]{2,1,0:T(2,128)S(1)}, f32[8,2,64]{2,1,0:T(2,128)S(1)}, u32[]{:S(2)}, u32[]{:S(2)}) collective-permute-start(f32[8,2,64]{2,1,0:T(2,128)S(1)} %pad_maximum_fusion.16), channel_id=1, source_target_pairs={{0,8},{8,0},{16,24},{24,16},{1,9},{9,1},{17,25},{25,17},{2,10},{10... | collective-permute-start | bytes 12296 | tf_op jit(solution)/shard_map/ppermute | solution.py:651
  273.5 19.8 %collective-permute-start.54 = (bf16[16,64,768]{2,1,0:T(8,128)(2,1)S(1)}, bf16[16,64,768]{2,1,0:T(8,128)(2,1)}, u32[]{:S(2)}, u32[]{:S(2)}) collective-permute-start(bf16[16,64,768]{2,1,0:T(8,128)(2,1)S(1)} %constant_dynamic-update-slice_fusion.12.held_ref), channel_id=1, source_target_pairs={{0,1},{1,0},{2,3},{3,2},{4,5},{5,4},{6,7},{7,6},{8,9},{9,8},{10,11... | collective-permute-start | bytes 4718600 | tf_op jit(solution)/shard_map/ppermute | solution.py:641
  273.6 18.4 %collective-permute-start.51 = (bf16[4,96,768]{2,1,0:T(8,128)(2,1)S(1)}, bf16[4,96,768]{2,1,0:T(8,128)(2,1)S(1)}, u32[]{:S(2)}, u32[]{:S(2)}) collective-permute-start(bf16[4,96,768]{2,1,0:T(8,128)(2,1)S(1)} %pad_maximum_fusion.5), channel_id=1, source_target_pairs={{0,8},{8,0},{16,24},{24,16},{1,9},{9,1},{17,25},{25,17},{2,10},{10... | collective-permute-start | bytes 1769480 | tf_op jit(solution)/shard_map/ppermute | solution.py:651
  274.7 17.3 %collective-permute-start.52 = (bf16[4,96,768]{2,1,0:T(8,128)(2,1)S(1)}, bf16[4,96,768]{2,1,0:T(8,128)(2,1)}, u32[]{:S(2)}, u32[]{:S(2)}) collective-permute-start(bf16[4,96,768]{2,1,0:T(8,128)(2,1)S(1)} %pad_maximum_fusion.6), channel_id=1, source_target_pairs={{0,16},{8,24},{16,0},{24,8},{1,17},{9,25},{17,1},{25,9},{2,18},{10... | collective-permute-start | bytes 1769480 | tf_op jit(solution)/shard_map/ppermute | solution.py:651
  281.3 11.9 %collective-permute-start.53 = (bf16[128,768]{1,0:T(8,128)(2,1)S(1)}, bf16[128,768]{1,0:T(8,128)(2,1)S(1)}, u32[]{:S(2)}, u32[]{:S(2)}) collective-permute-start(bf16[128,768]{1,0:T(8,128)(2,1)S(1)} %copy-done.24), channel_id=1, source_target_pairs={{0,1},{1,0},{2,3},{3,2},{4,5},{5,4},{6,7},{7,6},{8,9},{9,8},{10,11... | collective-permute-start | bytes 589832 | tf_op jit(solution)/shard_map/ppermute | solution.py:641
  299.3 12.3 %collective-permute-start.59 = (bf16[1,128,768]{2,1,0:T(8,128)(2,1)S(1)}, bf16[1,128,768]{2,1,0:T(8,128)(2,1)S(1)}, u32[]{:S(2)}, u32[]{:S(2)}) collective-permute-start(bf16[1,128,768]{2,1,0:T(8,128)(2,1)S(1)} %bitcast.265), channel_id=1, source_target_pairs={{0,4},{1,5},{2,6},{3,7},{4,0},{5,1},{6,2},{7,3},{8,12},{9,13},{10,... | collective-permute-start | bytes 589832 | tf_op jit(solution)/shard_map/ppermute | solution.py:646
  300.6 11.8 %collective-permute-start.57 = (bf16[2,24,3072]{2,1,0:T(8,128)(2,1)}, bf16[2,24,3072]{2,1,0:T(8,128)(2,1)S(1)}, u32[]{:S(2)}, u32[]{:S(2)}) collective-permute-start(bf16[2,24,3072]{2,1,0:T(8,128)(2,1)} %bitcast.273), channel_id=1, source_target_pairs={{0,8},{8,0},{16,24},{24,16},{1,9},{9,1},{17,25},{25,17},{2,10},{10... | collective-permute-start | bytes 884744 | tf_op jit(solution)/shard_map/ppermute | solution.py:651
  318.5 22.7 %collective-permute-start.63 = (bf16[2,96,768]{2,1,0:T(8,128)(2,1)S(1)}, bf16[2,96,768]{2,1,0:T(8,128)(2,1)S(1)}, u32[]{:S(2)}, u32[]{:S(2)}) collective-permute-start(bf16[2,96,768]{2,1,0:T(8,128)(2,1)S(1)} %fusion.4), channel_id=1, source_target_pairs={{0,2},{1,3},{2,0},{3,1},{4,6},{5,7},{6,4},{7,5},{8,10},{9,11},{10,... | collective-permute-start | bytes 884744 | tf_op jit(solution)/shard_map/ppermute | solution.py:646
  318.5 23.6 %collective-permute-start.62 = (bf16[2,128,768]{2,1,0:T(8,128)(2,1)S(1)}, bf16[2,128,768]{2,1,0:T(8,128)(2,1)S(1)}, u32[]{:S(2)}, u32[]{:S(2)}) collective-permute-start(bf16[2,128,768]{2,1,0:T(8,128)(2,1)S(1)} %maximum_bitcast_fusion.1), channel_id=1, source_target_pairs={{0,2},{1,3},{2,0},{3,1},{4,6},{5,7},{6,4},{7,5},{8,10},{9,11},{10,... | collective-permute-start | bytes 1179656 | tf_op jit(solution)/shard_map/ppermute | solution.py:646
  320.6 21.8 %collective-permute-start.60 = (bf16[4,24,3072]{2,1,0:T(8,128)(2,1)S(1)}, bf16[4,24,3072]{2,1,0:T(8,128)(2,1)S(1)}, u32[]{:S(2)}, u32[]{:S(2)}) collective-permute-start(bf16[4,24,3072]{2,1,0:T(8,128)(2,1)S(1)} %pad_maximum_fusion.7), channel_id=1, source_target_pairs={{0,8},{8,0},{16,24},{24,16},{1,9},{9,1},{17,25},{25,17},{2,10},{10... | collective-permute-start | bytes 1769480 | tf_op jit(solution)/shard_map/ppermute | solution.py:651
  321.6 20.8 %collective-permute-start.61 = (bf16[4,24,3072]{2,1,0:T(8,128)(2,1)S(1)}, bf16[4,24,3072]{2,1,0:T(8,128)(2,1)S(1)}, u32[]{:S(2)}, u32[]{:S(2)}) collective-permute-start(bf16[4,24,3072]{2,1,0:T(8,128)(2,1)S(1)} %pad_maximum_fusion.8), channel_id=1, source_target_pairs={{0,16},{8,24},{16,0},{24,8},{1,17},{9,25},{17,1},{25,9},{2,18},{10... | collective-permute-start | bytes 1769480 | tf_op jit(solution)/shard_map/ppermute | solution.py:651
  343.7 32.5 %collective-permute-start.66 = (bf16[4,128,768]{2,1,0:T(8,128)(2,1)S(1)}, bf16[4,128,768]{2,1,0:T(8,128)(2,1)}, u32[]{:S(2)}, u32[]{:S(2)}) collective-permute-start(bf16[4,128,768]{2,1,0:T(8,128)(2,1)S(1)} %bitcast.218), channel_id=1, source_target_pairs={{0,8},{8,0},{16,24},{24,16},{1,9},{9,1},{17,25},{25,17},{2,10},{10... | collective-permute-start | bytes 2359304 | tf_op jit(solution)/shard_map/ppermute | solution.py:651
  344.8 31.4 %collective-permute-start.67 = (bf16[4,128,768]{2,1,0:T(8,128)(2,1)S(1)}, bf16[4,128,768]{2,1,0:T(8,128)(2,1)}, u32[]{:S(2)}, u32[]{:S(2)}) collective-permute-start(bf16[4,128,768]{2,1,0:T(8,128)(2,1)S(1)} %bitcast.219), channel_id=1, source_target_pairs={{0,16},{8,24},{16,0},{24,8},{1,17},{9,25},{17,1},{25,9},{2,18},{10... | collective-permute-start | bytes 2359304 | tf_op jit(solution)/shard_map/ppermute | solution.py:651
  345.3 26.0 %collective-permute-start.68 = (bf16[2,24,3072]{2,1,0:T(8,128)(2,1)S(1)}, bf16[2,24,3072]{2,1,0:T(8,128)(2,1)}, u32[]{:S(2)}, u32[]{:S(2)}) collective-permute-start(bf16[2,24,3072]{2,1,0:T(8,128)(2,1)S(1)} %fusion.5), channel_id=1, source_target_pairs={{0,2},{1,3},{2,0},{3,1},{4,6},{5,7},{6,4},{7,5},{8,10},{9,11},{10,... | collective-permute-start | bytes 884744 | tf_op jit(solution)/shard_map/ppermute | solution.py:646
  345.4 27.8 %collective-permute-start.65 = (bf16[2,24,3328]{2,1,0:T(8,128)(2,1)}, bf16[2,24,3328]{2,1,0:T(8,128)(2,1)}, u32[]{:S(2)}, u32[]{:S(2)}) collective-permute-start(bf16[2,24,3328]{2,1,0:T(8,128)(2,1)} %bitcast.95), channel_id=1, source_target_pairs={{0,8},{8,0},{16,24},{24,16},{1,9},{9,1},{17,25},{25,17},{2,10},{10... | collective-permute-start | bytes 958472 | tf_op jit(solution)/shard_map/ppermute | solution.py:651
  346.4 27.7 %collective-permute-start.64 = (bf16[2,24,3328]{2,1,0:T(8,128)(2,1)}, bf16[2,24,3328]{2,1,0:T(8,128)(2,1)S(1)}, u32[]{:S(2)}, u32[]{:S(2)}) collective-permute-start(bf16[2,24,3328]{2,1,0:T(8,128)(2,1)} %bitcast.96), channel_id=1, source_target_pairs={{0,16},{8,24},{16,0},{24,8},{1,17},{9,25},{17,1},{25,9},{2,18},{10... | collective-permute-start | bytes 958472 | tf_op jit(solution)/shard_map/ppermute | solution.py:651
  379.0 23.4 %collective-permute-start.72 = (bf16[2,128,768]{2,1,0:T(8,128)(2,1)}, bf16[2,128,768]{2,1,0:T(8,128)(2,1)}, u32[]{:S(2)}, u32[]{:S(2)}) collective-permute-start(bf16[2,128,768]{2,1,0:T(8,128)(2,1)} %slice.163), channel_id=1, source_target_pairs={{0,8},{8,0},{16,24},{24,16},{1,9},{9,1},{17,25},{25,17},{2,10},{10... | collective-permute-start | bytes 1179656 | tf_op jit(solution)/shard_map/ppermute | solution.py:651
  380.1 23.3 %collective-permute-start.73 = (bf16[2,128,768]{2,1,0:T(8,128)(2,1)S(1)}, bf16[2,128,768]{2,1,0:T(8,128)(2,1)}, u32[]{:S(2)}, u32[]{:S(2)}) collective-permute-start(bf16[2,128,768]{2,1,0:T(8,128)(2,1)S(1)} %slice.164), channel_id=1, source_target_pairs={{0,16},{8,24},{16,0},{24,8},{1,17},{9,25},{17,1},{25,9},{2,18},{10... | collective-permute-start | bytes 1179656 | tf_op jit(solution)/shard_map/ppermute | solution.py:651
  380.6 21.1 %collective-permute-start.71 = (bf16[1,24,3072]{2,1,0:T(8,128)(2,1)}, bf16[1,24,3072]{2,1,0:T(8,128)(2,1)S(1)}, u32[]{:S(2)}, u32[]{:S(2)}) collective-permute-start(bf16[1,24,3072]{2,1,0:T(8,128)(2,1)} %dynamic-slice_convert_fusion.6), channel_id=1, source_target_pairs={{0,4},{1,5},{2,6},{3,7},{4,0},{5,1},{6,2},{7,3},{8,12},{9,13},{10,... | collective-permute-start | bytes 442376 | tf_op jit(solution)/shard_map/ppermute | solution.py:646
  382.8 21.7 %collective-permute-start.69 = (bf16[4,24,3328]{2,1,0:T(8,128)(2,1)}, bf16[4,24,3328]{2,1,0:T(8,128)(2,1)S(1)}, u32[]{:S(2)}, u32[]{:S(2)}) collective-permute-start(bf16[4,24,3328]{2,1,0:T(8,128)(2,1)} %pad_maximum_fusion.3), channel_id=1, source_target_pairs={{0,8},{8,0},{16,24},{24,16},{1,9},{9,1},{17,25},{25,17},{2,10},{10... | collective-permute-start | bytes 1916936 | tf_op jit(solution)/shard_map/ppermute | solution.py:651
  383.8 20.7 %collective-permute-start.70 = (bf16[4,24,3328]{2,1,0:T(8,128)(2,1)}, bf16[4,24,3328]{2,1,0:T(8,128)(2,1)}, u32[]{:S(2)}, u32[]{:S(2)}) collective-permute-start(bf16[4,24,3328]{2,1,0:T(8,128)(2,1)} %pad_maximum_fusion.4), channel_id=1, source_target_pairs={{0,16},{8,24},{16,0},{24,8},{1,17},{9,25},{17,1},{25,9},{2,18},{10... | collective-permute-start | bytes 1916936 | tf_op jit(solution)/shard_map/ppermute | solution.py:651
  407.5 27.1 %collective-permute-start.74 = (bf16[16,128,768]{2,1,0:T(8,128)(2,1)S(1)}, bf16[16,128,768]{2,1,0:T(8,128)(2,1)}, u32[]{:S(2)}, u32[]{:S(2)}) collective-permute-start(bf16[16,128,768]{2,1,0:T(8,128)(2,1)S(1)} %constant_dynamic-update-slice_fusion.17.held_ref), channel_id=1, source_target_pairs={{0,1},{1,0},{2,3},{3,2},{4,5},{5,4},{6,7},{7,6},{8,9},{9,8},{10,11... | collective-permute-start | bytes 9437192 | tf_op jit(solution)/shard_map/ppermute | solution.py:641
  410.6 14.8 %collective-permute-start.78 = (bf16[1,96,768]{2,1,0:T(8,128)(2,1)S(1)}, bf16[1,96,768]{2,1,0:T(8,128)(2,1)S(1)}, u32[]{:S(2)}, u32[]{:S(2)}) collective-permute-start(bf16[1,96,768]{2,1,0:T(8,128)(2,1)S(1)} %dynamic-slice_convert_fusion.5), channel_id=1, source_target_pairs={{0,4},{1,5},{2,6},{3,7},{4,0},{5,1},{6,2},{7,3},{8,12},{9,13},{10,... | collective-permute-start | bytes 442376 | tf_op jit(solution)/shard_map/ppermute | solution.py:646
  412.6 13.6 %collective-permute-start.75 = (bf16[24,3328]{1,0:T(8,128)(2,1)S(1)}, bf16[24,3328]{1,0:T(8,128)(2,1)S(1)}, u32[]{:S(2)}, u32[]{:S(2)}) collective-permute-start(bf16[24,3328]{1,0:T(8,128)(2,1)S(1)} %get-tuple-element.364), channel_id=1, source_target_pairs={{0,2},{1,3},{2,0},{3,1},{4,6},{5,7},{6,4},{7,5},{8,10},{9,11},{10,... | collective-permute-start | bytes 479240 | tf_op jit(solution)/shard_map/ppermute | solution.py:646
  414.6 16.3 %collective-permute-start.76 = (bf16[24,3328]{1,0:T(8,128)(2,1)S(1)}, bf16[24,3328]{1,0:T(8,128)(2,1)S(1)}, u32[]{:S(2)}, u32[]{:S(2)}) collective-permute-start(bf16[24,3328]{1,0:T(8,128)(2,1)S(1)} %get-tuple-element.365), channel_id=1, source_target_pairs={{0,4},{1,5},{2,6},{3,7},{4,0},{5,1},{6,2},{7,3},{8,12},{9,13},{10,... | collective-permute-start | bytes 479240 | tf_op jit(solution)/shard_map/ppermute | solution.py:646
  415.0 15.9 %collective-permute-start.77 = (bf16[24,3328]{1,0:T(8,128)(2,1)S(1)}, bf16[24,3328]{1,0:T(8,128)(2,1)S(1)}, u32[]{:S(2)}, u32[]{:S(2)}) collective-permute-start(bf16[24,3328]{1,0:T(8,128)(2,1)S(1)} %get-tuple-element.366), channel_id=1, source_target_pairs={{0,6},{1,7},{2,4},{3,5},{4,2},{5,3},{6,0},{7,1},{8,14},{9,15},{10,... | collective-permute-start | bytes 479240 | tf_op jit(solution)/shard_map/ppermute | solution.py:646
  (93 other events, 543.0 us)
